TPU v7x, 32 devices: a whole 2x2x4 slice. The times are simulated.
32 devices in a mesh: seq: 8 (over y, x, core), mp: 4 (over z).
Axes of the slice: x: 2, y: 2, z: 4, core: 2. Of those that a mesh axis runs over, the one named last changes fastest.
Arguments:
- tokens: bfloat16 [8192, 2048], P('seq'), may hold values from -6 to 6
- cotangent: bfloat16 [8192, 2048], P('seq'), may hold values from -6 to 6
- destination: int32 [8192], replicated, may hold values from 0 to 8191, as said below
- lengths: int32 [6], replicated, may hold values from 1 to 2048, 8192 in all
- norm_gain: float32 [2048], replicated, may hold values from 0.1 to 1.9
- w_branch: bfloat16 [2048, 2736], P(None, 'mp'), may hold values from -0.125 to 0.125
- w_input: bfloat16 [2048, 2736], P(None, 'mp'), may hold values from -0.125 to 0.125
- conv_weight: float32 [4, 2736], P(None, 'mp'), may hold values from -3 to 3
- conv_bias: float32 [2736], P('mp'), may hold values from -3 to 3
- w_recur: bfloat16 [16, 171, 171], P('mp'), may hold values from -0.4375 to 0.4375
- w_ingate: bfloat16 [16, 171, 171], P('mp'), may hold values from -0.4375 to 0.4375
- decay_param: float32 [2736], P('mp'), may hold values from 3 to 9
- w_out: bfloat16 [2736, 2048], P('mp'), may hold values from -0.15625 to 0.15625
- mlp_gain: float32 [2048], replicated, may hold values from 0.1 to 1.9
- w_gate: bfloat16 [2048, 6144], P(None, 'mp'), may hold values from -0.125 to 0.125
- w_up: bfloat16 [2048, 6144], P(None, 'mp'), may hold values from -0.125 to 0.125
- w_down: bfloat16 [6144, 2048], P('mp'), may hold values from -0.15625 to 0.15625
Outputs:
- block_out: float32 [8192, 2048], P('seq', 'mp')
- input_grad: float32 [8192, 2048], P('seq', 'mp')
- grad_norm_gain: float32 [2048], P('mp')
- grad_w_branch: float32 [2048, 2736], P('seq', 'mp')
- grad_w_input: float32 [2048, 2736], P('seq', 'mp')
- grad_conv_weight: float32 [4, 2736], P(None, 'mp')
- grad_conv_bias: float32 [2736], P('mp')
- grad_w_recur: float32 [16, 171, 171], P('mp')
- grad_w_ingate: float32 [16, 171, 171], P('mp')
- grad_decay_param: float32 [2736], P('mp')
- grad_w_out: float32 [2736, 2048], P('mp', 'seq')
- grad_mlp_gain: float32 [2048], P('mp')
- grad_w_gate: float32 [2048, 6144], P('seq', 'mp')
- grad_w_up: float32 [2048, 6144], P('seq', 'mp')
- grad_w_down: float32 [6144, 2048], P('mp', 'seq')
Inputs may be any that keep to these rules, and one draw needn't show every extreme that they name: destination is a permutation of the 8192 places; of the 1024 tokens in each aligned block of 1024 initial positions, exactly 128 go to each aligned block of 1024 places. The lengths sum to 8192, and the longest is exactly 2048.
All inputs are finite; a program needn't handle non-finite values.
Results may differ from a plain program's by a relative error of at most 0.0088.
Values may be sent and summed in bfloat16 or wider, within the bound.
No kernel may reach another device: no remote copies, remote signals or barrier semaphores. Data moves between devices by JAX's collectives and lax.ppermute only.
A program may use at most 320 MiB of HBM per device.

v0:
```python
import jax
import jax.numpy as jnp
from jax import lax
from jax.sharding import PartitionSpec as P

CONV = 4


EPSILON = 1e-06
GATE_POWER = 8.0
ROOT_FLOOR = 0.01
GROUP_ROWS = 8


def shifted(x, axis, by):
    size = lax.axis_size(axis)
    pairs = [(i, i + by) for i in range(size) if 0 <= i + by < size]
    return lax.ppermute(x, axis, pairs)


def entering(value, axis, join, neutral, backward):
    count, mine = (lax.axis_size(axis), lax.axis_index(axis))
    pieces = jax.tree.map(lambda part: lax.all_gather(part, axis), value)
    if backward:
        pieces = jax.tree.map(lambda part: part[::-1], pieces)
        mine = count - 1 - mine
    so_far = jax.tree.map(
        lambda part, zero: jnp.full_like(part, 0) + jnp.asarray(zero, part.dtype), value, neutral
    )

    def step(position, so_far):
        longer = join(so_far, jax.tree.map(lambda part: part[position], pieces))
        return jax.tree.map(lambda new, old: jnp.where(position < mine, new, old), longer, so_far)

    return lax.fori_loop(0, count - 1, step, so_far)


def rms_scale(values, gain):
    return values * lax.rsqrt(jnp.mean(values * values, axis=-1, keepdims=True) + EPSILON) * gain


def chain(first, second):
    return (first[0] * second[0], second[0] * first[1] + second[1])


def group_scan(rates, drives, reverse):
    total_rows, channels = rates.shape
    groups = total_rows // GROUP_ROWS
    rate_view = rates.reshape(groups, GROUP_ROWS, channels)
    drive_view = drives.reshape(groups, GROUP_ROWS, channels)
    order = range(GROUP_ROWS - 1, -1, -1) if reverse else range(GROUP_ROWS)
    run_keep = jnp.ones((groups, channels), jnp.float32)
    run_state = jnp.zeros((groups, channels), jnp.float32)
    keeps = [None] * GROUP_ROWS
    states = [None] * GROUP_ROWS
    for index in order:
        run_keep = run_keep * rate_view[:, index]
        run_state = rate_view[:, index] * run_state + drive_view[:, index]
        keeps[index] = run_keep
        states[index] = run_state
    total_keep, total_state = lax.associative_scan(chain, (run_keep, run_state), reverse=reverse)
    unit = jnp.ones((1, channels), jnp.float32)
    nothing = jnp.zeros((1, channels), jnp.float32)
    if reverse:
        carry_keep = jnp.concatenate([total_keep[1:], unit], axis=0)
        carry_state = jnp.concatenate([total_state[1:], nothing], axis=0)
    else:
        carry_keep = jnp.concatenate([unit, total_keep[:-1]], axis=0)
        carry_state = jnp.concatenate([nothing, total_state[:-1]], axis=0)
    keep_block = jnp.stack(keeps, axis=1)
    state_block = jnp.stack(states, axis=1)
    full_keep = keep_block * carry_keep[:, None, :]
    full_state = state_block + keep_block * carry_state[:, None, :]
    return (full_keep.reshape(total_rows, channels), full_state.reshape(total_rows, channels))


def gates(recur, ingate, convolved, decay_param, notstart):
    reset_gate = jax.nn.sigmoid(recur)
    input_gate = jax.nn.sigmoid(ingate)
    keep_rate = jnp.exp(-GATE_POWER * reset_gate * jax.nn.softplus(-decay_param))
    drive_term = jnp.sqrt(1.0 - keep_rate * keep_rate + ROOT_FLOOR) * (input_gate * convolved)
    return (keep_rate * notstart, drive_term)


def forward_product(left, right):
    return jnp.dot(left, right, preferred_element_type=jnp.float32)


def backward_product(left, right):
    return lax.dot_general(
        left, right, (((1,), (1,)), ((), ())), preferred_element_type=jnp.float32
    )


def weight_product(left, right):
    return lax.dot_general(
        left, right, (((0,), (0,)), ((), ())), preferred_element_type=jnp.float32
    )


def shards(
    tokens,
    cotangent,
    destination,
    lengths,
    norm_gain,
    w_branch,
    w_input,
    conv_weight,
    conv_bias,
    w_recur,
    w_ingate,
    decay_param,
    w_out,
    mlp_gain,
    w_gate,
    w_up,
    w_down,
):
    shard_count = lax.axis_size("seq")
    my_shard = lax.axis_index("seq")
    model_count = lax.axis_size("mp")
    my_model = lax.axis_index("mp")
    row_count = tokens.shape[0]
    model_width = tokens.shape[1]
    slab_width = model_width // model_count
    per_peer = row_count // shard_count
    edge_rows = CONV - 1
    local_dest = lax.dynamic_slice_in_dim(destination, my_shard * row_count, row_count)
    send_order = jnp.argsort(local_dest, stable=True)
    outgoing = (
        tokens[send_order].reshape(shard_count, per_peer, model_width),
        cotangent[send_order].reshape(shard_count, per_peer, model_width),
    )
    arrived_tokens, arrived_cot = (
        lax.all_to_all(outgoing[0], "seq", split_axis=0, concat_axis=0, tiled=True),
        lax.all_to_all(outgoing[1], "seq", split_axis=0, concat_axis=0, tiled=True),
    )
    sorted_dest = jnp.sort(destination.reshape(shard_count, row_count), axis=1)
    landing = (
        lax.dynamic_slice_in_dim(sorted_dest, my_shard * per_peer, per_peer, 1).reshape(-1)
        - my_shard * row_count
    )
    placing = jnp.argsort(landing)
    stream = arrived_tokens.reshape(row_count, model_width)[placing].astype(jnp.float32)
    upstream_low = arrived_cot.reshape(row_count, model_width)[placing]
    upstream = upstream_low.astype(jnp.float32)
    positions = my_shard * row_count + jnp.arange(row_count, dtype=jnp.int32)
    seq_starts = jnp.cumsum(lengths) - lengths
    seq_start = jnp.max(
        jnp.where(seq_starts[None, :] <= positions[:, None], seq_starts[None, :], 0), axis=1
    )
    notstart = (positions > seq_start).astype(jnp.float32)[:, None]
    windows = [
        (positions - offset >= seq_start).astype(jnp.float32)[:, None] for offset in range(CONV)
    ]
    hidden = rms_scale(stream, norm_gain).astype(jnp.bfloat16)
    branch = forward_product(hidden, w_branch)
    inputs = forward_product(hidden, w_input)
    tail_rows = shifted(inputs[row_count - edge_rows :], "seq", 1)
    extended = jnp.concatenate([tail_rows, inputs], axis=0)
    convolved = conv_bias + jnp.zeros_like(inputs)
    for offset in range(CONV):
        convolved = (
            convolved
            + conv_weight[offset]
            * extended[edge_rows - offset : edge_rows - offset + row_count]
            * windows[offset]
        )
    conv_low = convolved.astype(jnp.bfloat16)
    conv_float = conv_low.astype(jnp.float32)
    heads_local = w_recur.shape[0]
    block_width = w_recur.shape[1]
    blocked = conv_low.reshape(row_count, heads_local, block_width)
    recur = jnp.einsum(
        "thb,hbe->the", blocked, w_recur, preferred_element_type=jnp.float32
    ).reshape(row_count, -1)
    ingate = jnp.einsum(
        "thb,hbe->the", blocked, w_ingate, preferred_element_type=jnp.float32
    ).reshape(row_count, -1)
    keep_rate, drive_term = gates(recur, ingate, conv_float, decay_param, notstart)
    prefix_keep, local_states = group_scan(keep_rate, drive_term, False)
    carry_keep, carry_state = entering(
        (prefix_keep[-1], local_states[-1]),
        "seq",
        chain,
        (jnp.ones_like(decay_param), jnp.zeros_like(decay_param)),
        False,
    )
    states = local_states + prefix_keep * carry_state
    activated = jax.nn.gelu(branch)
    mixed = (states * activated).astype(jnp.bfloat16)
    resid = stream + lax.psum(forward_product(mixed, w_out), "mp")
    normed = rms_scale(resid, mlp_gain).astype(jnp.bfloat16)
    gate_pre = forward_product(normed, w_gate)
    up_pre = forward_product(normed, w_up)
    inner_act = (jax.nn.gelu(gate_pre) * up_pre).astype(jnp.bfloat16)
    mlp_share = lax.psum_scatter(
        forward_product(inner_act, w_down), "mp", scatter_dimension=1, tiled=True
    )
    resid_share = lax.dynamic_slice_in_dim(resid, my_model * slab_width, slab_width, 1)
    block_share = resid_share + mlp_share
    inner_grad = backward_product(upstream_low, w_down)
    grad_down = weight_product(inner_act, upstream_low)
    _, mlp_pull = jax.vjp(lambda gate_in, up_in: jax.nn.gelu(gate_in) * up_in, gate_pre, up_pre)
    gate_grad, up_grad = mlp_pull(inner_grad)
    gate_low = gate_grad.astype(jnp.bfloat16)
    up_low = up_grad.astype(jnp.bfloat16)
    grad_gate = weight_product(normed, gate_low)
    grad_up = weight_product(normed, up_low)
    normed_grad = lax.psum(
        backward_product(gate_low, w_gate) + backward_product(up_low, w_up), "mp"
    )
    _, second_pull = jax.vjp(rms_scale, resid, mlp_gain)
    resid_part, mlp_gain_full = second_pull(normed_grad)
    resid_grad = upstream + resid_part
    resid_low = resid_grad.astype(jnp.bfloat16)
    mixed_grad = backward_product(resid_low, w_out)
    grad_out = weight_product(mixed, resid_low)
    _, gelu_pull = jax.vjp(jax.nn.gelu, branch)
    (branch_grad,) = gelu_pull(mixed_grad * states)
    branch_low = branch_grad.astype(jnp.bfloat16)
    states_direct = mixed_grad * activated
    next_keep = jnp.concatenate([keep_rate[1:], jnp.ones_like(keep_rate[:1])], axis=0)
    after_keep, local_grad = group_scan(next_keep, states_direct, True)
    keep_behind, back_carry = entering(
        (prefix_keep[-1], keep_rate[0] * local_grad[0]),
        "seq",
        chain,
        (jnp.ones_like(decay_param), jnp.zeros_like(decay_param)),
        True,
    )
    states_grad = local_grad + after_keep * back_carry
    previous = jnp.concatenate([carry_state[None, :], states[:-1]], axis=0)
    _, gate_pull = jax.vjp(
        lambda recur_in, ingate_in, conv_in, decay_in: gates(
            recur_in, ingate_in, conv_in, decay_in, notstart
        ),
        recur,
        ingate,
        conv_float,
        decay_param,
    )
    recur_grad, ingate_grad, conv_part, decay_grad = gate_pull(
        (states_grad * previous, states_grad)
    )
    recur_low = recur_grad.astype(jnp.bfloat16).reshape(row_count, heads_local, block_width)
    ingate_low = ingate_grad.astype(jnp.bfloat16).reshape(row_count, heads_local, block_width)
    grad_recur = jnp.einsum("thb,the->hbe", blocked, recur_low, preferred_element_type=jnp.float32)
    grad_ingate = jnp.einsum(
        "thb,the->hbe", blocked, ingate_low, preferred_element_type=jnp.float32
    )
    through_gates = jnp.einsum(
        "the,hbe->thb", recur_low, w_recur, preferred_element_type=jnp.float32
    ) + jnp.einsum("the,hbe->thb", ingate_low, w_ingate, preferred_element_type=jnp.float32)
    conv_grad = conv_part + through_gates.reshape(row_count, -1)
    grad_conv_bias = jnp.sum(conv_grad, axis=0)
    extended_grad = jnp.zeros_like(extended)
    tap_grads = []
    for offset in range(CONV):
        masked = conv_grad * windows[offset]
        tap_grads.append(
            jnp.sum(masked * extended[edge_rows - offset : edge_rows - offset + row_count], axis=0)
        )
        extended_grad = extended_grad.at[edge_rows - offset : edge_rows - offset + row_count].add(
            conv_weight[offset] * masked
        )
    grad_conv_weight = jnp.stack(tap_grads)
    returned = shifted(extended_grad[:edge_rows], "seq", -1)
    inputs_grad = extended_grad[edge_rows:] + jnp.pad(
        returned, ((row_count - edge_rows, 0), (0, 0))
    )
    inputs_low = inputs_grad.astype(jnp.bfloat16)
    grad_branch = weight_product(hidden, branch_low)
    grad_input = weight_product(hidden, inputs_low)
    hidden_grad = lax.psum(
        backward_product(branch_low, w_branch) + backward_product(inputs_low, w_input), "mp"
    )
    _, first_pull = jax.vjp(rms_scale, stream, norm_gain)
    stream_part, norm_gain_full = first_pull(hidden_grad)
    input_full = resid_grad + stream_part
    input_share = lax.dynamic_slice_in_dim(input_full, my_model * slab_width, slab_width, 1)
    norm_gain_share = lax.dynamic_slice_in_dim(norm_gain_full, my_model * slab_width, slab_width, 0)
    mlp_gain_share = lax.dynamic_slice_in_dim(mlp_gain_full, my_model * slab_width, slab_width, 0)
    sent_branch, sent_input, sent_out, sent_gate, sent_up, sent_down = (
        lax.psum_scatter(grad_branch, "seq", scatter_dimension=0, tiled=True),
        lax.psum_scatter(grad_input, "seq", scatter_dimension=0, tiled=True),
        lax.psum_scatter(grad_out, "seq", scatter_dimension=1, tiled=True),
        lax.psum_scatter(grad_gate, "seq", scatter_dimension=0, tiled=True),
        lax.psum_scatter(grad_up, "seq", scatter_dimension=0, tiled=True),
        lax.psum_scatter(grad_down, "seq", scatter_dimension=1, tiled=True),
    )
    summed = lax.psum(
        (
            norm_gain_share,
            grad_conv_weight,
            grad_conv_bias,
            grad_recur,
            grad_ingate,
            decay_grad,
            mlp_gain_share,
        ),
        "seq",
    )
    back_rows = (
        block_share[landing].reshape(shard_count, per_peer, slab_width),
        input_share[landing].reshape(shard_count, per_peer, slab_width),
    )
    home_out, home_grad = (
        lax.all_to_all(back_rows[0], "seq", split_axis=0, concat_axis=0, tiled=True),
        lax.all_to_all(back_rows[1], "seq", split_axis=0, concat_axis=0, tiled=True),
    )
    restore = jnp.argsort(send_order)
    block_out = home_out.reshape(row_count, slab_width)[restore]
    input_grad = home_grad.reshape(row_count, slab_width)[restore]
    return (
        block_out,
        input_grad,
        summed[0],
        sent_branch,
        sent_input,
        summed[1],
        summed[2],
        summed[3],
        summed[4],
        summed[5],
        sent_out,
        summed[6],
        sent_gate,
        sent_up,
        sent_down,
    )


def solution(mesh):
    in_specs = (
        P("seq", None),
        P("seq", None),
        P(),
        P(),
        P(),
        P(None, "mp"),
        P(None, "mp"),
        P(None, "mp"),
        P("mp"),
        P("mp", None, None),
        P("mp", None, None),
        P("mp"),
        P("mp", None),
        P(),
        P(None, "mp"),
        P(None, "mp"),
        P("mp", None),
    )
    out_specs = (
        P("seq", "mp"),
        P("seq", "mp"),
        P("mp"),
        P("seq", "mp"),
        P("seq", "mp"),
        P(None, "mp"),
        P("mp"),
        P("mp", None, None),
        P("mp", None, None),
        P("mp"),
        P("mp", "seq"),
        P("mp"),
        P("seq", "mp"),
        P("seq", "mp"),
        P("mp", "seq"),
    )
    return jax.shard_map(shards, mesh=mesh, in_specs=in_specs, out_specs=out_specs, check_vma=False)
```

profile of v0, /device:TPU:0, one launch (start us, length us, event | category | flops | bytes accessed | tf_op | source)
XLA Modules:
  0.0 2740.7 jit_solution(7376674607496513680)
XLA Ops:
  12.4 11.6 gather_fusion
  42.0 36.6 %all-to-all-done = bf16[8,128,2048]{2,1,0:T(8,128)(2,1)} async-done(((bf16[8,128,2048]{2,1,0:T(8,128)(2,1)}), bf16[8,128,2048]{2,1,0:T(8,128)(2,1)}, u32[]{:S(2)}, u32[]{:S(2)}) %all-to-all-start) | async-done | bytes 4194336 | tf_op jit(solution)/shard_map/all_to_all | solution.py:136
  78.6 11.6 gather_fusion.1
  103.4 9.2 add_convert_fusion
  151.9 11.0 fusion.105
  164.9 8.6 multiply_add_fusion.13
  173.4 10.4 slice_multiply_fusion.10
  215.1 8.5 slice.707
  223.6 9.0 slice.708
  232.6 9.4 slice.706
  242.0 8.5 slice.710
  357.6 8.9 slice.705
  366.5 8.9 slice.754
  487.5 8.3 pad.436
  513.8 8.3 pad.317
  550.6 9.3 stack.19
  559.9 9.4 stack.18
  584.1 15.1 all-gather.1
  607.7 10.3 multiply_convert_fusion.4
  625.5 11.6 gather_fusion.4
  637.1 54.2 %all_to_all.20 = bf16[8,128,2048]{2,1,0:T(8,128)(2,1)} all-to-all(bf16[8,128,2048]{2,1,0:T(8,128)(2,1)} %bitcast.283), channel_id=1, replica_groups=mesh['seq'=8,'mp'=4] {'seq'}, dimensions={0} | all-to-all | bytes 8388608 | tf_op jit(solution)/shard_map/all_to_all | solution.py:137
  691.3 11.8 gather_fusion.5
  703.1 214.1 %all-reduce.70.cloned.1.call-done = f32[1024,2048]{1,0:T(8,128)} async-done(((f32[1024,2048]{1,0:T(8,128)}), f32[1024,2048]{1,0:T(8,128)}) %all-reduce.70.cloned.1.call-update) | async-done | bytes 8388624 | tf_op jit(solution)/shard_map/psum | solution.py:193
  926.1 12.0 fusion.119
  938.1 10.6 fusion.120
  948.8 17.1 multiply_convert_fusion.2
  965.9 10.0 fusion.122
  975.9 10.9 convolution_add_fusion.1
  1000.9 10.5 slice_multiply_fusion.9
  1023.6 9.3 stack.21
  1032.9 11.7 fusion.121
  1044.7 232.1 %all-reduce.72.cloned.1.call-done = f32[1024,2048]{1,0:T(8,128)} async-done(((f32[1024,2048]{1,0:T(8,128)}), f32[1024,2048]{1,0:T(8,128)}) %all-reduce.72.cloned.1.call-update) | async-done | bytes 8388624 | tf_op jit(solution)/shard_map/psum | solution.py:211
  1291.9 11.6 fusion.32
  1307.0 22.0 multiply_add_fusion.5
  1333.7 10.5 fusion.104
  1357.7 9.0 slice.794
  1366.8 8.6 slice.796
  1375.4 8.5 slice.792
  1383.9 9.0 slice.799
  1523.6 9.2 slice.790
  1532.8 9.2 slice.844
  1668.6 8.3 pad.438
  1711.3 8.4 pad.439
  1739.4 9.4 stack.20
  1766.2 9.0 all-gather.2
  1790.9 9.0 multiply_reduce_fusion.6
  1829.6 10.1 multiply_reduce_fusion.9
  1845.2 15.5 scatter-add.15
  1865.9 15.5 scatter-add.16
  1904.1 10.1 fusion.27
  1914.9 8.4 fusion.99
  1923.3 9.1 fusion.78
  1932.7 12.5 fusion.126
  1945.2 12.5 fusion.127
  1957.8 12.3 fusion.128
  1995.3 197.1 %all-reduce.74.cloned.1.call-done = f32[1024,2048]{1,0:T(8,128)} async-done(((f32[1024,2048]{1,0:T(8,128)}), f32[1024,2048]{1,0:T(8,128)}) %all-reduce.74.cloned.1.call-update) | async-done | bytes 8388624 | tf_op jit(solution)/shard_map/psum | solution.py:276
  2219.5 38.2 %all-reduce.76.cloned.1.call-done = (f32[4,171,171]{2,1,0:T(8,128)}, f32[4,171,171]{2,1,0:T(8,128)}) async-done(((f32[4,171,171]{2,1,0:T(8,128)}, f32[4,171,171]{2,1,0:T(8,128)}), (f32[4,171,171]{2,1,0:T(8,128)}, f32[4,171,171]{2,1,0:T(8,128)})) %all-reduce.76.cloned.1.call-update) | async-done | bytes 935728 | tf_op jit(solution)/shard_map/psum | solution.py:293
  2262.5 23.0 all-reduce.63
  2299.2 20.1 reduce-scatter.14.cloned.1.call-done
  2319.4 62.5 %reduce-scatter.10.cloned.1.call-done = f32[256,684]{0,1:T(8,128)} async-done(((f32[2048,684]{0,1:T(8,128)}), f32[256,684]{0,1:T(8,128)}) %reduce-scatter.10.cloned.1.call-update) | async-done | bytes 700432 | tf_op jit(solution)/shard_map/reduce_scatter | solution.py:286
  2381.9 62.5 %reduce-scatter.12.cloned.1.call-done = f32[256,684]{0,1:T(8,128)} async-done(((f32[2048,684]{0,1:T(8,128)}), f32[256,684]{0,1:T(8,128)}) %reduce-scatter.12.cloned.1.call-update) | async-done | bytes 700432 | tf_op jit(solution)/shard_map/reduce_scatter | solution.py:287
  2444.4 96.3 %reduce-scatter.16.cloned.1.call-done = f32[256,1536]{1,0:T(8,128)} async-done(((f32[2048,1536]{1,0:T(8,128)}), f32[256,1536]{1,0:T(8,128)}) %reduce-scatter.16.cloned.1.call-update) | async-done | bytes 1572880 | tf_op jit(solution)/shard_map/reduce_scatter | solution.py:289
  2540.7 96.5 %reduce-scatter.18.cloned.1.call-done = f32[256,1536]{1,0:T(8,128)} async-done(((f32[2048,1536]{1,0:T(8,128)}), f32[256,1536]{1,0:T(8,128)}) %reduce-scatter.18.cloned.1.call-update) | async-done | bytes 1572880 | tf_op jit(solution)/shard_map/reduce_scatter | solution.py:290
  2637.3 96.4 %reduce-scatter.20.cloned.1.call-done = f32[1536,256]{1,0:T(8,128)} async-done(((f32[1536,2048]{1,0:T(8,128)}), f32[1536,256]{1,0:T(8,128)}) %reduce-scatter.20.cloned.1.call-update) | async-done | bytes 1572880 | tf_op jit(solution)/shard_map/reduce_scatter | solution.py:291
  (633 shorter events, 961.8 us)
Async XLA Ops:
  7.2 600.5 %copy-start = (bf16[2048,684]{0,1:T(8,128)(2,1)S(1)}, bf16[2048,684]{0,1:T(8,128)(2,1)}, u32[]{:S(2)}) copy-start(bf16[2048,684]{0,1:T(8,128)(2,1)} %param.34) | copy-start | bytes 8404996
  12.4 11.6 copy-start.83
  12.4 11.6 copy-start.70
  24.1 54.5 %all-to-all-start = ((bf16[8,128,2048]{2,1,0:T(8,128)(2,1)}), bf16[8,128,2048]{2,1,0:T(8,128)(2,1)}, u32[]{:S(2)}, u32[]{:S(2)}) async-start(bf16[8,128,2048]{2,1,0:T(8,128)(2,1)} %bitcast.282), calls=%async_computation | async-start | bytes 8388608 | tf_op jit(solution)/shard_map/all_to_all | solution.py:136
  30.1 887.0 %all-reduce.70.cloned.1.call-start = ((), (), s32[]{:S(2)}) async-start(), calls=%async_computation.11 | async-start | bytes 16777216 | tf_op jit(solution)/shard_map/psum | solution.py:193
  31.1 72.2 %copy-start.57 = (f32[1024]{0:T(1024)}, f32[1024]{0:T(1024)S(1)}, u32[]{:S(2)}) copy-start(f32[1024]{0:T(1024)S(1)} %get-tuple-element.1005) | copy-start | bytes 12292
  31.1 72.2 %copy-start.59 = (f32[1024]{0:T(1024)}, f32[1024]{0:T(1024)S(1)}, u32[]{:S(2)}) copy-start(f32[1024]{0:T(1024)S(1)} %get-tuple-element.1006) | copy-start | bytes 12292
  31.1 72.2 %copy-start.61 = (f32[1024]{0:T(1024)}, f32[1024]{0:T(1024)S(1)}, u32[]{:S(2)}) copy-start(f32[1024]{0:T(1024)S(1)} %get-tuple-element.1004) | copy-start | bytes 12292
  31.1 72.2 %copy-start.63 = (f32[1024]{0:T(1024)}, f32[1024]{0:T(1024)S(1)}, u32[]{:S(2)}) copy-start(f32[1024]{0:T(1024)S(1)} %get-tuple-element.1007) | copy-start | bytes 12292
  31.8 131.1 %copy-start.54 = (f32[684]{0:T(1024)}, f32[684]{0:T(1024)S(1)}, u32[]{:S(2)}) copy-start(f32[684]{0:T(1024)S(1)} %broadcast_multiply_fusion.2) | copy-start | bytes 8212
  42.0 48.1 %copy-start.72 = (s32[1024]{0:T(1024)}, s32[1024]{0:T(1024)S(1)}, u32[]{:S(2)}) copy-start(s32[1024]{0:T(1024)S(1)} %fusion.82) | copy-start | bytes 12292
  100.8 2.6 collective-permute-start
  102.9 12.5 copy-start.66
  102.9 12.5 copy-start.68
  103.4 12.1 copy-start.47
  103.4 12.1 copy-start.51
  151.9 11.1 copy-start.18
  151.9 11.1 copy-start.53
  183.8 16.9 copy-start.34
  201.8 9.4 copy-start.42
  215.1 48.7 %copy-start.19 = (f32[128,684]{0,1:T(8,128)}, f32[128,684]{0,1:T(8,128)S(1)}, u32[]{:S(2)}) copy-start(f32[128,684]{0,1:T(8,128)S(1)} %get-tuple-element.937) | copy-start | bytes 1050628
  215.1 48.6 %copy-start.21 = (f32[128,684]{0,1:T(8,128)}, f32[128,684]{0,1:T(8,128)S(1)}, u32[]{:S(2)}) copy-start(f32[128,684]{0,1:T(8,128)S(1)} %get-tuple-element.938) | copy-start | bytes 1050628
  276.2 20.9 copy-start.24
  276.2 20.9 copy-start.26
  325.4 32.2 %copy-start.20 = (f32[128,684]{0,1:T(8,128)S(1)}, f32[128,684]{0,1:T(8,128)}, u32[]{:S(2)}) copy-start(f32[128,684]{0,1:T(8,128)} %copy-done.19) | copy-start | bytes 1050628
  328.5 37.9 %copy-start.22 = (f32[128,684]{0,1:T(8,128)S(1)}, f32[128,684]{0,1:T(8,128)}, u32[]{:S(2)}) copy-start(f32[128,684]{0,1:T(8,128)} %copy-done.21) | copy-start | bytes 1050628
  513.8 13.8 copy-start.45
  536.8 13.8 copy-start.35
  559.9 9.4 copy-start.43
  580.6 27.1 copy-start.79
  580.6 27.1 copy-start.89
  607.7 11.4 copy-start.91
  624.9 652.0 %all-reduce.72.cloned.1.call-start = ((), (), s32[]{:S(2)}) async-start(), calls=%async_computation.13 | async-start | bytes 16777216 | tf_op jit(solution)/shard_map/psum | solution.py:211
  637.1 54.2 %copy-start.73 = (s32[1024]{0:T(1024)S(1)}, s32[1024]{0:T(1024)}, u32[]{:S(2)}) copy-start(s32[1024]{0:T(1024)} %copy-done.72) | copy-start | bytes 12292
  703.1 219.8 %copy-start.56 = (f32[2048]{0:T(1024)S(1)}, f32[2048]{0:T(1024)}, u32[]{:S(2)}) copy-start(f32[2048]{0:T(1024)} %param.42) | copy-start | bytes 24580
  926.1 12.0 copy-start.33
  938.1 10.6 copy-start.10
  965.9 10.0 copy-start.97
  965.9 10.0 copy-start.98
  986.8 984.1 %reduce-scatter.8.cloned.1.call-start = ((), (), s32[]{:S(2)}) async-start(), calls=%async_computation.12 | async-start | bytes 10485760 | tf_op jit(solution)/shard_map/reduce_scatter | solution.py:198
  1000.9 10.5 copy-start.6
  1044.6 1147.8 %all-reduce.74.cloned.1.call-start = ((), (), s32[]{:S(2)}) async-start(), calls=%async_computation.14 | async-start | bytes 16777216 | tf_op jit(solution)/shard_map/psum | solution.py:276
  1276.8 10.2 copy-start.11
  1291.9 11.6 copy-start.12
  1357.7 47.0 %copy-start.30 = (f32[128,684]{0,1:T(8,128)}, f32[128,684]{0,1:T(8,128)S(1)}, u32[]{:S(2)}) copy-start(f32[128,684]{0,1:T(8,128)S(1)} %get-tuple-element.935) | copy-start | bytes 1050628
  1357.7 47.0 %copy-start.31 = (f32[128,684]{0,1:T(8,128)}, f32[128,684]{0,1:T(8,128)S(1)}, u32[]{:S(2)}) copy-start(f32[128,684]{0,1:T(8,128)S(1)} %get-tuple-element.936) | copy-start | bytes 1050628
  1678.8 20.5 copy-start.40
  1781.6 9.3 copy-start.46
  1781.6 9.3 copy-start.82
  1790.9 9.0 copy-start.4
  1829.6 10.1 copy-start.77
  1845.2 15.5 copy-start.67
  1865.9 15.5 copy-start.76
  1886.2 4.9 collective-permute-start.1
  1898.8 358.8 %all-reduce.76.cloned.1.call-start = ((), (), s32[]{:S(2)}) async-start(), calls=%async_computation.21 | async-start | bytes 2883584 | tf_op jit(solution)/shard_map/psum | solution.py:293
  1903.7 415.7 %reduce-scatter.14.cloned.1.call-start = ((), (), s32[]{:S(2)}) async-start(), calls=%async_computation.17 | async-start | bytes 6340608 | tf_op jit(solution)/shard_map/reduce_scatter | solution.py:288
  1914.2 467.6 %reduce-scatter.10.cloned.1.call-start = ((), (), s32[]{:S(2)}) async-start(), calls=%async_computation.15 | async-start | bytes 6340608 | tf_op jit(solution)/shard_map/reduce_scatter | solution.py:286
  1923.3 521.1 %reduce-scatter.12.cloned.1.call-start = ((), (), s32[]{:S(2)}) async-start(), calls=%async_computation.16 | async-start | bytes 6340608 | tf_op jit(solution)/shard_map/reduce_scatter | solution.py:287
  1932.4 608.3 %reduce-scatter.16.cloned.1.call-start = ((), (), s32[]{:S(2)}) async-start(), calls=%async_computation.18 | async-start | bytes 14155776 | tf_op jit(solution)/shard_map/reduce_scatter | solution.py:289
  1945.2 692.1 %reduce-scatter.18.cloned.1.call-start = ((), (), s32[]{:S(2)}) async-start(), calls=%async_computation.19 | async-start | bytes 14155776 | tf_op jit(solution)/shard_map/reduce_scatter | solution.py:290
  1957.8 775.8 %reduce-scatter.20.cloned.1.call-start = ((), (), s32[]{:S(2)}) async-start(), calls=%async_computation.20 | async-start | bytes 14155776 | tf_op jit(solution)/shard_map/reduce_scatter | solution.py:291
  1981.8 228.0 %all-to-all-start.1 = ((f32[8,128,512]{2,1,0:T(8,128)}), f32[8,128,512]{2,1,0:T(8,128)}, u32[]{:S(2)}, u32[]{:S(2)}) async-start(f32[8,128,512]{2,1,0:T(8,128)} %bitcast.303), calls=%async_computation.2 | async-start | bytes 4194304 | tf_op jit(solution)/shard_map/all_to_all | solution.py:310
  1995.3 203.3 %copy-start.75 = (f32[1024]{0:T(1024)S(1)}, f32[1024]{0:T(1024)}, u32[]{:S(2)}) copy-start(f32[1024]{0:T(1024)} %copy-done.74) | copy-start | bytes 12292
  2209.8 82.5 %all-to-all-start.3 = ((f32[8,128,512]{2,1,0:T(8,128)}), f32[8,128,512]{2,1,0:T(8,128)}, u32[]{:S(2)}, u32[]{:S(2)}) async-start(f32[8,128,512]{2,1,0:T(8,128)} %bitcast.302), calls=%async_computation.4 | async-start | bytes 4194304 | tf_op jit(solution)/shard_map/all_to_all | solution.py:311
  (52 other events, 198.9 us)
Sparse Core Ops, SparseCore 0:
  33.2 3.4 sort.63.cloned.1.call-done
  625.0 292.0 all-reduce.69
  987.0 289.8 all-reduce.71
  1279.2 143.4 reduce-scatter.7
  1898.9 293.4 all-reduce.73
  2195.8 61.7 all-reduce.75
  2261.7 57.6 reduce-scatter.13
  2323.4 58.4 reduce-scatter.9
  2385.9 58.4 reduce-scatter.11
  2448.3 92.3 reduce-scatter.15
  2544.8 92.3 reduce-scatter.17
  2641.2 92.3 reduce-scatter.19
  (1 shorter events, 0.0 us)
where the time goes:
time: 2760 us; the launch traced here: 2740 us
  waiting for transfers between devices  1150 us (42%)
  local copies, waits for them, and re-layouts  931 us (34%)
  other arithmetic  310 us (11%)
  matrix products  201 us (7%)
  blocking collectives  109 us (4%)
    slice x77, local copies, waits for them, and re-layouts, group_scan(): lax.associative_scan(chain, (run_keep, run_state), reverse=reverse)  335 us
    psum x1, waiting for transfers between devices, shards(): lax.psum(backward_product(gate_low, w_gate) + backward_product(up_low, w_...  232 us
    psum x1, waiting for transfers between devices, shards(): resid = stream + lax.psum(forward_product(mixed, w_out), 'mp')  214 us
    psum x1, waiting for transfers between devices, shards(): lax.psum(backward_product(branch_low, w_branch) + backward_product(inputs...  197 us
    pad x40, local copies, waits for them, and re-layouts, group_scan(): lax.associative_scan(chain, (run_keep, run_state), reverse=reverse)  143 us
    reduce_scatter x1, waiting for transfers between devices, shards(): lax.psum_scatter(grad_up, 'seq', scatter_dimension=0, tiled=True)  96.5 us
    reduce_scatter x1, waiting for transfers between devices, shards(): lax.psum_scatter(grad_down, 'seq', scatter_dimension=1, tiled=True)  96.4 us
    reduce_scatter x1, waiting for transfers between devices, shards(): lax.psum_scatter(grad_gate, 'seq', scatter_dimension=0, tiled=True)  96.3 us
  transfers between devices with their start and end apart: 16, of which 12 were waited for; matrix products, arithmetic and copies ran while one was open for 30% of the time, Pallas kernels for 0%

commit v1 on v0

v1 whole, which is shorter than its diff:
```python
import functools

import jax
import jax.numpy as jnp
import numpy as np
from jax import lax
from jax.experimental import pallas as pl
from jax.experimental.pallas import tpu as pltpu
from jax.sharding import PartitionSpec as P

CONV = 4
EPSILON = 1e-06
GATE_POWER = 8.0
ROOT_FLOOR = 0.01
LANES = 128
GROUP = 8
CHUNKS = 2
F32 = jnp.float32
BF16 = jnp.bfloat16
MIB = 1 << 20
GELU_A = 0.7978845608028654
GELU_B = 0.044715

NN = (((1,), (0,)), ((), ()))
NT = (((1,), (1,)), ((), ()))
TN = (((0,), (0,)), ((), ()))


def mm(left, right, dims=NN):
    return lax.dot_general(left, right, dims, preferred_element_type=F32)


def call(body, grid, in_specs, out_specs, out_shape, scratch=(), prefetch=0, aliases=None, flops=0, moved=0):
    return pl.pallas_call(
        body,
        grid_spec=pltpu.PrefetchScalarGridSpec(
            num_scalar_prefetch=prefetch,
            grid=grid,
            in_specs=in_specs,
            out_specs=out_specs,
            scratch_shapes=list(scratch),
        ),
        out_shape=out_shape,
        input_output_aliases=aliases or {},
        compiler_params=pltpu.CompilerParams(
            dimension_semantics=("arbitrary",) * len(grid), vmem_limit_bytes=60 * MIB
        ),
        cost_estimate=pl.CostEstimate(flops=flops, bytes_accessed=moved, transcendentals=0),
    )


def whole(shape):
    zeros = (0,) * len(shape)
    return pl.BlockSpec(shape, lambda *_: zeros)


def struct(shape, dtype):
    return jax.ShapeDtypeStruct(shape, dtype)


def sigmoid(x):
    return 0.5 * jnp.tanh(0.5 * x) + 0.5


def gelu(x):
    return 0.5 * x * (1.0 + jnp.tanh(GELU_A * (x + GELU_B * x * x * x)))


def gelu_both(x):
    square = x * x
    t = jnp.tanh(GELU_A * x * (1.0 + GELU_B * square))
    half = 0.5 * (1.0 + t)
    slope = half + 0.5 * x * (1.0 - t * t) * (GELU_A * (1.0 + 3.0 * GELU_B * square))
    return x * half, slope


def softplus_neg(x):
    return jnp.log1p(jnp.exp(-jnp.abs(x))) + jnp.maximum(-x, 0.0)


def one_hot(rows, lanes):
    return jnp.where(rows == lanes, 1.0, 0.0).astype(BF16)


def send_order(turn, dest_row, dest_col, values):
    rows, width = values.shape
    tile = 256

    def body(turn_ref, row_ref, col_ref, val_ref, out_ref, rank_ref):
        i = pl.program_id(0)

        @pl.when(i == 0)
        def _():
            before = jnp.where(col_ref[...] < row_ref[...], 1.0, 0.0)
            rank = jnp.sum(before, axis=0, keepdims=True).astype(jnp.int32)
            rank_ref[...] = rank ^ turn_ref[0]

        place = lax.broadcasted_iota(jnp.int32, (tile, rows), 0) + i * tile
        out_ref[...] = mm(one_hot(place, rank_ref[...]), val_ref[...]).astype(BF16)

    return call(
        body,
        (rows // tile,),
        [whole((1, rows)), whole((rows, 1)), whole((rows, width))],
        pl.BlockSpec((tile, width), lambda i, *_: (i, 0)),
        struct((rows, width), BF16),
        [pltpu.VMEM((1, rows), jnp.int32)],
        prefetch=1,
        flops=2 * rows * rows * width,
        moved=4 * rows * width,
    )(turn, dest_row, dest_col, values)


def place_rows(place_col, landing_row, values):
    rows, width = values.shape
    tile = 256

    def body(place_ref, land_ref, val_ref, out_ref):
        out_ref[...] = mm(one_hot(place_ref[...], land_ref[...]), val_ref[...]).astype(out_ref.dtype)

    return call(
        body,
        (rows // tile,),
        [pl.BlockSpec((tile, 1), lambda i: (i, 0)), whole((1, rows)), whole((rows, width))],
        pl.BlockSpec((tile, width), lambda i: (i, 0)),
        struct((rows, width), BF16),
        flops=2 * rows * rows * width,
        moved=4 * rows * width,
    )(place_col, landing_row, values)


def split_columns(near_ref, far_ref, values, parity, parts):
    size = values.shape[1] // parts
    for q in range(parts // 2):
        to = slice(q * size, (q + 1) * size)
        even = values[:, 2 * q * size : (2 * q + 1) * size]
        odd = values[:, (2 * q + 1) * size : (2 * q + 2) * size]
        near_ref[:, to] = jnp.where(parity == 0, even, odd)
        far_ref[:, to] = jnp.where(parity == 0, odd, even)


def place_upstream(place, place_col, landing_row, blocks, parts):
    count = len(blocks)
    size, width = blocks[0].shape
    rows = count * size
    tile = 256

    def body(my_ref, place_ref, land_ref, *refs):
        out_ref, near_ref, far_ref, val_ref, sem = refs[count:]

        @pl.when(pl.program_id(0) == 0)
        def _():
            copies = [
                pltpu.make_async_copy(refs[k], val_ref.at[k * size : (k + 1) * size], sem.at[k])
                for k in range(count)
            ]
            for copy in copies:
                copy.start()
            for copy in copies:
                copy.wait()

        moved = mm(one_hot(place_ref[...], land_ref[...]), val_ref[...])
        out_ref[...] = moved.astype(BF16)
        split_columns(near_ref, far_ref, moved.astype(BF16), my_ref[2], parts)

    return call(
        body,
        (rows // tile,),
        [pl.BlockSpec((tile, 1), lambda i, *_: (i, 0)), whole((1, rows))]
        + [pl.BlockSpec(memory_space=pl.ANY)] * count,
        [
            pl.BlockSpec((tile, width), lambda i, *_: (i, 0)),
            pl.BlockSpec((tile, width // 2), lambda i, *_: (i, 0)),
            pl.BlockSpec((tile, width // 2), lambda i, *_: (i, 0)),
        ],
        [
            struct((rows, width), BF16),
            struct((rows, width // 2), BF16),
            struct((rows, width // 2), BF16),
        ],
        [pltpu.VMEM((rows, width), BF16), pltpu.SemaphoreType.DMA((count,))],
        prefetch=1,
        flops=2 * rows * rows * width,
        moved=6 * rows * width,
    )(place, place_col, landing_row, *blocks)


def restore_rows(dest_row, dest_col, values):
    rows, width = values.shape
    tile = 256

    def body(row_ref, col_ref, val_ref, out_ref):
        before = jnp.where(row_ref[...] < col_ref[...], 1.0, 0.0)
        rank = jnp.sum(before, axis=1, keepdims=True).astype(jnp.int32)
        spot = lax.broadcasted_iota(jnp.int32, (tile, rows), 1)
        out_ref[...] = mm(one_hot(spot, rank), val_ref[...])

    return call(
        body,
        (rows // tile,),
        [whole((1, rows)), pl.BlockSpec((tile, 1), lambda i: (i, 0)), whole((rows, width))],
        pl.BlockSpec((tile, width), lambda i: (i, 0)),
        struct((rows, width), F32),
        flops=2 * rows * rows * width,
        moved=6 * rows * width,
    )(dest_row, dest_col, values)


def project(place, landing_row, arrived, gain, weights, parts):
    rows, width = arrived.shape
    wide = weights.shape[1]
    half = wide // 2
    tile = 256

    def body(
        my_ref, land_ref, arr_ref, gain_ref, w_ref, stream_ref, near_ref, far_ref, branch_ref, inputs_ref
    ):
        i = pl.program_id(0)
        place = lax.broadcasted_iota(jnp.int32, (tile, rows), 0) + i * tile
        x = mm(one_hot(place, land_ref[...]), arr_ref[...])
        stream_ref[...] = x.astype(BF16)
        inv = lax.rsqrt(jnp.mean(x * x, axis=-1, keepdims=True) + EPSILON)
        hidden = (x * inv * gain_ref[...]).astype(BF16)
        split_columns(near_ref, far_ref, hidden, my_ref[2], parts)
        branch_ref[...] = mm(hidden, w_ref[:, :half])
        inputs_ref[...] = mm(hidden, w_ref[:, half:])

    return call(
        body,
        (rows // tile,),
        [whole((1, rows)), whole((rows, width)), whole((1, width)), whole((width, wide))],
        [
            pl.BlockSpec((tile, width), lambda i, *_: (i, 0)),
            pl.BlockSpec((tile, width // 2), lambda i, *_: (i, 0)),
            pl.BlockSpec((tile, width // 2), lambda i, *_: (i, 0)),
            pl.BlockSpec((tile, half), lambda i, *_: (i, 0)),
            pl.BlockSpec((tile, half), lambda i, *_: (i, 0)),
        ],
        [
            struct((rows, width), BF16),
            struct((rows, width // 2), BF16),
            struct((rows, width // 2), BF16),
            struct((rows, half), F32),
            struct((rows, half), F32),
        ],
        prefetch=1,
        flops=2 * rows * width * (rows + wide),
        moved=6 * rows * width + 2 * width * wide + 4 * rows * wide,
    )(place, landing_row, arrived, gain, weights)


def tile_scan(rates, drives, keep_in, state_in, reverse):
    rows, lanes = rates.shape
    groups = rows // GROUP
    a = rates.reshape(groups, GROUP, lanes)
    d = drives.reshape(groups, GROUP, lanes)
    spot = lax.broadcasted_iota(jnp.int32, (groups, GROUP, lanes), 1)
    for by in (1, 2, 4):
        turn = GROUP - by if reverse else by
        ok = spot < GROUP - by if reverse else spot >= by
        d_near = pltpu.roll(d, turn, 1)
        a_near = pltpu.roll(a, turn, 1)
        d = jnp.where(ok, a * d_near + d, d)
        a = jnp.where(ok, a * a_near, a)
    end = 0 if reverse else GROUP - 1
    keeps, states = [None] * groups, [None] * groups
    for g in range(groups - 1, -1, -1) if reverse else range(groups):
        keeps[g] = a[g] * keep_in
        states[g] = d[g] + a[g] * state_in
        keep_in = keeps[g][end : end + 1]
        state_in = states[g][end : end + 1]
    return jnp.concatenate(keeps, 0), jnp.concatenate(states, 0), keep_in, state_in


def recurrent_forward(inputs, halo, dist, conv_weight, conv_bias, decay, gate_weights):
    rows, width = inputs.shape
    tile = 256
    last = rows // tile - 1

    def body(
        in_ref, halo_ref, dist_ref, cw_ref, cb_ref, dp_ref, gw_ref,
        conv_ref, pre_ref, keep_ref, prefix_ref, local_ref, tail_ref,
        ext, carry,
    ):
        i = pl.program_id(0)

        @pl.when(i == 0)
        def _():
            ext[0:8] = halo_ref[...]
            carry[0:1] = jnp.ones((1, width), F32)
            carry[1:2] = jnp.zeros((1, width), F32)

        @pl.when(i > 0)
        def _():
            ext[0:8] = ext[tile : tile + 8]

        ext[8 : 8 + tile] = in_ref[...]
        dist = dist_ref[...]
        conv = cb_ref[...] + cw_ref[0:1] * ext[8 : 8 + tile]
        for k in range(1, CONV):
            conv = conv + jnp.where(dist >= k, cw_ref[k : k + 1] * ext[8 - k : 8 - k + tile], 0.0)
        conv_low = conv.astype(BF16)
        conv_ref[...] = conv_low
        pre_ref[...] = mm(conv_low, gw_ref[...])
        notstart = dist > 0
        for lane in range(0, width, LANES):
            cut = slice(lane, lane + LANES)
            far = slice(width + lane, width + lane + LANES)
            reset = sigmoid(pre_ref[:, cut])
            gate = sigmoid(pre_ref[:, far])
            keep = jnp.exp((-GATE_POWER * softplus_neg(dp_ref[:, cut])) * reset)
            drive = jnp.sqrt(1.0 - keep * keep + ROOT_FLOOR) * (gate * conv_ref[:, cut].astype(F32))
            rate = jnp.where(notstart, keep, 0.0)
            keep_ref[:, cut] = rate
            keeps, states, keep_out, state_out = tile_scan(
                rate, drive, carry[0:1, cut], carry[1:2, cut], False
            )
            prefix_ref[:, cut] = keeps
            local_ref[:, cut] = states
            carry[0:1, cut] = keep_out
            carry[1:2, cut] = state_out

        @pl.when(i == last)
        def _():
            tail_ref[...] = carry[...]

    tiles = pl.BlockSpec((tile, width), lambda i: (i, 0))
    return call(
        body,
        (rows // tile,),
        [
            tiles,
            whole((8, width)),
            pl.BlockSpec((tile, 1), lambda i: (i, 0)),
            whole((CONV, width)),
            whole((1, width)),
            whole((1, width)),
            whole((width, 2 * width)),
        ],
        [
            tiles,
            pl.BlockSpec((tile, 2 * width), lambda i: (i, 0)),
            tiles,
            tiles,
            tiles,
            whole((8, width)),
        ],
        [
            struct((rows, width), BF16),
            struct((rows, 2 * width), F32),
            struct((rows, width), F32),
            struct((rows, width), F32),
            struct((rows, width), F32),
            struct((8, width), F32),
        ],
        [pltpu.VMEM((tile + 8, width), F32), pltpu.VMEM((8, width), F32)],
        flops=4 * rows * width * width + 200 * rows * width,
        moved=30 * rows * width,
    )(inputs, halo, dist, conv_weight, conv_bias, decay, gate_weights)


def finish_states(place, pieces, local, prefix, branch, owners):
    rows, width = local.shape
    shards = pieces.shape[0]
    tile = rows // owners // CHUNKS

    def body(my_ref, pieces_ref, local_ref, prefix_ref, branch_ref, states_ref, mixed_ref, carry_ref):
        mine = my_ref[0]

        @pl.when(pl.program_id(0) == 0)
        def _():
            entering = jnp.zeros((1, width), F32)
            for s in range(shards - 1):
                longer = pieces_ref[s, 0:1] * entering + pieces_ref[s, 1:2]
                entering = jnp.where(s < mine, longer, entering)
            carry_ref[...] = jnp.broadcast_to(entering, (8, width))

        states = local_ref[...] + prefix_ref[...] * carry_ref[0:1]
        states_ref[...] = states
        mixed_ref[0, 0] = (states * gelu(branch_ref[...])).astype(BF16)

    tiles = pl.BlockSpec((tile, width), lambda i, *_: (i, 0))
    return call(
        body,
        (rows // tile,),
        [whole(pieces.shape), tiles, tiles, tiles],
        [
            tiles,
            pl.BlockSpec((1, 1, tile, width), lambda i, *_: (i % CHUNKS, i // CHUNKS, 0, 0)),
            whole((8, width)),
        ],
        [
            struct((rows, width), F32),
            struct((CHUNKS, owners, tile, width), BF16),
            struct((8, width), F32),
        ],
        prefetch=1,
        flops=60 * rows * width,
        moved=18 * rows * width,
    )(place, pieces, local, prefix, branch)


def output_rows(chunk, place, mixed_full, w_near, w_far, stream, gain):
    sources, own, width = mixed_full.shape
    model = stream.shape[1]
    half = model // 2

    def body(place_ref, mixed_ref, near_ref, far_ref, stream_ref, gain_ref, resid_ref, normed_ref):
        s = pl.program_id(0)
        near = pl.ds(pl.multiple_of(place_ref[2] * half, half), half)
        far = pl.ds(pl.multiple_of((1 - place_ref[2]) * half, half), half)

        @pl.when(s == 0)
        def _():
            resid_ref[...] = stream_ref[...].astype(F32)

        resid_ref[:, near] += mm(mixed_ref[0], near_ref[0])
        resid_ref[:, far] += mm(mixed_ref[0], far_ref[0])

        @pl.when(s == sources - 1)
        def _():
            x = resid_ref[...]
            inv = lax.rsqrt(jnp.mean(x * x, axis=-1, keepdims=True) + EPSILON)
            normed_ref[...] = (x * inv * gain_ref[...]).astype(BF16)

    return call(
        body,
        (sources,),
        [
            pl.BlockSpec((1, own, width), lambda s, *_: (s, 0, 0)),
            pl.BlockSpec((1, width, half), lambda s, *_: (s, 0, 0)),
            pl.BlockSpec((1, width, half), lambda s, *_: (s, 0, 0)),
            pl.BlockSpec((own, model), lambda s, p: (p[1] * CHUNKS + chunk, 0)),
            whole((1, model)),
        ],
        [whole((own, model)), whole((own, model))],
        [struct((own, model), F32), struct((own, model), BF16)],
        prefetch=1,
        flops=2 * sources * own * width * model,
        moved=2 * sources * width * model + 8 * own * model,
    )(place, mixed_full, w_near, w_far, stream, gain)


def mlp_chunk(chunk, place, normed, upstream, resid_own, w_gate, w_up, w_down, parts, kept):
    rows, model = normed.shape
    hidden = w_gate.shape[1]
    total = upstream.shape[0]
    sub = resid_own.shape[0]
    tile = 256 if hidden % 256 == 0 else LANES
    steps = hidden // tile

    def body(place_ref, n_ref, u_ref, r_ref, wg_ref, wu_ref, wd_ref, *rest):
        act_ref, gate_ref, up_ref, near_ref, far_ref, down_ref, grad_ref, down_acc, grad_acc = rest[-9:]
        s = pl.program_id(0)

        @pl.when(s == 0)
        def _():
            split_columns(near_ref, far_ref, n_ref[...], place_ref[2], parts)
            down_acc[...] = jnp.zeros_like(down_acc)
            own = pl.ds(pl.multiple_of(place_ref[1] * sub, sub), sub)
            down_acc[own, :] = r_ref[...]

        gate_pre = mm(n_ref[...], wg_ref[...])
        up_pre = mm(n_ref[...], wu_ref[...])
        inner = mm(u_ref[...], wd_ref[...], NT)
        act, slope = gelu_both(gate_pre)
        inner_act = (act * up_pre).astype(BF16)
        gate_low = (inner * up_pre * slope).astype(BF16)
        up_low = (inner * act).astype(BF16)
        act_ref[...] = inner_act
        gate_ref[...] = gate_low
        up_ref[...] = up_low
        down_acc[...] += mm(inner_act, wd_ref[...])
        both = mm(gate_low, wg_ref[...], NT) + mm(up_low, wu_ref[...], NT)

        @pl.when(s == 0)
        def _():
            grad_acc[...] = both

        @pl.when(s > 0)
        def _():
            grad_acc[...] += both

        @pl.when(s == steps - 1)
        def _():
            down_ref[...] = down_acc[...].astype(BF16)
            grad_ref[...] = grad_acc[...].astype(BF16)

    slots = pl.BlockSpec((rows, tile), lambda s, *_: (chunk, s))
    any_spec = pl.BlockSpec(memory_space=pl.ANY)
    kept = tuple(kept)
    return call(
        body,
        (steps,),
        [
            whole((rows, model)),
            pl.BlockSpec((rows, model), lambda s, *_: (chunk, 0)),
            whole((sub, model)),
            pl.BlockSpec((model, tile), lambda s, *_: (0, s)),
            pl.BlockSpec((model, tile), lambda s, *_: (0, s)),
            pl.BlockSpec((tile, model), lambda s, *_: (s, 0)),
        ]
        + [any_spec] * len(kept),
        [
            slots,
            slots,
            slots,
            pl.BlockSpec((rows, model // 2), lambda s, *_: (chunk, 0)),
            pl.BlockSpec((rows, model // 2), lambda s, *_: (chunk, 0)),
            pl.BlockSpec((rows, model), lambda s, *_: (chunk, 0)),
            whole((rows, model)),
        ],
        [
            struct((total, hidden), BF16),
            struct((total, hidden), BF16),
            struct((total, hidden), BF16),
            struct((total, model // 2), BF16),
            struct((total, model // 2), BF16),
            struct((total, model), BF16),
            struct((rows, model), BF16),
        ],
        [pltpu.VMEM((rows, model), F32), pltpu.VMEM((rows, model), F32)],
        prefetch=1,
        aliases={7 + j: j for j in range(len(kept))},
        flops=12 * rows * hidden * model,
        moved=6 * hidden * model + 10 * rows * model,
    )(place, normed, upstream, resid_own, w_gate, w_up, w_down, *kept)


def resid_backward(chunk, place, normed_grad, upstream, resid_own, gain, w_near, w_far):
    own, model = resid_own.shape
    sources, width, half = w_near.shape

    def body(place_ref, g_ref, up_ref, r_ref, gain_ref, near_ref, far_ref, rg_ref, low_ref, mg_ref, sum_ref):
        @pl.when(pl.program_id(0) == 0)
        def _():
            x = r_ref[...]
            g = g_ref[...].astype(F32)
            inv = lax.rsqrt(jnp.mean(x * x, axis=-1, keepdims=True) + EPSILON)
            unit = x * inv
            scaled = g * gain_ref[...]
            dot = jnp.mean(scaled * unit, axis=-1, keepdims=True)
            grad = up_ref[...].astype(F32) + inv * (scaled - unit * dot)
            rg_ref[...] = grad
            low_ref[...] = grad.astype(BF16)
            sum_ref[...] = jnp.sum(g * unit, axis=0, keepdims=True)

        near = pl.ds(pl.multiple_of(place_ref[2] * half, half), half)
        far = pl.ds(pl.multiple_of((1 - place_ref[2]) * half, half), half)
        mg_ref[0] = (mm(low_ref[:, near], near_ref[0], NT) + mm(low_ref[:, far], far_ref[0], NT)).astype(BF16)

    rows = whole((own, model))
    return call(
        body,
        (sources,),
        [
            rows,
            pl.BlockSpec((own, model), lambda s, p: (chunk * sources + p[1], 0)),
            rows,
            whole((1, model)),
            pl.BlockSpec((1, width, half), lambda s, *_: (s, 0, 0)),
            pl.BlockSpec((1, width, half), lambda s, *_: (s, 0, 0)),
        ],
        [rows, rows, pl.BlockSpec((1, own, width), lambda s, *_: (s, 0, 0)), whole((1, model))],
        [
            struct((own, model), F32),
            struct((own, model), BF16),
            struct((sources, own, width), BF16),
            struct((1, model), F32),
        ],
        prefetch=1,
        flops=2 * sources * own * width * model,
        moved=2 * sources * width * model + 14 * own * model,
    )(place, normed_grad, upstream, resid_own, gain, w_near, w_far)


def recurrent_back_scan(mixed_grads, branch, keep, tail):
    rows, width = branch.shape
    owners, sub = mixed_grads[0].shape[:2]
    tile = sub * CHUNKS
    tiles_n = owners

    def body(*refs):
        parts = refs[:CHUNKS]
        branch_ref, keep_ref, tail_ref, grad_ref, after_ref, edge_ref, mg_ref, ext, carry = refs[CHUNKS:]
        i = pl.program_id(0)
        for c in range(CHUNKS):
            mg_ref[c * sub : (c + 1) * sub] = parts[c][0]

        @pl.when(i == 0)
        def _():
            ext[tile : tile + 8] = jnp.ones((8, width), F32)
            carry[0:1] = jnp.ones((1, width), F32)
            carry[1:2] = jnp.zeros((1, width), F32)

        @pl.when(i > 0)
        def _():
            ext[tile : tile + 8] = ext[0:8]

        ext[0:tile] = keep_ref[...]
        for lane in range(0, width, LANES):
            cut = slice(lane, lane + LANES)
            direct = mg_ref[:, cut].astype(F32) * gelu(branch_ref[:, cut])
            keeps, grads, keep_out, grad_out = tile_scan(
                ext[1 : tile + 1, cut], direct, carry[0:1, cut], carry[1:2, cut], True
            )
            grad_ref[:, cut] = grads
            after_ref[:, cut] = keeps
            carry[0:1, cut] = keep_out
            carry[1:2, cut] = grad_out

        @pl.when(i == tiles_n - 1)
        def _():
            edge_ref[0:1] = tail_ref[0:1]
            edge_ref[1:2] = keep_ref[0:1] * carry[1:2]
            edge_ref[2:8] = jnp.zeros((6, width), F32)

    tiles = pl.BlockSpec((tile, width), lambda i: (tiles_n - 1 - i, 0))
    return call(
        body,
        (tiles_n,),
        [pl.BlockSpec((1, sub, width), lambda i: (tiles_n - 1 - i, 0, 0))] * CHUNKS
        + [tiles, tiles, whole((8, width))],
        [tiles, tiles, whole((8, width)), tiles],
        [
            struct((rows, width), F32),
            struct((rows, width), F32),
            struct((8, width), F32),
            struct((rows, width), BF16),
        ],
        [pltpu.VMEM((tile + 8, width), F32), pltpu.VMEM((8, width), F32)],
        flops=100 * rows * width,
        moved=18 * rows * width,
    )(*mixed_grads, branch, keep, tail)


def recurrent_backward(
    place, pieces, local_grad, after_keep, mixed_grad, branch, states, carry_in, pre, conv_low,
    dist, inputs, halo, conv_weight, decay, gate_weights,
):
    rows, width = branch.shape
    shards = pieces.shape[0]
    tile = 256
    tiles_n = rows // tile
    blocks = tile // 8

    def body(
        place_ref, pieces_ref, lg_ref, ak_ref, mg_ref, branch_ref, states_ref, before_ref, carry_ref,
        pre_ref, conv_ref, dist_ref, in_ref, in_before_ref, halo_ref, cw_ref, dp_ref, gw_ref,
        bl_ref, il_ref, pl_ref, sums_ref, end_ref, edge_ref,
        back, prev, ext, acc, cg,
    ):
        i = pl.program_id(0)
        mine = place_ref[0]

        @pl.when(i == 0)
        def _():
            entering = jnp.zeros((1, width), F32)
            for s in range(shards - 1, 0, -1):
                longer = pieces_ref[s, 0:1] * entering + pieces_ref[s, 1:2]
                entering = jnp.where(s > mine, longer, entering)
            back[...] = jnp.broadcast_to(entering, (8, width))
            sums_ref[...] = jnp.zeros_like(sums_ref)
            acc[tile : tile + 16] = jnp.zeros((16, width), F32)

        @pl.when(i > 0)
        def _():
            acc[tile : tile + 8] = acc[0:8]
            acc[tile + 8 : tile + 16] = jnp.zeros((8, width), F32)

        @pl.when(i == tiles_n - 1)
        def _():
            prev[0:8] = carry_ref[...]
            ext[0:8] = halo_ref[...]

        @pl.when(i < tiles_n - 1)
        def _():
            prev[0:8] = before_ref[...]
            ext[0:8] = in_before_ref[...]

        prev[8 : 8 + tile] = states_ref[...]
        ext[8 : 8 + tile] = in_ref[...]
        acc[0:tile] = jnp.zeros((tile, width), F32)
        dist = dist_ref[...]
        notstart = dist > 0
        for lane in range(0, width, LANES):
            cut = slice(lane, lane + LANES)
            far = slice(width + lane, width + lane + LANES)
            grad = lg_ref[:, cut] + ak_ref[:, cut] * back[0:1, cut]
            _, slope = gelu_both(branch_ref[:, cut])
            bl_ref[:, cut] = (mg_ref[:, cut].astype(F32) * states_ref[:, cut] * slope).astype(BF16)
            reset = sigmoid(pre_ref[:, cut])
            gate = sigmoid(pre_ref[:, far])
            power = -GATE_POWER * softplus_neg(dp_ref[:, cut])
            keep = jnp.exp(power * reset)
            inside = 1.0 - keep * keep + ROOT_FLOOR
            unroot = lax.rsqrt(inside)
            root = inside * unroot
            conv = conv_ref[:, cut].astype(F32)
            through = gate * conv
            keep_grad = jnp.where(notstart, grad * prev[7 : 7 + tile, cut], 0.0) - grad * through * (
                keep * unroot
            )
            kg = keep_grad * keep * reset
            pl_ref[:, cut] = (kg * power * (1.0 - reset)).astype(BF16)
            rooted = grad * root
            cg[:, cut] = rooted * gate
            pl_ref[:, far] = (rooted * through * (1.0 - gate)).astype(BF16)
            sums_ref[40:48, cut] += jnp.sum(kg.reshape(blocks, 8, LANES), axis=0)
        cg[...] += mm(pl_ref[...], gw_ref[...], NT)
        for lane in range(0, width, LANES):
            cut = slice(lane, lane + LANES)
            conv_grad = cg[:, cut]
            sums_ref[32:40, cut] += jnp.sum(conv_grad.reshape(blocks, 8, LANES), axis=0)
            for k in range(CONV):
                masked = conv_grad if k == 0 else jnp.where(dist >= k, conv_grad, 0.0)
                tap = masked * ext[8 - k : 8 - k + tile, cut]
                sums_ref[8 * k : 8 * k + 8, cut] += jnp.sum(tap.reshape(blocks, 8, LANES), axis=0)
                acc[8 - k : 8 - k + tile, cut] += cw_ref[k : k + 1, cut] * masked
        il_ref[...] = acc[8 : 8 + tile].astype(BF16)

        @pl.when(i == 0)
        def _():
            end_ref[...] = acc[tile : tile + 8]

        @pl.when(i == tiles_n - 1)
        def _():
            edge_ref[...] = acc[0:8]

    tiles = pl.BlockSpec((tile, width), lambda i, *_: (tiles_n - 1 - i, 0))
    wide = pl.BlockSpec((tile, 2 * width), lambda i, *_: (tiles_n - 1 - i, 0))
    before = pl.BlockSpec(
        (8, width), lambda i, *_: (jnp.maximum((tiles_n - 1 - i) * blocks - 1, 0), 0)
    )
    small = whole((8, width))
    return call(
        body,
        (tiles_n,),
        [
            whole(pieces.shape), tiles, tiles, tiles, tiles, tiles, before, small, wide, tiles,
            pl.BlockSpec((tile, 1), lambda i, *_: (tiles_n - 1 - i, 0)),
            tiles, before, small, whole((CONV, width)), whole((1, width)), whole((width, 2 * width)),
        ],
        [tiles, tiles, wide, whole((48, width)), small, small],
        [
            struct((rows, width), BF16),
            struct((rows, width), BF16),
            struct((rows, 2 * width), BF16),
            struct((48, width), F32),
            struct((8, width), F32),
            struct((8, width), F32),
        ],
        [
            pltpu.VMEM((8, width), F32),
            pltpu.VMEM((tile + 8, width), F32),
            pltpu.VMEM((tile + 8, width), F32),
            pltpu.VMEM((tile + 16, width), F32),
            pltpu.VMEM((tile, width), F32),
        ],
        prefetch=1,
        flops=4 * rows * width * width + 300 * rows * width,
        moved=40 * rows * width,
    )(
        place, pieces, local_grad, after_keep, mixed_grad, branch, states, states, carry_in, pre,
        conv_low, dist, inputs, inputs, halo, conv_weight, decay, gate_weights,
    )


def input_backward(place, branch_low, inputs_low, end, returned, weights, stream, gain, resid_grads):
    rows, width = branch_low.shape
    model = stream.shape[1]
    sub = resid_grads[0].shape[0]
    tile = sub * CHUNKS
    steps = rows // tile

    def body(
        place_ref, bl_ref, il_ref, end_ref, ret_ref, w_ref, x_ref, gain_ref, *rest
    ):
        part_ref, fixed_ref, sum_ref = rest[CHUNKS:]
        i = pl.program_id(0)
        fixed_ref[...] = il_ref[...]

        @pl.when(i == steps - 1)
        def _():
            tail = jnp.concatenate(
                [il_ref[tile - 16 : tile - 8].astype(F32), end_ref[...] + ret_ref[...]], axis=0
            )
            fixed_ref[tile - 16 : tile] = tail.astype(BF16)

        g = mm(bl_ref[...], w_ref[:, :width], NT) + mm(fixed_ref[...], w_ref[:, width:], NT)
        x = x_ref[...].astype(F32)
        inv = lax.rsqrt(jnp.mean(x * x, axis=-1, keepdims=True) + EPSILON)
        unit = x * inv
        scaled = g * gain_ref[...]
        dot = jnp.mean(scaled * unit, axis=-1, keepdims=True)
        part = inv * (scaled - unit * dot)
        sums = jnp.sum(g * unit, axis=0, keepdims=True)

        @pl.when(i == 0)
        def _():
            sum_ref[...] = sums

        @pl.when(i > 0)
        def _():
            sum_ref[...] += sums

        @pl.when(i == place_ref[1])
        def _():
            for c in range(CHUNKS):
                cut = slice(c * sub, (c + 1) * sub)
                part_ref[cut] = (part[cut] + rest[c][...]).astype(BF16)

        @pl.when(i != place_ref[1])
        def _():
            part_ref[...] = part.astype(BF16)

    tiles = pl.BlockSpec((tile, width), lambda i, *_: (i, 0))
    wide = pl.BlockSpec((tile, model), lambda i, *_: (i, 0))
    return call(
        body,
        (steps,),
        [
            tiles, tiles, whole((8, width)), whole((8, width)), whole((model, 2 * width)), wide,
            whole((1, model)),
        ]
        + [whole((sub, model))] * CHUNKS,
        [wide, tiles, whole((1, model))],
        [struct((rows, model), BF16), struct((rows, width), BF16), struct((1, model), F32)],
        prefetch=1,
        flops=4 * rows * width * model + 30 * rows * model,
        moved=4 * rows * model + 4 * width * model + 6 * rows * width,
    )(place, branch_low, inputs_low, end, returned, weights, stream, gain, *resid_grads)


def block_diagonal(blocks, width):
    heads, size = blocks.shape[0], blocks.shape[1]
    rows = [
        jnp.pad(blocks[h], ((0, 0), (h * size, width - (h + 1) * size))) for h in range(heads)
    ]
    return jnp.pad(jnp.concatenate(rows, axis=0), ((0, width - heads * size), (0, 0)))


def diagonal_blocks(full, heads, size):
    return jnp.stack([full[h * size : (h + 1) * size, h * size : (h + 1) * size] for h in range(heads)])


def shards(
    tokens,
    cotangent,
    destination,
    lengths,
    norm_gain,
    w_branch,
    w_input,
    conv_weight,
    conv_bias,
    w_recur,
    w_ingate,
    decay_param,
    w_out,
    mlp_gain,
    w_gate,
    w_up,
    w_down,
):
    shard_count = lax.axis_size("seq")
    my_shard = lax.axis_index("seq")
    model_count = lax.axis_size("mp")
    my_model = lax.axis_index("mp")
    row_count, model_width = tokens.shape
    slab_width = model_width // model_count
    per_peer = row_count // shard_count
    own_rows = row_count // model_count
    sub = own_rows // CHUNKS
    channels = w_branch.shape[1]
    heads, block_width = w_recur.shape[0], w_recur.shape[1]
    width = -(-channels // LANES) * LANES
    parity = my_shard % 2
    place = jnp.stack([my_shard, my_model, parity]).astype(jnp.int32)
    pad_lanes = functools.partial(jnp.pad, pad_width=((0, 0), (0, width - channels)))

    bits = shard_count.bit_length() - 1

    def scatter_sum(x, axis, dim):
        return lax.psum_scatter(x, axis, scatter_dimension=dim, tiled=True)

    def exchange(x, axis):
        return lax.all_to_all(x, axis, split_axis=0, concat_axis=0, tiled=True)

    def swap(x, bit):
        return lax.ppermute(x, "seq", [(i, i ^ (1 << bit)) for i in range(shard_count)])

    def add_low(left, right):
        return (left.astype(F32) + right.astype(F32)).astype(BF16)

    def tie(*values):
        return lax.optimization_barrier(values)

    def tie_with(value, ring, running):
        value, ring, arrays = tie(value, ring, [x for x, _ in running])
        return value, ring, [(x, up) for x, (_, up) in zip(arrays, running)]

    def halve_once(x, up, bits):
        done = bits - x.shape[0].bit_length() + 1
        bit = done if up else bits - done
        mine = (my_shard >> bit) & 1
        axis = 1 if up else 0
        x = x.reshape(-1, 2, *x.shape[1:]) if up else x.reshape(2, -1, *x.shape[1:])
        other = lax.dynamic_index_in_dim(x, 1 - mine, axis, False)
        return add_low(lax.dynamic_index_in_dim(x, mine, axis, False), swap(other, bit))

    def ring_start(x):
        return ((x, x), (x,), ())

    def ring_step(ring):
        (right, left), rights, lefts = ring
        right = lax.ppermute(right, "mp", [(i, i + 1) for i in range(model_count - 1)])
        left = lax.ppermute(left, "mp", [(i + 1, i) for i in range(model_count - 1)])
        return ((right, left), rights + (right,), lefts + (left,))

    def ring_end(ring):
        _, rights, lefts = ring
        return [rights[0]] + [
            jnp.where(my_model >= k, rights[k], lefts[model_count - k - 1])
            for k in range(1, model_count)
        ]

    local_dest = lax.dynamic_slice_in_dim(destination, my_shard * row_count, row_count)
    dest_row, dest_col = local_dest.reshape(1, -1), local_dest.reshape(-1, 1)
    straight = jnp.zeros((1,), jnp.int32)
    turn = (my_shard * per_peer).astype(jnp.int32)[None]
    arrived_tokens = exchange(send_order(straight, dest_row, dest_col, tokens), "seq")
    sent_cot = send_order(turn, dest_row, dest_col, cotangent)
    sorted_dest = jnp.sort(destination.reshape(shard_count, row_count), axis=1)
    landing = (
        lax.dynamic_slice_in_dim(sorted_dest, my_shard * per_peer, per_peer, 1).reshape(-1)
        - my_shard * row_count
    )
    landing_row = landing.reshape(1, -1)
    turned = jnp.stack(
        [
            lax.dynamic_index_in_dim(landing.reshape(shard_count, per_peer), my_shard ^ k, 0, False)
            for k in range(shard_count)
        ]
    ).reshape(1, -1)
    mlp_place = np.arange(row_count, dtype=np.int32).reshape(model_count, CHUNKS, sub)
    mlp_place = jnp.asarray(mlp_place.transpose(1, 0, 2).reshape(-1, 1))
    mlp_landing = (
        (landing % own_rows) // sub * (model_count * sub) + landing // own_rows * sub + landing % sub
    )

    positions = my_shard * row_count + jnp.arange(row_count, dtype=jnp.int32)
    count = lengths.shape[0]
    earlier = np.tril(np.ones((count, count), np.int32), -1)
    seq_starts = jnp.sum(jnp.asarray(earlier) * lengths[None, :], axis=1)
    seq_start = jnp.max(
        jnp.where(seq_starts[None, :] <= positions[:, None], seq_starts[None, :], 0), axis=1
    )
    dist = (positions - seq_start).reshape(-1, 1)

    w_rec = jnp.concatenate([pad_lanes(w_branch), pad_lanes(w_input)], axis=1)
    w_gates = jnp.concatenate(
        [block_diagonal(w_recur, width), block_diagonal(w_ingate, width)], axis=1
    )
    taps = pad_lanes(conv_weight)
    bias = pad_lanes(conv_bias[None])
    decay = pad_lanes(decay_param[None])
    gain = norm_gain[None]
    gain2 = mlp_gain[None]
    half = model_width // 2
    w_out_half = jnp.pad(
        lax.dynamic_slice_in_dim(w_out, parity * half, half, 1), ((0, width - channels), (0, 0))
    )
    w_near = lax.all_gather(w_out_half, "mp", axis=0)

    arrived_tokens, sent_cot, w_rec, w_gates = lax.optimization_barrier(
        (arrived_tokens, sent_cot, w_rec, w_gates)
    )
    stream, hidden_near, hidden_far, branch, inputs = project(
        place, landing_row, arrived_tokens, gain, w_rec, shard_count
    )
    halo = lax.ppermute(
        inputs[row_count - 8 :], "seq", [(i, i + 1) for i in range(shard_count - 1)]
    )
    conv_low, pre, keep, prefix, local, tail = recurrent_forward(
        inputs, halo, dist, taps, bias, decay, w_gates
    )
    pieces = lax.all_gather(tail, "seq")
    pieces, sent_cot, w_near = tie(pieces, sent_cot, w_near)
    cot_blocks = [sent_cot[:per_peer]]
    for k in range(1, shard_count):
        block = sent_cot[k * per_peer : (k + 1) * per_peer]
        cot_blocks.append(
            lax.ppermute(block, "seq", [(i, i ^ k) for i in range(shard_count)])
        )
    w_far = swap(w_near, 0)
    states, mixed, carry_in = finish_states(place, pieces, local, prefix, branch, model_count)

    resids, normeds = [], []
    upstream, upstream_near, upstream_far = place_upstream(
        place, mlp_place, turned, cot_blocks, shard_count
    )
    for c in range(CHUNKS):
        mixed_full = exchange(mixed[c], "mp")
        if c == CHUNKS - 1:
            mixed_full, upstream = tie(mixed_full, upstream)
        resid_own, normed_own = output_rows(c, place, mixed_full, w_near, w_far, stream, gain2)
        resids.append(resid_own)
        normeds.append(normed_own)
    kept, grads = (), []
    for c in range(CHUNKS):
        normed = lax.all_gather(normeds[c], "mp", axis=0, tiled=True)
        *kept, grad = mlp_chunk(
            c, place, normed, upstream, resids[c], w_gate, w_up, w_down, shard_count, kept
        )
        grads.append(scatter_sum(grad, "mp", 0))
    inner_act, gate_low, up_low, normed_near, normed_far, block_part = kept

    parts = shard_count // 2
    part_width = model_width // shard_count
    hidden_units = w_gate.shape[1]

    def outer(left, right):
        return mm(left, right, TN).astype(BF16)

    def with_partner(near, sent, right):
        return (mm(near, right, TN) + sent.astype(F32)).astype(BF16).reshape(
            parts, part_width, right.shape[1]
        )

    far_gate = outer(normed_far, gate_low)
    far_up = outer(normed_far, up_low)
    far_down = outer(upstream_far, inner_act)
    grads[0], far_gate, far_up, far_down = tie(grads[0], far_gate, far_up, far_down)
    far_gate, far_up, far_down = swap(far_gate, 0), swap(far_up, 0), swap(far_down, 0)
    resid_grads, resid_lows, mixed_grads, mlp_gain_part = [], [], [], 0.0
    for c in range(CHUNKS):
        resid_grad, resid_low, mixed_grad_full, gain_part = resid_backward(
            c, place, grads[c], upstream, resids[c], gain2, w_near, w_far
        )
        if c == 0:
            mixed_grad_full, gate_low, up_low, inner_act = tie(
                mixed_grad_full, gate_low, up_low, inner_act
            )
            grad_gate = with_partner(normed_near, far_gate, gate_low)
            grad_up = with_partner(normed_near, far_up, up_low)
            grad_down = with_partner(upstream_near, far_down, inner_act)
            grads[1], grad_gate, grad_up, grad_down = tie(grads[1], grad_gate, grad_up, grad_down)
        mlp_gain_part = mlp_gain_part + gain_part
        resid_grads.append(resid_grad)
        resid_lows.append(resid_low)
        mixed_grads.append(exchange(mixed_grad_full, "mp"))
    halves = (grad_down[..., : hidden_units // 2], grad_down[..., hidden_units // 2 :])
    running = [
        (grad_gate, True),
        (grad_up, False),
        (halves[0], True),
        (halves[1], False),
    ]

    def step(entries):
        return [(halve_once(x, up, bits), up) for x, up in entries]

    mixed_grads[-1], *resid_lows = tie(mixed_grads[-1], *resid_lows)
    ring = ring_start(jnp.stack(resid_lows))
    block_share = scatter_sum(block_part, "mp", 1)
    local_grad, after_keep, edge_pair, mixed_grad = recurrent_back_scan(
        mixed_grads, branch, keep, tail
    )
    back_pieces = lax.all_gather(edge_pair, "seq")
    branch_low, inputs_part, pre_low, sums, end, edge = recurrent_backward(
        place, back_pieces, local_grad, after_keep, mixed_grad, branch, states, carry_in, pre,
        conv_low, dist, inputs, halo, taps, decay, w_gates,
    )
    returned = lax.ppermute(edge, "seq", [(i + 1, i) for i in range(shard_count - 1)])
    running = step(running)
    ring = ring_step(ring)
    returned, ring, running = tie_with(returned, ring, running)
    returned, block_share = tie(returned, block_share)
    input_part, inputs_low, norm_gain_part = input_backward(
        place, branch_low, inputs_part, end, returned, w_rec, stream, gain, resid_grads
    )
    ring = ring_step(ring)
    input_part, ring, running = tie_with(input_part, ring, running)
    for _ in range(bits - 2):
        running = step(running)
    for _ in range(model_count - 3):
        ring = ring_step(ring)
    input_share = scatter_sum(input_part, "mp", 1)
    sent_gate, sent_up, *sent_down = [x[0] for x, _ in running]
    sent_gate, sent_up = sent_gate.astype(F32), sent_up.astype(F32)
    sent_down = jnp.concatenate(sent_down, axis=-1).astype(F32).T

    gathered = ring_end(ring)
    mixed_near = [
        lax.dynamic_index_in_dim(mixed, (my_model - k) % model_count, 1, False)
        for k in range(model_count)
    ]
    grad_out = mm(
        jnp.stack(mixed_near).reshape(row_count, width),
        jnp.stack(gathered).reshape(row_count, model_width),
        TN,
    ).astype(BF16)
    sent_out = scatter_sum(grad_out, "seq", 1)
    grad_gates = mm(conv_low, pre_low, TN)
    rec_low = jnp.concatenate([branch_low, inputs_low], axis=1)
    grad_rec = with_partner(hidden_near, swap(outer(hidden_far, rec_low), 0), rec_low)
    running = [(grad_rec[..., :width], True), (grad_rec[..., width:], False)]
    for _ in range(bits - 1):
        running = step(running)
    sent_branch, sent_input = [x[0] for x, _ in running]
    sent_branch = sent_branch[:, :channels].astype(F32)
    sent_input = sent_input[:, :channels].astype(F32)
    all_rows = jnp.arange(row_count, dtype=jnp.int32)[None]
    home_block = exchange(place_rows(mlp_landing.reshape(-1, 1), all_rows, block_share), "seq")
    input_share, sent_branch, sent_input, home_block, sent_gate, sent_up, sent_down = tie(
        input_share, sent_branch, sent_input, home_block, sent_gate, sent_up, sent_down
    )

    sums = jnp.sum(sums.reshape(CONV + 2, 8, width), axis=1)[:, :channels]
    sums = jnp.concatenate(
        [sums[: CONV + 1], sums[CONV + 1 :] * (GATE_POWER * jax.nn.sigmoid(-decay_param))], axis=0
    )
    gains = jnp.concatenate([norm_gain_part, mlp_gain_part], axis=0)
    gains = gains.reshape(2, model_count, slab_width).transpose(1, 0, 2)
    gains = jnp.sum(exchange(gains, "mp"), axis=0)
    sum_rows = sums.size // block_width
    gain_rows = -(-gains.size // block_width)
    gains = jnp.pad(gains.reshape(-1), (0, gain_rows * block_width - gains.size))
    extra = jnp.concatenate(
        [sums.reshape(sum_rows, block_width), gains.reshape(gain_rows, block_width)], axis=0
    )
    extra = jnp.pad(extra, ((0, block_width - sum_rows - gain_rows), (0, 0)))
    small = jnp.concatenate(
        [
            diagonal_blocks(grad_gates[:, :width], heads, block_width),
            diagonal_blocks(grad_gates[:, width:], heads, block_width),
            extra[None],
        ],
        axis=0,
    )
    small = lax.psum(small, "seq")
    input_share, small, sent_out = tie(input_share, small, sent_out)
    sent_out = sent_out[:channels].astype(F32)
    sums = small[2 * heads, :sum_rows].reshape(CONV + 2, channels)
    gains = small[2 * heads, sum_rows : sum_rows + gain_rows].reshape(-1)
    gains = gains[: 2 * slab_width].reshape(2, slab_width)

    home_input = exchange(place_rows(landing.reshape(-1, 1), all_rows, input_share), "seq")
    block_out = restore_rows(dest_row, dest_col, home_block)
    input_grad = restore_rows(dest_row, dest_col, home_input)
    return (
        block_out,
        input_grad,
        gains[0],
        sent_branch,
        sent_input,
        sums[:CONV],
        sums[CONV],
        small[:heads],
        small[heads : 2 * heads],
        sums[CONV + 1],
        sent_out,
        gains[1],
        sent_gate,
        sent_up,
        sent_down,
    )


def solution(mesh):
    in_specs = (
        P("seq", None),
        P("seq", None),
        P(),
        P(),
        P(),
        P(None, "mp"),
        P(None, "mp"),
        P(None, "mp"),
        P("mp"),
        P("mp", None, None),
        P("mp", None, None),
        P("mp"),
        P("mp", None),
        P(),
        P(None, "mp"),
        P(None, "mp"),
        P("mp", None),
    )
    out_specs = (
        P("seq", "mp"),
        P("seq", "mp"),
        P("mp"),
        P("seq", "mp"),
        P("seq", "mp"),
        P(None, "mp"),
        P("mp"),
        P("mp", None, None),
        P("mp", None, None),
        P("mp"),
        P("mp", "seq"),
        P("mp"),
        P("seq", "mp"),
        P("seq", "mp"),
        P("mp", "seq"),
    )
    return jax.shard_map(shards, mesh=mesh, in_specs=in_specs, out_specs=out_specs, check_vma=False)
```

time: 2760 us -> 784 us (0.28)
  waiting for transfers between devices: 1150 us -> 223 us
  local copies, waits for them, and re-layouts: 931 us -> 71.1 us
  other arithmetic: 310 us -> 39.9 us
  Pallas kernels: 0 us -> 240 us
  matrix products: 201 us -> 61.7 us
  blocking collectives: 109 us -> 46.3 us
  starting transfers between devices: 20.4 us -> 70.4 us
    psum x4 -> x1, waiting for transfers between devices: 681 us -> 0.02 us  [shards(): small = lax.psum(small, 'seq')]
    slice x120 -> x12, local copies, waits for them, and re-layouts: 452 us -> 12.8 us  [the longest x1 3.82 us: shards(): block = sent_cot[k * per_peer:(k + 1) * per_peer]]
    reduce_scatter x7 -> x5, waiting for transfers between devices: 434 us -> 6.59 us  [scatter_sum(): return lax.psum_scatter(x, axis, scatter_dimension=dim, tiled=True)]
    pallas_call x0 -> x19, Pallas kernels: none -> 240 us  [the longest x2 66.2 us: mlp_chunk(): call(body, (steps,), [whole((rows, model)), pl.BlockSpec((rows, model), l...]
    pad x40 -> x5, local copies, waits for them, and re-layouts: 143 us -> 3.08 us  [the longest x1 1.29 us: shards(): jnp.pad(lax.dynamic_slice_in_dim(w_out, parity * half, half, 1), ((0, wid...]
    dot_general x24 -> x10, matrix products: 201 us -> 61.7 us  [mm(): return lax.dot_general(left, right, dims, preferred_element_type=F32)]
    ppermute x2 -> x32, waiting for transfers between devices: 0.44 us -> 119 us  [the longest x17 41.4 us: swap(): lax.ppermute(x, 'seq', [(i, i ^ 1 << bit) for i in range(shard_count)])]
    add x44 -> x2, other arithmetic: 111 us -> 1.74 us  [the longest x1 1.73 us: shards(): landing % own_rows // sub * (model_count * sub) + landing // own_rows * sub]
  transfers between devices with their start and end apart: 16 -> 48, of which waited for: 12 -> 19; matrix products, arithmetic and copies ran while one was open for 30% -> 21% of each run, Pallas kernels for 0% -> 29%
where the time goes in v1:
time: 784 us; the launch traced here: 770 us
  Pallas kernels  240 us (31%)
  waiting for transfers between devices  223 us (28%)
  local copies, waits for them, and re-layouts  71.1 us (9%)
  starting transfers between devices  70.4 us (9%)
  matrix products  61.7 us (8%)
  blocking collectives  46.3 us (6%)
  other arithmetic  39.9 us (5%)
  between operations  17.1 us (2%)
    all_to_all x7, waiting for transfers between devices, exchange(): return lax.all_to_all(x, axis, split_axis=0, concat_axis=0, tiled=True)  78.7 us
    pallas_call x2, Pallas kernels, mlp_chunk(): call(body, (steps,), [whole((rows, model)), pl.BlockSpec((rows, model), l...  66.2 us
    dot_general x10, matrix products, mm(): return lax.dot_general(left, right, dims, preferred_element_type=F32)  61.7 us
    ppermute x17, waiting for transfers between devices, swap(): lax.ppermute(x, 'seq', [(i, i ^ 1 << bit) for i in range(shard_count)])  41.4 us
    ppermute x7, waiting for transfers between devices, shards(): lax.ppermute(block, 'seq', [(i, i ^ k) for i in range(shard_count)])  41.3 us
    ppermute x3, waiting for transfers between devices, ring_step(): lax.ppermute(right, 'mp', [(i, i + 1) for i in range(model_count - 1)])  30.4 us
    all_to_all x7, starting transfers between devices, exchange(): return lax.all_to_all(x, axis, split_axis=0, concat_axis=0, tiled=True)  28.4 us
    all_to_all x1, blocking collectives, exchange(): return lax.all_to_all(x, axis, split_axis=0, concat_axis=0, tiled=True)  24.1 us
  transfers between devices with their start and end apart: 48, of which 19 were waited for; matrix products, arithmetic and copies ran while one was open for 21% of the time, Pallas kernels for 29%

profile of v1, /device:TPU:0, one launch (start us, length us, event | category | flops | bytes accessed | tf_op | source)
XLA Modules:
  0.0 769.7 jit_solution(16872784646429037914)
XLA Ops:
  13.0 8.9 %shard_map.298 = bf16[1024,2048]{1,0:T(8,128)(2,1)} custom-call(s32[1]{0:T(128)} %constant.203.clone.1.turn_ref, s32[1,1024]{1,0:T(1,128)} %bitcast.217, s32[1024,1]{1,0:T(8,128)} %copy.134.col_ref, bf16[1024,2048]{1,0:T(8,128)(2,1)} %val_ref.2), custom_call_target="tpu_custom_call" | custom-call | flops 4294967296 | bytes 8388608 | tf_op jit(solution)/shard_map/pallas_call | solution.py:101
  21.9 5.4 all-to-all-start
  27.4 2.9 copy.118
  30.3 4.6 copy.117
  39.1 8.9 %shard_map.299 = bf16[1024,2048]{1,0:T(8,128)(2,1)} custom-call(s32[1]{0:T(128)} %bitcast.8.turn_ref, s32[1,1024]{1,0:T(1,128)} %bitcast.218, s32[1024,1]{1,0:T(8,128)} %copy.134.col_ref, bf16[1024,2048]{1,0:T(8,128)(2,1)} %val_ref.3), custom_call_target="tpu_custom_call" | custom-call | flops 4294967296 | bytes 8388608 | tf_op jit(solution)/shard_map/pallas_call | solution.py:101
  48.1 6.5 fusion.2.w_ref
  55.8 20.8 %all-to-all-done = bf16[8,128,2048]{2,1,0:T(8,128)(2,1)} async-done(((bf16[8,128,2048]{2,1,0:T(8,128)(2,1)}), bf16[8,128,2048]{2,1,0:T(8,128)(2,1)}, u32[]{:S(2)}, u32[]{:S(2)}) %all-to-all-start) | async-done | bytes 4194336 | tf_op jit(solution)/shard_map/all_to_all | solution.py:888
  76.6 18.4 %shard_map.300 = (bf16[1024,2048]{1,0:T(8,128)(2,1)}, bf16[1024,1024]{1,0:T(8,128)(2,1)}, bf16[1024,1024]{1,0:T(8,128)(2,1)}, f32[1024,768]{1,0:T(8,128)}, f32[1024,768]{1,0:T(8,128)}) custom-call(s32[3]{0:T(128)} %pad_add_fusion.my_ref.place_ref, s32[1,1024]{1,0:T(1,128)} %bitcast.214, bf16[1024,2048]{1,0:T(8,128)(2,1)} %bitcast.7.arr_ref, ...), custom_call_target="tpu_custom_call" | custom-call | flops 10737418240 | bytes 25165824 | tf_op jit(solution)/shard_map/pallas_call | solution.py:228
  100.3 13.3 %shard_map.301 = (bf16[1024,768]{1,0:T(8,128)(2,1)}, f32[1024,1536]{1,0:T(8,128)}, f32[1024,768]{1,0:T(8,128)}, f32[1024,768]{1,0:T(8,128)}, f32[1024,768]{1,0:T(8,128)}, /*index=5*/f32[8,768]{1,0:T(8,128)}) custom-call(f32[1024,768]{1,0:T(8,128)} %get-tuple-element.131.in_ref.in_before_ref, f32[8,768]{1,0:T(8,128)} %copy-done.28, ...), custom_call_target="tpu_custom_call" | custom-call | flops 2573205504 | bytes 23592960 | tf_op jit(solution)/shard_map/pallas_call | solution.py:328
  113.6 11.5 %all-gather = f32[64,768]{1,0:T(8,128)} all-gather(f32[8,768]{1,0:T(8,128)} %get-tuple-element.133.refs_4_), channel_id=2, replica_groups=mesh['seq'=8,'mp'=4] {'seq'}, dimensions={0}, use_global_device_ids=true | all-gather | bytes 221184 | tf_op jit(solution)/shard_map/all_gather | solution.py:988
  125.1 5.2 all-gather.11.cloned.1.call-done
  130.3 8.6 %shard_map.302 = (f32[1024,768]{1,0:T(8,128)}, bf16[2,4,128,768]{3,2,1,0:T(8,128)(2,1)}, f32[8,768]{1,0:T(8,128)}) custom-call(s32[3]{0:T(128)} %pad_add_fusion.my_ref.place_ref, f32[8,8,768]{2,1,0:T(8,128)} %bitcast.206, f32[1024,768]{1,0:T(8,128)} %get-tuple-element.136.local_ref, f32[1024,768]{1,0:T(8,128)} %get-tuple-element.137.prefix_ref, ...), custom_call_target="tpu_custom_call" | custom-call | flops 47185920 | bytes 14155776 | tf_op jit(solution)/shard_map/pallas_call | solution.py:383
  141.3 24.1 %all_to_all.60.mixed_ref = bf16[4,128,768]{2,1,0:T(8,128)(2,1)} all-to-all(bf16[4,128,768]{2,1,0:T(8,128)(2,1)S(1)} %get-tuple-element.326), channel_id=1, replica_groups=mesh['seq'=8,'mp'=4] {'mp'}, dimensions={0} | all-to-all | bytes 1572864 | tf_op jit(solution)/shard_map/all_to_all | solution.py:888
  165.4 9.0 %shard_map.303 = (f32[128,2048]{1,0:T(8,128)}, bf16[128,2048]{1,0:T(8,128)(2,1)}) custom-call(s32[3]{0:T(128)} %pad_add_fusion.my_ref.place_ref, bf16[4,128,768]{2,1,0:T(8,128)(2,1)} %all_to_all.60.mixed_ref, bf16[4,768,1024]{2,1,0:T(8,128)(2,1)} %bitcast.184, bf16[4,768,1024]{2,1,0:T(8,128)(2,1)} %collective-permute-done.1.far_ref, ...), custom_call_target="tpu_custom_call" | custom-call | flops 1610612736 | bytes 14680064 | tf_op jit(solution)/shard_map/pallas_call | solution.py:426
  174.5 3.8 fusion.74
  179.8 3.5 all-to-all-start.2
  187.8 5.5 collective-permute-done.3.refs_2_
  195.3 8.5 %collective-permute-done.4.refs_3_ = bf16[128,2048]{1,0:T(8,128)(2,1)} collective-permute-done((bf16[128,2048]{1,0:T(8,128)(2,1)}, bf16[128,2048]{1,0:T(8,128)(2,1)}, u32[]{:S(2)}, u32[]{:S(2)}) %collective-permute-start.4) | collective-permute-done | bytes 524320 | tf_op jit(solution)/shard_map/ppermute | solution.py:994
  203.8 27.3 %collective-permute-done.6.refs_5_ = bf16[128,2048]{1,0:T(8,128)(2,1)} collective-permute-done((bf16[128,2048]{1,0:T(8,128)(2,1)S(1)}, bf16[128,2048]{1,0:T(8,128)(2,1)}, u32[]{:S(2)}, u32[]{:S(2)}) %collective-permute-start.6) | collective-permute-done | bytes 524320 | tf_op jit(solution)/shard_map/ppermute | solution.py:994
  231.1 10.5 %shard_map.304 = (bf16[1024,2048]{1,0:T(8,128)(2,1)}, bf16[1024,1024]{1,0:T(8,128)(2,1)}, bf16[1024,1024]{1,0:T(8,128)(2,1)}) custom-call(s32[3]{0:T(128)} %pad_add_fusion.my_ref.place_ref, s32[1024,1]{1,0:T(8,128)} %constant.223.clone.place_ref, s32[1,1024]{1,0:T(1,128)} %bitcast.224, bf16[128,2048]{1,0:T(8,128)(2,1)} %get-tuple-element.310.refs_0_, ...), custom_call_target="tpu_custom_call" | custom-call | flops 4294967296 | bytes 12582912 | tf_op jit(solution)/shard_map/pallas_call | solution.py:166
  242.5 8.9 %shard_map.306 = (f32[128,2048]{1,0:T(8,128)}, bf16[128,2048]{1,0:T(8,128)(2,1)}) custom-call(s32[3]{0:T(128)} %pad_add_fusion.my_ref.place_ref, bf16[4,128,768]{2,1,0:T(8,128)(2,1)} %copy-done.6, bf16[4,768,1024]{2,1,0:T(8,128)(2,1)} %bitcast.185, bf16[4,768,1024]{2,1,0:T(8,128)(2,1)} %collective-permute-done.1.far_ref, ...), custom_call_target="tpu_custom_call" | custom-call | flops 1610612736 | bytes 14680064 | tf_op jit(solution)/shard_map/pallas_call | solution.py:426
  251.6 33.1 %shard_map.305 = (bf16[1024,1536]{1,0:T(8,128)(2,1)}, bf16[1024,1536]{1,0:T(8,128)(2,1)}, bf16[1024,1536]{1,0:T(8,128)(2,1)}, bf16[1024,1024]{1,0:T(8,128)(2,1)}...) custom-call(s32[3]{0:T(128)} %pad_add_fusion.my_ref.place_ref, ...), custom_call_target="tpu_custom_call" | custom-call | flops 19327352832 | bytes 29360128 | tf_op jit(solution)/shard_map/pallas_call | solution.py:492
  285.0 13.8 %all-gather.9.cloned.1.call-done.n_ref = bf16[512,2048]{1,0:T(8,128)(2,1)} async-done(((bf16[128,2048]{1,0:T(8,128)(2,1)}), bf16[512,2048]{1,0:T(8,128)(2,1)}) %all-gather.9.cloned.1.call-update) | async-done | bytes 2097168 | tf_op jit(solution)/shard_map/all_gather | solution.py:1012
  298.8 33.1 %shard_map.307 = (bf16[1024,1536]{1,0:T(8,128)(2,1)}, bf16[1024,1536]{1,0:T(8,128)(2,1)}, bf16[1024,1536]{1,0:T(8,128)(2,1)}, bf16[1024,1024]{1,0:T(8,128)(2,1)}...) custom-call(s32[3]{0:T(128)} %pad_add_fusion.my_ref.place_ref, ...), custom_call_target="tpu_custom_call", output_to_operand_aliasing={{0}: (7, {}), {1}: (8, {}), {2}: (9, {}), {3}: (10, {}), {4... | custom-call | flops 19327352832 | bytes 29360128 | tf_op jit(solution)/shard_map/pallas_call | solution.py:492
  331.9 7.9 %convolution_convert_fusion.3 = bf16[1024,1536]{1,0:T(8,128)(2,1)} fusion(bf16[1024,1024]{1,0:T(8,128)(2,1)} %get-tuple-element.157, bf16[1024,1536]{1,0:T(8,128)(2,1)} %get-tuple-element.167), kind=kOutput, calls=%fused_computation.25 | convolution fusion | flops 3222798336 | bytes 8388608 | tf_op jit(solution)/shard_map/dot_general | solution.py:30
  339.8 5.4 convolution_convert_fusion.2
  345.2 5.1 convolution_convert_fusion.1
  350.9 10.5 %shard_map.308 = (f32[128,2048]{1,0:T(8,128)}, bf16[128,2048]{1,0:T(8,128)(2,1)}, bf16[4,128,768]{2,1,0:T(8,128)(2,1)}, f32[1,2048]{1,0:T(1,128)}) custom-call(s32[3]{0:T(128)} %pad_add_fusion.my_ref.place_ref, bf16[128,2048]{1,0:T(8,128)(2,1)} %reduce-scatter.6.cloned.1.call-done.g_ref, bf16[1024,2048]{1,0:T(8,128)(2,1)} %get-tuple-element.145.u_ref.up_ref, ...), custom_call_target="tpu_custom_call" | custom-call | flops 1610612736 | bytes 16252928 | tf_op jit(solution)/shard_map/pallas_call | solution.py:553
  361.4 7.4 add_convert_fusion.3
  368.9 6.6 add_convert_fusion.2
  375.5 6.5 add_convert_fusion.1
  382.0 6.5 reduce-scatter.8.cloned.1.call-done.g_ref
  388.5 11.3 %shard_map.309 = (f32[128,2048]{1,0:T(8,128)}, bf16[128,2048]{1,0:T(8,128)(2,1)}, bf16[4,128,768]{2,1,0:T(8,128)(2,1)}, f32[1,2048]{1,0:T(1,128)}) custom-call(s32[3]{0:T(128)} %pad_add_fusion.my_ref.place_ref, bf16[128,2048]{1,0:T(8,128)(2,1)} %reduce-scatter.8.cloned.1.call-done.g_ref, bf16[1024,2048]{1,0:T(8,128)(2,1)} %get-tuple-element.145.u_ref.up_ref, ...), custom_call_target="tpu_custom_call" | custom-call | flops 1610612736 | bytes 16252928 | tf_op jit(solution)/shard_map/pallas_call | solution.py:553
  399.8 3.5 all-to-all-start.4
  411.8 33.3 %all-to-all-done.4.refs_1_ = bf16[4,128,768]{2,1,0:T(8,128)(2,1)S(1)} async-done(((bf16[4,128,768]{2,1,0:T(8,128)(2,1)}), bf16[4,128,768]{2,1,0:T(8,128)(2,1)S(1)}, u32[]{:S(2)}, u32[]{:S(2)}) %all-to-all-start.4) | async-done | bytes 786464 | tf_op jit(solution)/shard_map/all_to_all | solution.py:888
  445.1 4.2 all-to-all-start.3
  449.3 2.8 dynamic-slice_bitcast_fusion
  458.3 4.8 collective-permute-start.13
  464.4 24.0 %all-to-all-done.3.refs_0_ = bf16[4,128,768]{2,1,0:T(8,128)(2,1)} async-done(((bf16[4,128,768]{2,1,0:T(8,128)(2,1)}), bf16[4,128,768]{2,1,0:T(8,128)(2,1)}, u32[]{:S(2)}, u32[]{:S(2)}) %all-to-all-start.3) | async-done | bytes 786464 | tf_op jit(solution)/shard_map/all_to_all | solution.py:888
  488.4 9.2 %shard_map.310 = (f32[1024,768]{1,0:T(8,128)}, f32[1024,768]{1,0:T(8,128)}, f32[8,768]{1,0:T(8,128)}, bf16[1024,768]{1,0:T(8,128)(2,1)}) custom-call(bf16[4,128,768]{2,1,0:T(8,128)(2,1)} %all-to-all-done.3.refs_0_, bf16[4,128,768]{2,1,0:T(8,128)(2,1)} %copy-done.7, f32[1024,768]{1,0:T(8,128)} %get-tuple-element.138.branch_ref.refs_2_, ...), custom_call_target="tpu_custom_call" | custom-call | flops 78643200 | bytes 14155776 | tf_op jit(solution)/shard_map/pallas_call | solution.py:619
  497.6 10.8 %all-gather.2 = f32[64,768]{1,0:T(8,128)} all-gather(f32[8,768]{1,0:T(8,128)} %get-tuple-element.180), channel_id=4, replica_groups=mesh['seq'=8,'mp'=4] {'seq'}, dimensions={0}, use_global_device_ids=true | all-gather | bytes 221184 | tf_op jit(solution)/shard_map/all_gather | solution.py:1070
  508.4 20.0 %shard_map.311 = (bf16[1024,768]{1,0:T(8,128)(2,1)}, bf16[1024,768]{1,0:T(8,128)(2,1)}, bf16[1024,1536]{1,0:T(8,128)(2,1)}, f32[48,768]{1,0:T(8,128)}, f32[8,768]{1,0:T(8,128)}, /*index=5*/f32[8,768]{1,0:T(8,128)}) custom-call(s32[3]{0:T(128)} %pad_add_fusion.my_ref.place_ref, f32[8,8,768]{2,1,0:T(8,128)} %bitcast.204, ...), custom_call_target="tpu_custom_call" | custom-call | flops 2651848704 | bytes 31457280 | tf_op jit(solution)/shard_map/pallas_call | solution.py:736
  530.0 3.4 fusion.16
  539.0 15.8 %shard_map.312 = (bf16[1024,2048]{1,0:T(8,128)(2,1)}, bf16[1024,768]{1,0:T(8,128)(2,1)}, f32[1,2048]{1,0:T(1,128)}) custom-call(s32[3]{0:T(128)} %pad_add_fusion.my_ref.place_ref, bf16[1024,768]{1,0:T(8,128)(2,1)} %get-tuple-element.188.bl_ref, bf16[1024,768]{1,0:T(8,128)(2,1)} %get-tuple-element.189.il_ref, f32[8,768]{1,0:T(8,128)} %get-tuple-element.190.end_ref, ...), custom_call_target="tpu_custom_call" | custom-call | flops 6505365504 | bytes 19398656 | tf_op jit(solution)/shard_map/pallas_call | solution.py:819
  554.7 5.4 collective-permute-done.19
  560.1 5.6 collective-permute-done.20
  578.8 4.1 fusion.82
  585.6 5.1 convolution_convert_fusion
  591.6 3.3 all-to-all-start.6
  595.5 4.6 shard_map.313
  600.7 4.2 all-to-all-start.5
  612.5 3.3 collective-permute-start.31
  620.2 14.2 %collective-permute-done.29 = bf16[1,256,768]{2,1,0:T(8,128)(2,1)S(1)} collective-permute-done((bf16[1,256,768]{2,1,0:T(8,128)(2,1)S(1)}, bf16[1,256,768]{2,1,0:T(8,128)(2,1)S(1)}, u32[]{:S(2)}, u32[]{:S(2)}) %collective-permute-start.29) | collective-permute-done | bytes 393248 | tf_op jit(solution)/shard_map/ppermute | solution.py:891
  634.8 25.0 %collective-permute-done.31 = bf16[2,128,2048]{2,1,0:T(8,128)(2,1)S(1)} collective-permute-done((bf16[2,128,2048]{2,1,0:T(8,128)(2,1)}, bf16[2,128,2048]{2,1,0:T(8,128)(2,1)S(1)}, u32[]{:S(2)}, u32[]{:S(2)}) %collective-permute-start.31) | collective-permute-done | bytes 1048608 | tf_op jit(solution)/shard_map/ppermute | solution.py:917
  664.1 6.1 bitcast_convert_fusion
  670.3 5.0 collective-permute-done.28
  676.3 7.6 add_convert_fusion
  696.2 12.6 %collective-permute-done.22 = bf16[2,256,768]{2,1,0:T(8,128)(2,1)} collective-permute-done((bf16[2,256,768]{2,1,0:T(8,128)(2,1)}, bf16[2,256,768]{2,1,0:T(8,128)(2,1)}, u32[]{:S(2)}, u32[]{:S(2)}) %collective-permute-start.22) | collective-permute-done | bytes 786464 | tf_op jit(solution)/shard_map/ppermute | solution.py:891
  712.6 5.8 collective-permute-done.24
  723.7 3.0 collective-permute-done.23
  729.5 4.6 shard_map.315
  734.1 4.2 all-to-all-start.7
  749.4 5.4 shard_map.314
  756.3 5.5 shard_map.316
  (288 shorter events, 122.7 us)
Async XLA Ops:
  8.0 46.5 %sort.10.cloned.1.call-start = ((), (), s32[]{:S(2)}) async-start(), calls=%async_computation.22 | async-start | bytes 98336 | tf_op jit(solution)/shard_map/jit(sort)/sort | solution.py:934
  9.6 120.6 %all-gather.11.cloned.1.call-start = ((), (), s32[]{:S(2)}) async-start(), calls=%async_computation.21 | async-start | bytes 7864320 | tf_op jit(solution)/shard_map/all_gather | solution.py:974
  21.9 54.7 %all-to-all-start = ((bf16[8,128,2048]{2,1,0:T(8,128)(2,1)}), bf16[8,128,2048]{2,1,0:T(8,128)(2,1)}, u32[]{:S(2)}, u32[]{:S(2)}) async-start(bf16[8,128,2048]{2,1,0:T(8,128)(2,1)} %bitcast.195), calls=%async_computation | async-start | bytes 8388608 | tf_op jit(solution)/shard_map/all_to_all | solution.py:888
  27.4 224.2 %all-gather.7.cloned.1.call-start = ((), (), s32[]{:S(2)}) async-start(), calls=%async_computation.13 | async-start | bytes 2621440 | tf_op jit(solution)/shard_map/all_gather | solution.py:1012
  76.6 21.3 %copy-start.35 = (f32[684]{0:T(1024)S(1)}, f32[684]{0:T(1024)}, u32[]{:S(2)}) copy-start(f32[684]{0:T(1024)} %param.27) | copy-start | bytes 8212
  76.6 21.3 %copy-start.31 = (f32[4,684]{1,0:T(4,128)S(1)}, f32[4,684]{1,0:T(4,128)}, u32[]{:S(2)}) copy-start(f32[4,684]{1,0:T(4,128)} %param.26) | copy-start | bytes 32836
  76.6 22.5 %copy-start.30 = (f32[684]{0:T(1024)S(1)}, f32[684]{0:T(1024)}, u32[]{:S(2)}) copy-start(f32[684]{0:T(1024)} %param.30) | copy-start | bytes 8212
  95.8 3.9 collective-permute-start
  130.3 35.2 %collective-permute-start.1 = (bf16[4,768,1024]{2,1,0:T(8,128)(2,1)}, bf16[4,768,1024]{2,1,0:T(8,128)(2,1)}, u32[]{:S(2)}, u32[]{:S(2)}) collective-permute-start(bf16[4,768,1024]{2,1,0:T(8,128)(2,1)} %bitcast.183), channel_id=1, source_target_pairs={{0,4},{4,0},{8,12},{12,8},{16,20},{20,16},{24,28},{28,24},{1,5},{5... | collective-permute-start | bytes 18874376 | tf_op jit(solution)/shard_map/ppermute | solution.py:891
  174.4 20.2 %copy-start.27 = (s32[8,128]{1,0:T(8,128)S(1)}, s32[8,128]{1,0:T(8,128)}, u32[]{:S(2)}) copy-start(s32[8,128]{1,0:T(8,128)} %fusion.72) | copy-start | bytes 12292
  178.3 7.1 collective-permute-start.2
  178.3 15.0 %collective-permute-start.3 = (bf16[128,2048]{1,0:T(8,128)(2,1)}, bf16[128,2048]{1,0:T(8,128)(2,1)}, u32[]{:S(2)}, u32[]{:S(2)}) collective-permute-start(bf16[128,2048]{1,0:T(8,128)(2,1)} %get-tuple-element.308), channel_id=1, source_target_pairs={{0,8},{4,12},{8,0},{12,4},{16,24},{20,28},{24,16},{28,20},{1,9},{5... | collective-permute-start | bytes 1572872 | tf_op jit(solution)/shard_map/ppermute | solution.py:994
  179.8 61.9 %all-to-all-start.2 = ((bf16[4,128,768]{2,1,0:T(8,128)(2,1)}), bf16[4,128,768]{2,1,0:T(8,128)(2,1)S(1)}, u32[]{:S(2)}, u32[]{:S(2)}) async-start(bf16[4,128,768]{2,1,0:T(8,128)(2,1)} %get-tuple-element.325), calls=%async_computation.2 | async-start | bytes 1572864 | tf_op jit(solution)/shard_map/all_to_all | solution.py:888
  183.3 115.5 %all-gather.9.cloned.1.call-start = ((), (), s32[]{:S(2)}) async-start(), calls=%async_computation.15 | async-start | bytes 2621440 | tf_op jit(solution)/shard_map/all_gather | solution.py:1012
  183.3 20.4 %collective-permute-start.4 = (bf16[128,2048]{1,0:T(8,128)(2,1)}, bf16[128,2048]{1,0:T(8,128)(2,1)}, u32[]{:S(2)}, u32[]{:S(2)}) collective-permute-start(bf16[128,2048]{1,0:T(8,128)(2,1)} %get-tuple-element.307), channel_id=1, source_target_pairs={{0,12},{4,8},{8,4},{12,0},{16,28},{20,24},{24,20},{28,16},{1,13},{... | collective-permute-start | bytes 1572872 | tf_op jit(solution)/shard_map/ppermute | solution.py:994
  183.8 20.0 %collective-permute-start.5 = (bf16[128,2048]{1,0:T(8,128)(2,1)S(1)}, bf16[128,2048]{1,0:T(8,128)(2,1)}, u32[]{:S(2)}, u32[]{:S(2)}) collective-permute-start(bf16[128,2048]{1,0:T(8,128)(2,1)S(1)} %get-tuple-element.306), channel_id=1, source_target_pairs={{0,16},{4,20},{8,24},{12,28},{16,0},{20,4},{24,8},{28,12},{1,17},{... | collective-permute-start | bytes 1572872 | tf_op jit(solution)/shard_map/ppermute | solution.py:994
  185.3 45.8 %collective-permute-start.6 = (bf16[128,2048]{1,0:T(8,128)(2,1)S(1)}, bf16[128,2048]{1,0:T(8,128)(2,1)}, u32[]{:S(2)}, u32[]{:S(2)}) collective-permute-start(bf16[128,2048]{1,0:T(8,128)(2,1)S(1)} %get-tuple-element.305), channel_id=1, source_target_pairs={{0,20},{4,16},{8,28},{12,24},{16,4},{20,0},{24,12},{28,8},{1,21},{... | collective-permute-start | bytes 1572872 | tf_op jit(solution)/shard_map/ppermute | solution.py:994
  185.4 45.6 %collective-permute-start.7 = (bf16[128,2048]{1,0:T(8,128)(2,1)S(1)}, bf16[128,2048]{1,0:T(8,128)(2,1)}, u32[]{:S(2)}, u32[]{:S(2)}) collective-permute-start(bf16[128,2048]{1,0:T(8,128)(2,1)S(1)} %get-tuple-element.304), channel_id=1, source_target_pairs={{0,24},{4,28},{8,16},{12,20},{16,8},{20,12},{24,0},{28,4},{1,25},{... | collective-permute-start | bytes 1572872 | tf_op jit(solution)/shard_map/ppermute | solution.py:994
  193.3 37.8 %collective-permute-start.8 = (bf16[128,2048]{1,0:T(8,128)(2,1)S(1)}, bf16[128,2048]{1,0:T(8,128)(2,1)}, u32[]{:S(2)}, u32[]{:S(2)}) collective-permute-start(bf16[128,2048]{1,0:T(8,128)(2,1)S(1)} %get-tuple-element.303), channel_id=1, source_target_pairs={{0,28},{4,24},{8,20},{12,16},{16,12},{20,8},{24,4},{28,0},{1,29},{... | collective-permute-start | bytes 1572872 | tf_op jit(solution)/shard_map/ppermute | solution.py:994
  251.5 98.8 %reduce-scatter.6.cloned.1.call-start = ((), (), s32[]{:S(2)}) async-start(), calls=%async_computation.14 | async-start | bytes 2621440 | tf_op jit(solution)/shard_map/reduce_scatter | solution.py:885
  284.7 103.8 %reduce-scatter.8.cloned.1.call-start = ((), (), s32[]{:S(2)}) async-start(), calls=%async_computation.16 | async-start | bytes 2621440 | tf_op jit(solution)/shard_map/reduce_scatter | solution.py:885
  331.9 207.1 %reduce-scatter.10.cloned.1.call-start = ((), (), s32[]{:S(2)}) async-start(), calls=%async_computation.17 | async-start | bytes 5242880 | tf_op jit(solution)/shard_map/reduce_scatter | solution.py:885
  331.9 7.9 %copy-start.41 = (bf16[1024,1536]{1,0:T(8,128)(2,1)S(1)}, bf16[1024,1536]{1,0:T(8,128)(2,1)}, u32[]{:S(2)}) copy-start(bf16[1024,1536]{1,0:T(8,128)(2,1)} %get-tuple-element.169) | copy-start | bytes 9437188
  331.9 7.9 %copy-start.46 = (bf16[1024,1024]{1,0:T(8,128)(2,1)S(1)}, bf16[1024,1024]{1,0:T(8,128)(2,1)}, u32[]{:S(2)}) copy-start(bf16[1024,1024]{1,0:T(8,128)(2,1)} %get-tuple-element.157) | copy-start | bytes 6291460
  350.3 11.1 %collective-permute-start.9 = (bf16[1024,1536]{1,0:T(8,128)(2,1)}, bf16[1024,1536]{1,0:T(8,128)(2,1)}, u32[]{:S(2)}, u32[]{:S(2)}) collective-permute-start(bf16[1024,1536]{1,0:T(8,128)(2,1)} %convolution_convert_fusion.3), channel_id=1, source_target_pairs={{0,4},{4,0},{8,12},{12,8},{16,20},{20,16},{24,28},{28,24},{1,5},{5... | collective-permute-start | bytes 9437192 | tf_op jit(solution)/shard_map/ppermute | solution.py:891
  350.3 18.6 %collective-permute-start.10 = (bf16[1024,1536]{1,0:T(8,128)(2,1)}, bf16[1024,1536]{1,0:T(8,128)(2,1)}, u32[]{:S(2)}, u32[]{:S(2)}) collective-permute-start(bf16[1024,1536]{1,0:T(8,128)(2,1)} %convolution_convert_fusion.2), channel_id=1, source_target_pairs={{0,4},{4,0},{8,12},{12,8},{16,20},{20,16},{24,28},{28,24},{1,5},{5... | collective-permute-start | bytes 9437192 | tf_op jit(solution)/shard_map/ppermute | solution.py:891
  350.8 24.7 %collective-permute-start.11 = (bf16[1024,1536]{1,0:T(8,128)(2,1)}, bf16[1024,1536]{1,0:T(8,128)(2,1)}, u32[]{:S(2)}, u32[]{:S(2)}) collective-permute-start(bf16[1024,1536]{1,0:T(8,128)(2,1)} %convolution_convert_fusion.1), channel_id=1, source_target_pairs={{0,4},{4,0},{8,12},{12,8},{16,20},{20,16},{24,28},{28,24},{1,5},{5... | collective-permute-start | bytes 9437192 | tf_op jit(solution)/shard_map/ppermute | solution.py:891
  350.8 10.6 %copy-start.47 = (bf16[1024,1024]{1,0:T(8,128)(2,1)S(1)}, bf16[1024,1024]{1,0:T(8,128)(2,1)}, u32[]{:S(2)}) copy-start(bf16[1024,1024]{1,0:T(8,128)(2,1)} %get-tuple-element.166) | copy-start | bytes 6291460
  361.4 7.5 copy-start.42
  361.4 7.5 copy-start.48
  368.9 6.6 copy-start.40
  368.9 6.6 copy-start.43
  399.8 45.2 %all-to-all-start.4 = ((bf16[4,128,768]{2,1,0:T(8,128)(2,1)}), bf16[4,128,768]{2,1,0:T(8,128)(2,1)S(1)}, u32[]{:S(2)}, u32[]{:S(2)}) async-start(bf16[4,128,768]{2,1,0:T(8,128)(2,1)} %get-tuple-element.175), calls=%async_computation.6 | async-start | bytes 1572864 | tf_op jit(solution)/shard_map/all_to_all | solution.py:888
  406.4 47.2 %collective-permute-start.17 = (bf16[2,256,768]{2,1,0:T(8,128)(2,1)}, bf16[2,256,768]{2,1,0:T(8,128)(2,1)}, u32[]{:S(2)}, u32[]{:S(2)}) collective-permute-start(bf16[2,256,768]{2,1,0:T(8,128)(2,1)} %dynamic-slice_bitcast_fusion.4), channel_id=1, source_target_pairs={{0,8},{4,12},{8,0},{12,4},{16,24},{20,28},{24,16},{28,20},{1,9},{5... | collective-permute-start | bytes 2359304 | tf_op jit(solution)/shard_map/ppermute | solution.py:891
  408.5 46.5 %collective-permute-start.18 = (bf16[2,256,768]{2,1,0:T(8,128)(2,1)}, bf16[2,256,768]{2,1,0:T(8,128)(2,1)}, u32[]{:S(2)}, u32[]{:S(2)}) collective-permute-start(bf16[2,256,768]{2,1,0:T(8,128)(2,1)} %dynamic-slice_bitcast_fusion.3), channel_id=1, source_target_pairs={{0,16},{4,20},{8,24},{12,28},{16,0},{20,4},{24,8},{28,12},{1,17},{... | collective-permute-start | bytes 2359304 | tf_op jit(solution)/shard_map/ppermute | solution.py:891
  411.2 118.8 %collective-permute-start.15 = (bf16[2,256,1536]{2,1,0:T(8,128)(2,1)}, bf16[2,256,1536]{2,1,0:T(8,128)(2,1)}, u32[]{:S(2)}, u32[]{:S(2)}) collective-permute-start(bf16[2,256,1536]{2,1,0:T(8,128)(2,1)} %dynamic-slice_bitcast_fusion.1), channel_id=1, source_target_pairs={{0,8},{4,12},{8,0},{12,4},{16,24},{20,28},{24,16},{28,20},{1,9},{5... | collective-permute-start | bytes 4718600 | tf_op jit(solution)/shard_map/ppermute | solution.py:891
  445.0 7.1 copy-start.7
  445.1 43.4 %all-to-all-start.3 = ((bf16[4,128,768]{2,1,0:T(8,128)(2,1)}), bf16[4,128,768]{2,1,0:T(8,128)(2,1)}, u32[]{:S(2)}, u32[]{:S(2)}) async-start(bf16[4,128,768]{2,1,0:T(8,128)(2,1)} %get-tuple-element.164), calls=%async_computation.4 | async-start | bytes 1572864 | tf_op jit(solution)/shard_map/all_to_all | solution.py:888
  449.2 279.5 %reduce-scatter.12.cloned.1.call-start = ((), (), s32[]{:S(2)}) async-start(), calls=%async_computation.18 | async-start | bytes 5242880 | tf_op jit(solution)/shard_map/reduce_scatter | solution.py:885
  452.1 81.3 %collective-permute-start.16 = (bf16[2,256,1536]{2,1,0:T(8,128)(2,1)}, bf16[2,256,1536]{2,1,0:T(8,128)(2,1)}, u32[]{:S(2)}, u32[]{:S(2)}) collective-permute-start(bf16[2,256,1536]{2,1,0:T(8,128)(2,1)} %dynamic-slice_bitcast_fusion), channel_id=1, source_target_pairs={{0,16},{4,20},{8,24},{12,28},{16,0},{20,4},{24,8},{28,12},{1,17},{... | collective-permute-start | bytes 4718600 | tf_op jit(solution)/shard_map/ppermute | solution.py:891
  458.3 77.0 %collective-permute-start.13 = (bf16[2,128,2048]{2,1,0:T(8,128)(2,1)}, bf16[2,128,2048]{2,1,0:T(8,128)(2,1)}, u32[]{:S(2)}, u32[]{:S(2)}) collective-permute-start(bf16[2,128,2048]{2,1,0:T(8,128)(2,1)} %pad_maximum_fusion), channel_id=1, source_target_pairs={{0,1},{1,2},{2,3},{4,5},{5,6},{6,7},{8,9},{9,10},{10,11},{12,13},{... | collective-permute-start | bytes 3145736 | tf_op jit(solution)/shard_map/ppermute | solution.py:917
  463.1 72.2 %collective-permute-start.14 = (bf16[2,128,2048]{2,1,0:T(8,128)(2,1)}, bf16[2,128,2048]{2,1,0:T(8,128)(2,1)}, u32[]{:S(2)}, u32[]{:S(2)}) collective-permute-start(bf16[2,128,2048]{2,1,0:T(8,128)(2,1)} %pad_maximum_fusion), channel_id=1, source_target_pairs={{1,0},{2,1},{3,2},{5,4},{6,5},{7,6},{9,8},{10,9},{11,10},{13,12},{... | collective-permute-start | bytes 3145736 | tf_op jit(solution)/shard_map/ppermute | solution.py:918
  528.4 6.8 collective-permute-start.12
  535.3 24.8 %collective-permute-start.19 = (bf16[2,128,2048]{2,1,0:T(8,128)(2,1)}, bf16[2,128,2048]{2,1,0:T(8,128)(2,1)}, u32[]{:S(2)}, u32[]{:S(2)}) collective-permute-start(bf16[2,128,2048]{2,1,0:T(8,128)(2,1)} %collective-permute-done.13), channel_id=1, source_target_pairs={{0,1},{1,2},{2,3},{4,5},{5,6},{6,7},{8,9},{9,10},{10,11},{12,13},{... | collective-permute-start | bytes 3145736 | tf_op jit(solution)/shard_map/ppermute | solution.py:917
  537.6 28.1 %collective-permute-start.20 = (bf16[2,128,2048]{2,1,0:T(8,128)(2,1)}, bf16[2,128,2048]{2,1,0:T(8,128)(2,1)}, u32[]{:S(2)}, u32[]{:S(2)}) collective-permute-start(bf16[2,128,2048]{2,1,0:T(8,128)(2,1)} %collective-permute-done.14), channel_id=1, source_target_pairs={{1,0},{2,1},{3,2},{5,4},{6,5},{7,6},{9,8},{10,9},{11,10},{13,12},{... | collective-permute-start | bytes 3145736 | tf_op jit(solution)/shard_map/ppermute | solution.py:918
  590.7 85.6 %collective-permute-start.21 = (bf16[1024,1536]{1,0:T(8,128)(2,1)}, bf16[1024,1536]{1,0:T(8,128)(2,1)}, u32[]{:S(2)}, u32[]{:S(2)}) collective-permute-start(bf16[1024,1536]{1,0:T(8,128)(2,1)} %convolution_convert_fusion), channel_id=1, source_target_pairs={{0,4},{4,0},{8,12},{12,8},{16,20},{20,16},{24,28},{28,24},{1,5},{5... | collective-permute-start | bytes 9437192 | tf_op jit(solution)/shard_map/ppermute | solution.py:891
  591.6 9.1 %all-to-all-start.6 = ((f32[4,2,512]{2,1,0:T(2,128)}), f32[4,2,512]{2,1,0:T(2,128)S(1)}, u32[]{:S(2)}, u32[]{:S(2)}) async-start(f32[4,2,512]{2,1,0:T(2,128)} %bitcast.70), calls=%async_computation.10 | async-start | bytes 32768 | tf_op jit(solution)/shard_map/all_to_all | solution.py:888
  600.7 128.1 %all-to-all-start.5 = ((bf16[8,128,512]{2,1,0:T(8,128)(2,1)}), bf16[8,128,512]{2,1,0:T(8,128)(2,1)}, u32[]{:S(2)}, u32[]{:S(2)}) async-start(bf16[8,128,512]{2,1,0:T(8,128)(2,1)} %bitcast.202), calls=%async_computation.9 | async-start | bytes 2097152 | tf_op jit(solution)/shard_map/all_to_all | solution.py:888
  604.9 123.9 %all-reduce.20.cloned.1.call-start = ((), (), s32[]{:S(2)}) async-start(), calls=%async_computation.19 | async-start | bytes 3244032 | tf_op jit(solution)/shard_map/psum | solution.py:1142
  605.8 123.0 %reduce-scatter.14.cloned.1.call-start = ((), (), s32[]{:S(2)}) async-start(), calls=%async_computation.20 | async-start | bytes 3538944 | tf_op jit(solution)/shard_map/reduce_scatter | solution.py:885
  608.1 84.2 %collective-permute-start.26 = (bf16[1,256,1536]{2,1,0:T(8,128)(2,1)}, bf16[1,256,1536]{2,1,0:T(8,128)(2,1)}, u32[]{:S(2)}, u32[]{:S(2)}) collective-permute-start(bf16[1,256,1536]{2,1,0:T(8,128)(2,1)} %constant_dynamic-slice_fusion.3), channel_id=1, source_target_pairs={{0,16},{4,20},{8,24},{12,28},{16,0},{20,4},{24,8},{28,12},{1,17},{... | collective-permute-start | bytes 2359304 | tf_op jit(solution)/shard_map/ppermute | solution.py:891
  611.0 23.7 %copy-start.10 = (bf16[2,256,768]{2,1,0:T(8,128)(2,1)S(1)}, bf16[2,256,768]{2,1,0:T(8,128)(2,1)}, u32[]{:S(2)}) copy-start(bf16[2,256,768]{2,1,0:T(8,128)(2,1)} %fusion.37) | copy-start | bytes 2359300
  611.0 23.4 %collective-permute-start.29 = (bf16[1,256,768]{2,1,0:T(8,128)(2,1)S(1)}, bf16[1,256,768]{2,1,0:T(8,128)(2,1)S(1)}, u32[]{:S(2)}, u32[]{:S(2)}) collective-permute-start(bf16[1,256,768]{2,1,0:T(8,128)(2,1)S(1)} %constant_dynamic-slice_fusion), channel_id=1, source_target_pairs={{0,8},{4,12},{8,0},{12,4},{16,24},{20,28},{24,16},{28,20},{1,9},{5... | collective-permute-start | bytes 1179656 | tf_op jit(solution)/shard_map/ppermute | solution.py:891
  612.5 47.3 %collective-permute-start.31 = (bf16[2,128,2048]{2,1,0:T(8,128)(2,1)}, bf16[2,128,2048]{2,1,0:T(8,128)(2,1)S(1)}, u32[]{:S(2)}, u32[]{:S(2)}) collective-permute-start(bf16[2,128,2048]{2,1,0:T(8,128)(2,1)} %collective-permute-done.19), channel_id=1, source_target_pairs={{0,1},{1,2},{2,3},{4,5},{5,6},{6,7},{8,9},{9,10},{10,11},{12,13},{... | collective-permute-start | bytes 3145736 | tf_op jit(solution)/shard_map/ppermute | solution.py:917
  615.9 47.1 %collective-permute-start.30 = (bf16[2,128,2048]{2,1,0:T(8,128)(2,1)}, bf16[2,128,2048]{2,1,0:T(8,128)(2,1)S(1)}, u32[]{:S(2)}, u32[]{:S(2)}) collective-permute-start(bf16[2,128,2048]{2,1,0:T(8,128)(2,1)} %collective-permute-done.20), channel_id=1, source_target_pairs={{1,0},{2,1},{3,2},{5,4},{6,5},{7,6},{9,8},{10,9},{11,10},{13,12},{... | collective-permute-start | bytes 3145736 | tf_op jit(solution)/shard_map/ppermute | solution.py:918
  634.4 86.8 %collective-permute-start.27 = (bf16[1,256,1536]{2,1,0:T(8,128)(2,1)}, bf16[1,256,1536]{2,1,0:T(8,128)(2,1)}, u32[]{:S(2)}, u32[]{:S(2)}) collective-permute-start(bf16[1,256,1536]{2,1,0:T(8,128)(2,1)} %constant_dynamic-slice_fusion.2), channel_id=1, source_target_pairs={{0,8},{4,12},{8,0},{12,4},{16,24},{20,28},{24,16},{28,20},{1,9},{5... | collective-permute-start | bytes 2359304 | tf_op jit(solution)/shard_map/ppermute | solution.py:891
  659.8 15.4 %collective-permute-start.28 = (bf16[1,256,768]{2,1,0:T(8,128)(2,1)}, bf16[1,256,768]{2,1,0:T(8,128)(2,1)}, u32[]{:S(2)}, u32[]{:S(2)}) collective-permute-start(bf16[1,256,768]{2,1,0:T(8,128)(2,1)} %constant_dynamic-slice_fusion.1), channel_id=1, source_target_pairs={{0,16},{4,20},{8,24},{12,28},{16,0},{20,4},{24,8},{28,12},{1,17},{... | collective-permute-start | bytes 1179656 | tf_op jit(solution)/shard_map/ppermute | solution.py:891
  685.2 23.6 %collective-permute-start.22 = (bf16[2,256,768]{2,1,0:T(8,128)(2,1)}, bf16[2,256,768]{2,1,0:T(8,128)(2,1)}, u32[]{:S(2)}, u32[]{:S(2)}) collective-permute-start(bf16[2,256,768]{2,1,0:T(8,128)(2,1)} %dynamic-slice_bitcast_fusion.2), channel_id=1, source_target_pairs={{0,8},{4,12},{8,0},{12,4},{16,24},{20,28},{24,16},{28,20},{1,9},{5... | collective-permute-start | bytes 2359304 | tf_op jit(solution)/shard_map/ppermute | solution.py:891
  691.3 27.1 %collective-permute-start.24 = (bf16[2,256,768]{1,2,0:T(8,128)(2,1)}, bf16[2,256,768]{1,2,0:T(8,128)(2,1)}, u32[]{:S(2)}, u32[]{:S(2)}) collective-permute-start(bf16[2,256,768]{1,2,0:T(8,128)(2,1)} %bitcast.205), channel_id=1, source_target_pairs={{0,16},{4,20},{8,24},{12,28},{16,0},{20,4},{24,8},{28,12},{1,17},{... | collective-permute-start | bytes 2359304 | tf_op jit(solution)/shard_map/ppermute | solution.py:891
  696.2 22.2 %copy-start.11 = (bf16[1,2,256,768]{2,3,1,0:T(8,128)(2,1)S(1)}, bf16[1,2,256,768]{2,3,1,0:T(8,128)(2,1)}, u32[]{:S(2)}) copy-start(bf16[1,2,256,768]{2,3,1,0:T(8,128)(2,1)} %copy.155) | copy-start | bytes 2359300
  710.4 16.3 %collective-permute-start.23 = (bf16[1,256,768]{2,1,0:T(8,128)(2,1)S(1)}, bf16[1,256,768]{2,1,0:T(8,128)(2,1)S(1)}, u32[]{:S(2)}, u32[]{:S(2)}) collective-permute-start(bf16[1,256,768]{2,1,0:T(8,128)(2,1)S(1)} %constant_dynamic-slice_fusion.7), channel_id=1, source_target_pairs={{0,16},{4,20},{8,24},{12,28},{16,0},{20,4},{24,8},{28,12},{1,17},{... | collective-permute-start | bytes 1179656 | tf_op jit(solution)/shard_map/ppermute | solution.py:891
  719.8 7.9 %collective-permute-start.25 = (bf16[1,256,768]{1,2,0:T(8,128)(2,1)S(1)}, bf16[1,256,768]{1,2,0:T(8,128)(2,1)S(1)}, u32[]{:S(2)}, u32[]{:S(2)}) collective-permute-start(bf16[1,256,768]{1,2,0:T(8,128)(2,1)S(1)} %constant_dynamic-slice_fusion.4), channel_id=1, source_target_pairs={{0,8},{4,12},{8,0},{12,4},{16,24},{20,28},{24,16},{28,20},{1,9},{5... | collective-permute-start | bytes 1179656 | tf_op jit(solution)/shard_map/ppermute | solution.py:891
  734.1 22.2 %all-to-all-start.7 = ((bf16[8,128,512]{2,1,0:T(8,128)(2,1)}), bf16[8,128,512]{2,1,0:T(8,128)(2,1)}, u32[]{:S(2)}, u32[]{:S(2)}) async-start(bf16[8,128,512]{2,1,0:T(8,128)(2,1)} %bitcast.203), calls=%async_computation.12 | async-start | bytes 2097152 | tf_op jit(solution)/shard_map/all_to_all | solution.py:888
  755.4 6.4 copy-start.1
  (34 other events, 131.0 us)
Sparse Core Ops, SparseCore 0:
  12.4 3.7 sort.12.cloned.1.call-done
  609.4 68.9 all-reduce.19
  (1 shorter events, 0.0 us)
Sparse Core Ops, SparseCore 1:
  12.3 117.9 all-gather.10
  174.5 61.4 all-gather.6
  251.6 47.1 all-gather.8
  301.2 42.3 reduce-scatter.5
  345.8 42.7 reduce-scatter.7
  391.0 113.0 reduce-scatter.9
  565.8 93.8 reduce-scatter.11
  670.3 56.3 reduce-scatter.13

commit v2 on v1

--- a/solution.py
+++ b/solution.py
@@ -45,7 +45,9 @@
         compiler_params=pltpu.CompilerParams(
             dimension_semantics=("arbitrary",) * len(grid), vmem_limit_bytes=60 * MIB
         ),
-        cost_estimate=pl.CostEstimate(flops=flops, bytes_accessed=moved, transcendentals=0),
+        cost_estimate=pl.CostEstimate(
+            flops=flops, bytes_accessed=moved, transcendentals=0
+        ),
     )
 
 
@@ -111,6 +113,41 @@
     )(turn, dest_row, dest_col, values)
 
 
+def send_blocks(turn, dest_row, dest_col, values, count):
+    rows, width = values.shape
+    size = rows // count
+
+    def body(turn_ref, row_ref, col_ref, val_ref, *refs):
+        rank_ref = refs[count]
+        i = pl.program_id(0)
+
+        @pl.when(i == 0)
+        def _():
+            before = jnp.where(col_ref[...] < row_ref[...], 1.0, 0.0)
+            rank = jnp.sum(before, axis=0, keepdims=True).astype(jnp.int32)
+            rank_ref[...] = rank ^ turn_ref[0]
+
+        spot = lax.broadcasted_iota(jnp.int32, (size, rows), 0) + i * size
+        moved = mm(one_hot(spot, rank_ref[...]), val_ref[...]).astype(BF16)
+        for k in range(count):
+
+            @pl.when(i == k)
+            def _(k=k):
+                refs[k][...] = moved
+
+    return call(
+        body,
+        (count,),
+        [whole((1, rows)), whole((rows, 1)), whole((rows, width))],
+        [whole((size, width))] * count,
+        [struct((size, width), BF16)] * count,
+        [pltpu.VMEM((1, rows), jnp.int32)],
+        prefetch=1,
+        flops=2 * rows * rows * width,
+        moved=4 * rows * width,
+    )(turn, dest_row, dest_col, values)
+
+
 def place_rows(place_col, landing_row, values):
     rows, width = values.shape
     tile = 256
@@ -159,9 +196,9 @@
             for copy in copies:
                 copy.wait()
 
-        moved = mm(one_hot(place_ref[...], land_ref[...]), val_ref[...])
-        out_ref[...] = moved.astype(BF16)
-        split_columns(near_ref, far_ref, moved.astype(BF16), my_ref[2], parts)
+        moved = mm(one_hot(place_ref[...], land_ref[...]), val_ref[...]).astype(BF16)
+        out_ref[...] = moved
+        split_columns(near_ref, far_ref, moved, my_ref[2], parts)
 
     return call(
         body,
@@ -206,14 +243,14 @@
     )(dest_row, dest_col, values)
 
 
-def project(place, landing_row, arrived, gain, weights, parts):
+def project(place, landing_row, arrived, gain, w_branch, w_input, half, parts):
     rows, width = arrived.shape
-    wide = weights.shape[1]
-    half = wide // 2
+    channels = w_branch.shape[0]
+    wide = 2 * half
     tile = 256
 
     def body(
-        my_ref, land_ref, arr_ref, gain_ref, w_ref, stream_ref, near_ref, far_ref, branch_ref, inputs_ref
+        my_ref, land_ref, arr_ref, gain_ref, wb_ref, wi_ref, stream_ref, near_ref, far_ref, branch_ref, inputs_ref
     ):
         i = pl.program_id(0)
         place = lax.broadcasted_iota(jnp.int32, (tile, rows), 0) + i * tile
@@ -222,13 +259,15 @@
         inv = lax.rsqrt(jnp.mean(x * x, axis=-1, keepdims=True) + EPSILON)
         hidden = (x * inv * gain_ref[...]).astype(BF16)
         split_columns(near_ref, far_ref, hidden, my_ref[2], parts)
-        branch_ref[...] = mm(hidden, w_ref[:, :half])
-        inputs_ref[...] = mm(hidden, w_ref[:, half:])
+        for out_ref, w_ref in ((branch_ref, wb_ref), (inputs_ref, wi_ref)):
+            if channels < half:
+                out_ref[...] = jnp.zeros_like(out_ref)
+            out_ref[:, :channels] = mm(hidden, w_ref[...], NT)
 
     return call(
         body,
         (rows // tile,),
-        [whole((1, rows)), whole((rows, width)), whole((1, width)), whole((width, wide))],
+        [whole((1, rows)), whole((rows, width)), whole((1, width))] + [whole((channels, width))] * 2,
         [
             pl.BlockSpec((tile, width), lambda i, *_: (i, 0)),
             pl.BlockSpec((tile, width // 2), lambda i, *_: (i, 0)),
@@ -246,7 +285,7 @@
         prefetch=1,
         flops=2 * rows * width * (rows + wide),
         moved=6 * rows * width + 2 * width * wide + 4 * rows * wide,
-    )(place, landing_row, arrived, gain, weights)
+    )(place, landing_row, arrived, gain, w_branch, w_input)
 
 
 def tile_scan(rates, drives, keep_in, state_in, reverse):
@@ -364,10 +403,11 @@
     shards = pieces.shape[0]
     tile = rows // owners // CHUNKS
 
-    def body(my_ref, pieces_ref, local_ref, prefix_ref, branch_ref, states_ref, mixed_ref, carry_ref):
+    def body(my_ref, pieces_ref, local_ref, prefix_ref, branch_ref, states_ref, carry_ref, *mixed_refs):
         mine = my_ref[0]
-
-        @pl.when(pl.program_id(0) == 0)
+        i = pl.program_id(0)
+
+        @pl.when(i == 0)
         def _():
             entering = jnp.zeros((1, width), F32)
             for s in range(shards - 1):
@@ -377,7 +417,12 @@
 
         states = local_ref[...] + prefix_ref[...] * carry_ref[0:1]
         states_ref[...] = states
-        mixed_ref[0, 0] = (states * gelu(branch_ref[...])).astype(BF16)
+        mixed = (states * gelu(branch_ref[...])).astype(BF16)
+        for c in range(CHUNKS):
+
+            @pl.when(i % CHUNKS == c)
+            def _(c=c):
+                mixed_refs[c][0] = mixed
 
     tiles = pl.BlockSpec((tile, width), lambda i, *_: (i, 0))
     return call(
@@ -386,27 +431,28 @@
         [whole(pieces.shape), tiles, tiles, tiles],
         [
             tiles,
-            pl.BlockSpec((1, 1, tile, width), lambda i, *_: (i % CHUNKS, i // CHUNKS, 0, 0)),
             whole((8, width)),
-        ],
-        [
-            struct((rows, width), F32),
-            struct((CHUNKS, owners, tile, width), BF16),
-            struct((8, width), F32),
-        ],
+        ]
+        + [pl.BlockSpec((1, tile, width), lambda i, *_: (i // CHUNKS, 0, 0))] * CHUNKS,
+        [struct((rows, width), F32), struct((8, width), F32)]
+        + [struct((owners, tile, width), BF16)] * CHUNKS,
         prefetch=1,
         flops=60 * rows * width,
         moved=18 * rows * width,
     )(place, pieces, local, prefix, branch)
 
 
-def output_rows(chunk, place, mixed_full, w_near, w_far, stream, gain):
-    sources, own, width = mixed_full.shape
+def output_rows(chunk, place, mixed_full, w_near, w_far, stream, gain, kept):
+    sources, sub, width = mixed_full.shape
+    own = sub * CHUNKS
+    channels = w_near.shape[1]
     model = stream.shape[1]
     half = model // 2
 
-    def body(place_ref, mixed_ref, near_ref, far_ref, stream_ref, gain_ref, resid_ref, normed_ref):
+    def body(place_ref, mixed_ref, near_ref, far_ref, stream_ref, gain_ref, *rest):
+        resid_ref, rows_ref, normed_ref = rest[-3:]
         s = pl.program_id(0)
+        rows_ref[...] = mixed_ref[0]
         near = pl.ds(pl.multiple_of(place_ref[2] * half, half), half)
         far = pl.ds(pl.multiple_of((1 - place_ref[2]) * half, half), half)
 
@@ -414,8 +460,9 @@
         def _():
             resid_ref[...] = stream_ref[...].astype(F32)
 
-        resid_ref[:, near] += mm(mixed_ref[0], near_ref[0])
-        resid_ref[:, far] += mm(mixed_ref[0], far_ref[0])
+        mixed = mixed_ref[0, :, :channels]
+        resid_ref[:, near] += mm(mixed, near_ref[0])
+        resid_ref[:, far] += mm(mixed, far_ref[0])
 
         @pl.when(s == sources - 1)
         def _():
@@ -423,34 +470,49 @@
             inv = lax.rsqrt(jnp.mean(x * x, axis=-1, keepdims=True) + EPSILON)
             normed_ref[...] = (x * inv * gain_ref[...]).astype(BF16)
 
+    kept = tuple(kept)
     return call(
         body,
         (sources,),
         [
-            pl.BlockSpec((1, own, width), lambda s, *_: (s, 0, 0)),
-            pl.BlockSpec((1, width, half), lambda s, *_: (s, 0, 0)),
-            pl.BlockSpec((1, width, half), lambda s, *_: (s, 0, 0)),
-            pl.BlockSpec((own, model), lambda s, p: (p[1] * CHUNKS + chunk, 0)),
+            pl.BlockSpec((1, sub, width), lambda s, *_: (s, 0, 0)),
+            pl.BlockSpec((1, channels, half), lambda s, *_: (s, 0, 0)),
+            pl.BlockSpec((1, channels, half), lambda s, *_: (s, 0, 0)),
+            pl.BlockSpec((sub, model), lambda s, p: (p[1] * CHUNKS + chunk, 0)),
             whole((1, model)),
-        ],
-        [whole((own, model)), whole((own, model))],
-        [struct((own, model), F32), struct((own, model), BF16)],
+        ]
+        + [pl.BlockSpec(memory_space=pl.ANY)] * len(kept),
+        [
+            pl.BlockSpec((sub, model), lambda s, *_: (chunk, 0)),
+            pl.BlockSpec((sub, width), lambda s, *_: (chunk, s)),
+            whole((sub, model)),
+        ],
+        [
+            struct((own, model), F32),
+            struct((own, sources * width), BF16),
+            struct((sub, model), BF16),
+        ],
         prefetch=1,
-        flops=2 * sources * own * width * model,
-        moved=2 * sources * width * model + 8 * own * model,
-    )(place, mixed_full, w_near, w_far, stream, gain)
+        aliases={6 + j: j for j in range(len(kept))},
+        flops=2 * sources * sub * width * model,
+        moved=2 * sources * width * model + 8 * sub * model,
+    )(place, mixed_full, w_near, w_far, stream, gain, *kept)
+
+
+def mlp_tile(hidden):
+    return 256 if hidden % 256 == 0 else LANES
 
 
 def mlp_chunk(chunk, place, normed, upstream, resid_own, w_gate, w_up, w_down, parts, kept):
     rows, model = normed.shape
     hidden = w_gate.shape[1]
     total = upstream.shape[0]
-    sub = resid_own.shape[0]
-    tile = 256 if hidden % 256 == 0 else LANES
+    sub = resid_own.shape[0] // CHUNKS
+    tile = mlp_tile(hidden)
     steps = hidden // tile
 
     def body(place_ref, n_ref, u_ref, r_ref, wg_ref, wu_ref, wd_ref, *rest):
-        act_ref, gate_ref, up_ref, near_ref, far_ref, down_ref, grad_ref, down_acc, grad_acc = rest[-9:]
+        act_ref, pair_ref, near_ref, far_ref, down_ref, grad_ref, down_acc, grad_acc = rest[-8:]
         s = pl.program_id(0)
 
         @pl.when(s == 0)
@@ -468,8 +530,8 @@
         gate_low = (inner * up_pre * slope).astype(BF16)
         up_low = (inner * act).astype(BF16)
         act_ref[...] = inner_act
-        gate_ref[...] = gate_low
-        up_ref[...] = up_low
+        pair_ref[:, :tile] = gate_low
+        pair_ref[:, tile:] = up_low
         down_acc[...] += mm(inner_act, wd_ref[...])
         both = mm(gate_low, wg_ref[...], NT) + mm(up_low, wu_ref[...], NT)
 
@@ -486,34 +548,31 @@
             down_ref[...] = down_acc[...].astype(BF16)
             grad_ref[...] = grad_acc[...].astype(BF16)
 
-    slots = pl.BlockSpec((rows, tile), lambda s, *_: (chunk, s))
-    any_spec = pl.BlockSpec(memory_space=pl.ANY)
+    rows_of = pl.BlockSpec((rows, model), lambda s, *_: (chunk, 0))
     kept = tuple(kept)
     return call(
         body,
         (steps,),
         [
             whole((rows, model)),
-            pl.BlockSpec((rows, model), lambda s, *_: (chunk, 0)),
-            whole((sub, model)),
+            rows_of,
+            pl.BlockSpec((sub, model), lambda s, *_: (chunk, 0)),
             pl.BlockSpec((model, tile), lambda s, *_: (0, s)),
             pl.BlockSpec((model, tile), lambda s, *_: (0, s)),
             pl.BlockSpec((tile, model), lambda s, *_: (s, 0)),
         ]
-        + [any_spec] * len(kept),
-        [
-            slots,
-            slots,
-            slots,
+        + [pl.BlockSpec(memory_space=pl.ANY)] * len(kept),
+        [
+            pl.BlockSpec((rows, tile), lambda s, *_: (chunk, s)),
+            pl.BlockSpec((rows, 2 * tile), lambda s, *_: (chunk, s)),
             pl.BlockSpec((rows, model // 2), lambda s, *_: (chunk, 0)),
             pl.BlockSpec((rows, model // 2), lambda s, *_: (chunk, 0)),
-            pl.BlockSpec((rows, model), lambda s, *_: (chunk, 0)),
+            rows_of,
             whole((rows, model)),
         ],
         [
             struct((total, hidden), BF16),
-            struct((total, hidden), BF16),
-            struct((total, hidden), BF16),
+            struct((total, 2 * hidden), BF16),
             struct((total, model // 2), BF16),
             struct((total, model // 2), BF16),
             struct((total, model), BF16),
@@ -527,11 +586,14 @@
     )(place, normed, upstream, resid_own, w_gate, w_up, w_down, *kept)
 
 
-def resid_backward(chunk, place, normed_grad, upstream, resid_own, gain, w_near, w_far):
-    own, model = resid_own.shape
-    sources, width, half = w_near.shape
-
-    def body(place_ref, g_ref, up_ref, r_ref, gain_ref, near_ref, far_ref, rg_ref, low_ref, mg_ref, sum_ref):
+def resid_backward(chunk, place, normed_grad, upstream, resid_own, gain, w_near, w_far, width, parts, kept):
+    sub, model = normed_grad.shape
+    own = resid_own.shape[0]
+    sources, channels, half = w_near.shape
+
+    def body(place_ref, g_ref, up_ref, r_ref, gain_ref, near_ref, far_ref, *rest):
+        low_near_ref, low_far_ref, rg_ref, mg_ref, sum_ref, low_ref = rest[-6:]
+
         @pl.when(pl.program_id(0) == 0)
         def _():
             x = r_ref[...]
@@ -543,49 +605,60 @@
             grad = up_ref[...].astype(F32) + inv * (scaled - unit * dot)
             rg_ref[...] = grad
             low_ref[...] = grad.astype(BF16)
+            split_columns(low_near_ref, low_far_ref, grad.astype(BF16), place_ref[2], parts)
             sum_ref[...] = jnp.sum(g * unit, axis=0, keepdims=True)
 
         near = pl.ds(pl.multiple_of(place_ref[2] * half, half), half)
         far = pl.ds(pl.multiple_of((1 - place_ref[2]) * half, half), half)
-        mg_ref[0] = (mm(low_ref[:, near], near_ref[0], NT) + mm(low_ref[:, far], far_ref[0], NT)).astype(BF16)
-
-    rows = whole((own, model))
+        if channels < width:
+            mg_ref[...] = jnp.zeros_like(mg_ref)
+        mg_ref[0, :, :channels] = (
+            mm(low_ref[:, near], near_ref[0], NT) + mm(low_ref[:, far], far_ref[0], NT)
+        ).astype(BF16)
+
+    rows = pl.BlockSpec((sub, model), lambda s, *_: (chunk, 0))
+    kept = tuple(kept)
     return call(
         body,
         (sources,),
         [
-            rows,
-            pl.BlockSpec((own, model), lambda s, p: (chunk * sources + p[1], 0)),
+            whole((sub, model)),
+            pl.BlockSpec((sub, model), lambda s, p: (chunk * sources + p[1], 0)),
             rows,
             whole((1, model)),
-            pl.BlockSpec((1, width, half), lambda s, *_: (s, 0, 0)),
-            pl.BlockSpec((1, width, half), lambda s, *_: (s, 0, 0)),
-        ],
-        [rows, rows, pl.BlockSpec((1, own, width), lambda s, *_: (s, 0, 0)), whole((1, model))],
-        [
+            pl.BlockSpec((1, channels, half), lambda s, *_: (s, 0, 0)),
+            pl.BlockSpec((1, channels, half), lambda s, *_: (s, 0, 0)),
+        ]
+        + [pl.BlockSpec(memory_space=pl.ANY)] * len(kept),
+        [
+            pl.BlockSpec((sub, half), lambda s, *_: (chunk, 0)),
+            pl.BlockSpec((sub, half), lambda s, *_: (chunk, 0)),
+            rows,
+            pl.BlockSpec((1, sub, width), lambda s, *_: (s, chunk, 0)),
+            whole((1, model)),
+        ],
+        [
+            struct((own, half), BF16),
+            struct((own, half), BF16),
             struct((own, model), F32),
-            struct((own, model), BF16),
             struct((sources, own, width), BF16),
             struct((1, model), F32),
         ],
+        [pltpu.VMEM((sub, model), BF16)],
         prefetch=1,
-        flops=2 * sources * own * width * model,
-        moved=2 * sources * width * model + 14 * own * model,
-    )(place, normed_grad, upstream, resid_own, gain, w_near, w_far)
-
-
-def recurrent_back_scan(mixed_grads, branch, keep, tail):
+        aliases={7 + j: j for j in range(len(kept))},
+        flops=2 * sources * sub * width * model,
+        moved=2 * sources * width * model + 14 * sub * model,
+    )(place, normed_grad, upstream, resid_own, gain, w_near, w_far, *kept)
+
+
+def recurrent_back_scan(mixed_grad, branch, keep, tail):
     rows, width = branch.shape
-    owners, sub = mixed_grads[0].shape[:2]
-    tile = sub * CHUNKS
-    tiles_n = owners
-
-    def body(*refs):
-        parts = refs[:CHUNKS]
-        branch_ref, keep_ref, tail_ref, grad_ref, after_ref, edge_ref, mg_ref, ext, carry = refs[CHUNKS:]
+    tile = 256
+    tiles_n = rows // tile
+
+    def body(mg_ref, branch_ref, keep_ref, tail_ref, grad_ref, after_ref, edge_ref, ext, carry):
         i = pl.program_id(0)
-        for c in range(CHUNKS):
-            mg_ref[c * sub : (c + 1) * sub] = parts[c][0]
 
         @pl.when(i == 0)
         def _():
@@ -619,19 +692,13 @@
     return call(
         body,
         (tiles_n,),
-        [pl.BlockSpec((1, sub, width), lambda i: (tiles_n - 1 - i, 0, 0))] * CHUNKS
-        + [tiles, tiles, whole((8, width))],
-        [tiles, tiles, whole((8, width)), tiles],
-        [
-            struct((rows, width), F32),
-            struct((rows, width), F32),
-            struct((8, width), F32),
-            struct((rows, width), BF16),
-        ],
+        [tiles, tiles, tiles, whole((8, width))],
+        [tiles, tiles, whole((8, width))],
+        [struct((rows, width), F32), struct((rows, width), F32), struct((8, width), F32)],
         [pltpu.VMEM((tile + 8, width), F32), pltpu.VMEM((8, width), F32)],
         flops=100 * rows * width,
         moved=18 * rows * width,
-    )(*mixed_grads, branch, keep, tail)
+    )(mixed_grad, branch, keep, tail)
 
 
 def recurrent_backward(
@@ -743,7 +810,7 @@
         ],
         [tiles, tiles, wide, whole((48, width)), small, small],
         [
-            struct((rows, width), BF16),
+            struct((rows, 2 * width), BF16),
             struct((rows, width), BF16),
             struct((rows, 2 * width), BF16),
             struct((48, width), F32),
@@ -766,17 +833,17 @@
     )
 
 
-def input_backward(place, branch_low, inputs_low, end, returned, weights, stream, gain, resid_grads):
-    rows, width = branch_low.shape
+def input_backward(place, rec_low, inputs_low, end, returned, w_branch, w_input, stream, gain, resid_grad):
+    rows, width = inputs_low.shape
+    channels = w_branch.shape[0]
     model = stream.shape[1]
-    sub = resid_grads[0].shape[0]
-    tile = sub * CHUNKS
+    tile = resid_grad.shape[0]
     steps = rows // tile
 
     def body(
-        place_ref, bl_ref, il_ref, end_ref, ret_ref, w_ref, x_ref, gain_ref, *rest
+        place_ref, bl_ref, il_ref, end_ref, ret_ref, wb_ref, wi_ref, x_ref, gain_ref, rg_ref,
+        part_ref, fixed_ref, sum_ref,
     ):
-        part_ref, fixed_ref, sum_ref = rest[CHUNKS:]
         i = pl.program_id(0)
         fixed_ref[...] = il_ref[...]
 
@@ -787,7 +854,7 @@
             )
             fixed_ref[tile - 16 : tile] = tail.astype(BF16)
 
-        g = mm(bl_ref[...], w_ref[:, :width], NT) + mm(fixed_ref[...], w_ref[:, width:], NT)
+        g = mm(bl_ref[:, :channels], wb_ref[...]) + mm(fixed_ref[:, :channels], wi_ref[...])
         x = x_ref[...].astype(F32)
         inv = lax.rsqrt(jnp.mean(x * x, axis=-1, keepdims=True) + EPSILON)
         unit = x * inv
@@ -806,9 +873,7 @@
 
         @pl.when(i == place_ref[1])
         def _():
-            for c in range(CHUNKS):
-                cut = slice(c * sub, (c + 1) * sub)
-                part_ref[cut] = (part[cut] + rest[c][...]).astype(BF16)
+            part_ref[...] = (part + rg_ref[...]).astype(BF16)
 
         @pl.when(i != place_ref[1])
         def _():
@@ -820,16 +885,40 @@
         body,
         (steps,),
         [
-            tiles, tiles, whole((8, width)), whole((8, width)), whole((model, 2 * width)), wide,
-            whole((1, model)),
-        ]
-        + [whole((sub, model))] * CHUNKS,
-        [wide, tiles, whole((1, model))],
-        [struct((rows, model), BF16), struct((rows, width), BF16), struct((1, model), F32)],
+            tiles, tiles, whole((8, width)), whole((8, width)), whole((channels, model)), whole((channels, model)), wide,
+            whole((1, model)), whole((tile, model)),
+        ],
+        [wide, pl.BlockSpec((tile, width), lambda i, *_: (i, 1)), whole((1, model))],
+        [struct((rows, model), BF16), struct((rows, 2 * width), BF16), struct((1, model), F32)],
         prefetch=1,
+        aliases={1: 1},
         flops=4 * rows * width * model + 30 * rows * model,
         moved=4 * rows * model + 4 * width * model + 6 * rows * width,
-    )(place, branch_low, inputs_low, end, returned, weights, stream, gain, *resid_grads)
+    )(place, rec_low, inputs_low, end, returned, w_branch, w_input, stream, gain, resid_grad)
+
+
+def gate_gradients(conv_low, pre_low, extra, heads):
+    rows, width = conv_low.shape
+    size = extra.shape[0]
+
+    def body(conv_ref, pre_ref, extra_ref, out_ref, full):
+        full[...] = mm(conv_ref[...], pre_ref[...], TN)
+        for g in range(2):
+            for h in range(heads):
+                at = h * size
+                out_ref[g * heads + h] = full[at : at + size, g * width + at : g * width + at + size]
+        out_ref[2 * heads] = extra_ref[...]
+
+    return call(
+        body,
+        (1,),
+        [whole((rows, width)), whole((rows, 2 * width)), whole((size, size))],
+        whole((2 * heads + 1, size, size)),
+        struct((2 * heads + 1, size, size), F32),
+        [pltpu.VMEM((width, 2 * width), F32)],
+        flops=4 * rows * width * width,
+        moved=6 * rows * width,
+    )(conv_low, pre_low, extra)
 
 
 def block_diagonal(blocks, width):
@@ -838,10 +927,6 @@
         jnp.pad(blocks[h], ((0, 0), (h * size, width - (h + 1) * size))) for h in range(heads)
     ]
     return jnp.pad(jnp.concatenate(rows, axis=0), ((0, width - heads * size), (0, 0)))
-
-
-def diagonal_blocks(full, heads, size):
-    return jnp.stack([full[h * size : (h + 1) * size, h * size : (h + 1) * size] for h in range(heads)])
 
 
 def shards(
@@ -896,41 +981,38 @@
     def tie(*values):
         return lax.optimization_barrier(values)
 
-    def tie_with(value, ring, running):
-        value, ring, arrays = tie(value, ring, [x for x, _ in running])
-        return value, ring, [(x, up) for x, (_, up) in zip(arrays, running)]
-
-    def halve_once(x, up, bits):
+    def halves(x, up):
         done = bits - x.shape[0].bit_length() + 1
         bit = done if up else bits - done
         mine = (my_shard >> bit) & 1
         axis = 1 if up else 0
         x = x.reshape(-1, 2, *x.shape[1:]) if up else x.reshape(2, -1, *x.shape[1:])
-        other = lax.dynamic_index_in_dim(x, 1 - mine, axis, False)
-        return add_low(lax.dynamic_index_in_dim(x, mine, axis, False), swap(other, bit))
-
-    def ring_start(x):
-        return ((x, x), (x,), ())
-
-    def ring_step(ring):
-        (right, left), rights, lefts = ring
-        right = lax.ppermute(right, "mp", [(i, i + 1) for i in range(model_count - 1)])
-        left = lax.ppermute(left, "mp", [(i + 1, i) for i in range(model_count - 1)])
-        return ((right, left), rights + (right,), lefts + (left,))
-
-    def ring_end(ring):
-        _, rights, lefts = ring
-        return [rights[0]] + [
-            jnp.where(my_model >= k, rights[k], lefts[model_count - k - 1])
-            for k in range(1, model_count)
-        ]
+        return bit, [lax.dynamic_index_in_dim(x, m, axis, False) for m in (mine, 1 - mine)]
+
+    def others(pair):
+        return [halves(x, up)[1][1] for x, up in zip(pair, (True, False))]
+
+    def send_others(pair, made):
+        return [swap(o, halves(x, up)[0]) for x, up, o in zip(pair, (True, False), made)]
+
+    def send_all(pair):
+        return send_others(pair, others(pair))
+
+    def add_all(pair, received):
+        return [add_low(halves(x, up)[1][0], r) for x, up, r in zip(pair, (True, False), received)]
 
     local_dest = lax.dynamic_slice_in_dim(destination, my_shard * row_count, row_count)
     dest_row, dest_col = local_dest.reshape(1, -1), local_dest.reshape(-1, 1)
     straight = jnp.zeros((1,), jnp.int32)
     turn = (my_shard * per_peer).astype(jnp.int32)[None]
-    arrived_tokens = exchange(send_order(straight, dest_row, dest_col, tokens), "seq")
-    sent_cot = send_order(turn, dest_row, dest_col, cotangent)
+    w_gates = jnp.concatenate(
+        [block_diagonal(w_recur, width), block_diagonal(w_ingate, width)], axis=1
+    )
+    sent_tokens, w_gates, cotangent = tie(
+        send_order(straight, dest_row, dest_col, tokens), w_gates, cotangent
+    )
+    arrived_tokens = exchange(sent_tokens, "seq")
+    cot_blocks = send_blocks(turn, dest_row, dest_col, cotangent, shard_count)
     sorted_dest = jnp.sort(destination.reshape(shard_count, row_count), axis=1)
     landing = (
         lax.dynamic_slice_in_dim(sorted_dest, my_shard * per_peer, per_peer, 1).reshape(-1)
@@ -943,6 +1025,10 @@
             for k in range(shard_count)
         ]
     ).reshape(1, -1)
+    cot_other = swap(jnp.concatenate(cot_blocks[1::2], axis=0), 0).reshape(-1, per_peer, model_width)
+    sent_cot = [
+        jnp.concatenate([cot_blocks[2 * q], cot_other[q]], axis=0) for q in range(shard_count // 2)
+    ]
     mlp_place = np.arange(row_count, dtype=np.int32).reshape(model_count, CHUNKS, sub)
     mlp_place = jnp.asarray(mlp_place.transpose(1, 0, 2).reshape(-1, 1))
     mlp_landing = (
@@ -958,10 +1044,7 @@
     )
     dist = (positions - seq_start).reshape(-1, 1)
 
-    w_rec = jnp.concatenate([pad_lanes(w_branch), pad_lanes(w_input)], axis=1)
-    w_gates = jnp.concatenate(
-        [block_diagonal(w_recur, width), block_diagonal(w_ingate, width)], axis=1
-    )
+    w_branch, w_input = w_branch.T, w_input.T
     taps = pad_lanes(conv_weight)
     bias = pad_lanes(conv_bias[None])
     decay = pad_lanes(decay_param[None])
@@ -969,15 +1052,13 @@
     gain2 = mlp_gain[None]
     half = model_width // 2
     w_out_half = jnp.pad(
-        lax.dynamic_slice_in_dim(w_out, parity * half, half, 1), ((0, width - channels), (0, 0))
+        lax.dynamic_slice_in_dim(w_out, parity * half, half, 1), ((0, -channels % 16), (0, 0))
     )
     w_near = lax.all_gather(w_out_half, "mp", axis=0)
 
-    arrived_tokens, sent_cot, w_rec, w_gates = lax.optimization_barrier(
-        (arrived_tokens, sent_cot, w_rec, w_gates)
-    )
+    arrived_tokens, w_gates, *sent_cot = tie(arrived_tokens, w_gates, *sent_cot)
     stream, hidden_near, hidden_far, branch, inputs = project(
-        place, landing_row, arrived_tokens, gain, w_rec, shard_count
+        place, landing_row, arrived_tokens, gain, w_branch, w_input, width, shard_count
     )
     halo = lax.ppermute(
         inputs[row_count - 8 :], "seq", [(i, i + 1) for i in range(shard_count - 1)]
@@ -986,35 +1067,44 @@
         inputs, halo, dist, taps, bias, decay, w_gates
     )
     pieces = lax.all_gather(tail, "seq")
-    pieces, sent_cot, w_near = tie(pieces, sent_cot, w_near)
-    cot_blocks = [sent_cot[:per_peer]]
-    for k in range(1, shard_count):
-        block = sent_cot[k * per_peer : (k + 1) * per_peer]
-        cot_blocks.append(
-            lax.ppermute(block, "seq", [(i, i ^ k) for i in range(shard_count)])
+    pieces, *sent_cot = tie(pieces, *sent_cot)
+    cot_blocks = [sent_cot[0]] + [
+        lax.ppermute(sent_cot[q], "seq", [(i, i ^ (2 * q)) for i in range(shard_count)])
+        for q in range(1, shard_count // 2)
+    ]
+    states, carry_in, *mixed = finish_states(
+        place, pieces, local, prefix, branch, model_count
+    )
+    mixed[0], w_near = tie(mixed[0], w_near)
+    w_far = swap(w_near, 0)
+
+    rows_kept, normeds = (), []
+    for c in range(CHUNKS):
+        mixed_full = exchange(mixed[c], "mp")
+        if c == 0:
+            mixed_full, *cot_blocks[1:3] = tie(mixed_full, *cot_blocks[1:3])
+        *rows_kept, normed_own = output_rows(
+            c, place, mixed_full, w_near, w_far, stream, gain2, rows_kept
         )
-    w_far = swap(w_near, 0)
-    states, mixed, carry_in = finish_states(place, pieces, local, prefix, branch, model_count)
-
-    resids, normeds = [], []
+        normeds.append(normed_own)
+    resid_own, mixed_rows = rows_kept
+    normeds[-1], *cot_blocks = tie(normeds[-1], *cot_blocks)
     upstream, upstream_near, upstream_far = place_upstream(
         place, mlp_place, turned, cot_blocks, shard_count
     )
-    for c in range(CHUNKS):
-        mixed_full = exchange(mixed[c], "mp")
-        if c == CHUNKS - 1:
-            mixed_full, upstream = tie(mixed_full, upstream)
-        resid_own, normed_own = output_rows(c, place, mixed_full, w_near, w_far, stream, gain2)
-        resids.append(resid_own)
-        normeds.append(normed_own)
     kept, grads = (), []
     for c in range(CHUNKS):
-        normed = lax.all_gather(normeds[c], "mp", axis=0, tiled=True)
+        if c == 0:
+            normed = lax.all_gather(normeds[c], "mp", axis=0, tiled=True)
+        else:
+            normed = exchange(
+                jnp.broadcast_to(normeds[c], (model_count, *normeds[c].shape)), "mp"
+            ).reshape(-1, model_width)
         *kept, grad = mlp_chunk(
-            c, place, normed, upstream, resids[c], w_gate, w_up, w_down, shard_count, kept
+            c, place, normed, upstream, resid_own, w_gate, w_up, w_down, shard_count, kept
         )
         grads.append(scatter_sum(grad, "mp", 0))
-    inner_act, gate_low, up_low, normed_near, normed_far, block_part = kept
+    inner_act, pair_low, normed_near, normed_far, block_part = kept
 
     parts = shard_count // 2
     part_width = model_width // shard_count
@@ -1028,94 +1118,69 @@
             parts, part_width, right.shape[1]
         )
 
-    far_gate = outer(normed_far, gate_low)
-    far_up = outer(normed_far, up_low)
+    def two_ways(x):
+        cut = x.shape[2] // 2
+        return [x[..., :cut], x[..., cut:]]
+
+    def finish(pair):
+        while pair[0].shape[0] > 1:
+            pair = add_all(pair, send_all(pair))
+        return jnp.concatenate([x[0] for x in pair], axis=1)
+
+    far_pair = outer(normed_far, pair_low)
     far_down = outer(upstream_far, inner_act)
-    grads[0], far_gate, far_up, far_down = tie(grads[0], far_gate, far_up, far_down)
-    far_gate, far_up, far_down = swap(far_gate, 0), swap(far_up, 0), swap(far_down, 0)
-    resid_grads, resid_lows, mixed_grads, mlp_gain_part = [], [], [], 0.0
-    for c in range(CHUNKS):
-        resid_grad, resid_low, mixed_grad_full, gain_part = resid_backward(
-            c, place, grads[c], upstream, resids[c], gain2, w_near, w_far
+    grads[0], far_pair, far_down = tie(grads[0], far_pair, far_down)
+    far_pair, far_down = swap(far_pair, 0), swap(far_down, 0)
+
+    def second_norm(c, kept):
+        return resid_backward(
+            c, place, grads[c], upstream, resid_own, gain2, w_near, w_far, width, shard_count, kept
         )
-        if c == 0:
-            mixed_grad_full, gate_low, up_low, inner_act = tie(
-                mixed_grad_full, gate_low, up_low, inner_act
-            )
-            grad_gate = with_partner(normed_near, far_gate, gate_low)
-            grad_up = with_partner(normed_near, far_up, up_low)
-            grad_down = with_partner(upstream_near, far_down, inner_act)
-            grads[1], grad_gate, grad_up, grad_down = tie(grads[1], grad_gate, grad_up, grad_down)
-        mlp_gain_part = mlp_gain_part + gain_part
-        resid_grads.append(resid_grad)
-        resid_lows.append(resid_low)
-        mixed_grads.append(exchange(mixed_grad_full, "mp"))
-    halves = (grad_down[..., : hidden_units // 2], grad_down[..., hidden_units // 2 :])
-    running = [
-        (grad_gate, True),
-        (grad_up, False),
-        (halves[0], True),
-        (halves[1], False),
-    ]
-
-    def step(entries):
-        return [(halve_once(x, up, bits), up) for x, up in entries]
-
-    mixed_grads[-1], *resid_lows = tie(mixed_grads[-1], *resid_lows)
-    ring = ring_start(jnp.stack(resid_lows))
+
+    *lows, gain_first = second_norm(0, ())
+    lows[0], pair_low = tie(lows[0], pair_low)
+    grad_pair = with_partner(normed_near, far_pair, pair_low)
+    grad_pair, inner_act = tie(grad_pair, inner_act)
+    pair = two_ways(grad_pair)
+    pair_received = send_all(pair)
+    down = two_ways(with_partner(upstream_near, far_down, inner_act))
+    grads[1], *down = tie(grads[1], *down)
+    near_low, far_low, resid_grad, mixed_grad_full, gain_second = second_norm(1, lows)
+    mlp_gain_part = gain_first + gain_second
+    mixed_grad = exchange(mixed_grad_full.reshape(row_count, width), "mp")
+    far_out = outer(far_low, mixed_rows)
+    far_out, *pair_received = tie(far_out, *pair_received)
+    pair = add_all(pair, pair_received)
+    pair_received = send_all(pair)
+    mixed_grad, far_out, block_part, *pair_received = tie(
+        mixed_grad, far_out, block_part, *pair_received
+    )
+    far_out = swap(far_out, 0)
     block_share = scatter_sum(block_part, "mp", 1)
-    local_grad, after_keep, edge_pair, mixed_grad = recurrent_back_scan(
-        mixed_grads, branch, keep, tail
-    )
+
+    local_grad, after_keep, edge_pair = recurrent_back_scan(mixed_grad, branch, keep, tail)
     back_pieces = lax.all_gather(edge_pair, "seq")
-    branch_low, inputs_part, pre_low, sums, end, edge = recurrent_backward(
+    back_pieces, *down = tie(back_pieces, *down)
+    down_received = send_all(down)
+    rec_low, inputs_part, pre_low, sums, end, edge = recurrent_backward(
         place, back_pieces, local_grad, after_keep, mixed_grad, branch, states, carry_in, pre,
         conv_low, dist, inputs, halo, taps, decay, w_gates,
     )
+    edge, far_out, near_low, *down_received = tie(edge, far_out, near_low, *down_received)
     returned = lax.ppermute(edge, "seq", [(i + 1, i) for i in range(shard_count - 1)])
-    running = step(running)
-    ring = ring_step(ring)
-    returned, ring, running = tie_with(returned, ring, running)
-    returned, block_share = tie(returned, block_share)
-    input_part, inputs_low, norm_gain_part = input_backward(
-        place, branch_low, inputs_part, end, returned, w_rec, stream, gain, resid_grads
-    )
-    ring = ring_step(ring)
-    input_part, ring, running = tie_with(input_part, ring, running)
-    for _ in range(bits - 2):
-        running = step(running)
-    for _ in range(model_count - 3):
-        ring = ring_step(ring)
+    out = two_ways(with_partner(near_low, far_out, mixed_rows))
+    out_others = others(out)
+    returned, out, out_others = tie(returned, out, out_others)
+    out_received = send_others(out, out_others)
+    input_part, rec_low, norm_gain_part = input_backward(
+        place, rec_low, inputs_part, end, returned, w_branch, w_input, stream, gain, resid_grad
+    )
+    input_part, block_share, pre_low, pair, down, pair_received, down_received, *out_received = tie(
+        input_part, block_share, pre_low, pair, down, pair_received, down_received, *out_received
+    )
     input_share = scatter_sum(input_part, "mp", 1)
-    sent_gate, sent_up, *sent_down = [x[0] for x, _ in running]
-    sent_gate, sent_up = sent_gate.astype(F32), sent_up.astype(F32)
-    sent_down = jnp.concatenate(sent_down, axis=-1).astype(F32).T
-
-    gathered = ring_end(ring)
-    mixed_near = [
-        lax.dynamic_index_in_dim(mixed, (my_model - k) % model_count, 1, False)
-        for k in range(model_count)
-    ]
-    grad_out = mm(
-        jnp.stack(mixed_near).reshape(row_count, width),
-        jnp.stack(gathered).reshape(row_count, model_width),
-        TN,
-    ).astype(BF16)
-    sent_out = scatter_sum(grad_out, "seq", 1)
-    grad_gates = mm(conv_low, pre_low, TN)
-    rec_low = jnp.concatenate([branch_low, inputs_low], axis=1)
-    grad_rec = with_partner(hidden_near, swap(outer(hidden_far, rec_low), 0), rec_low)
-    running = [(grad_rec[..., :width], True), (grad_rec[..., width:], False)]
-    for _ in range(bits - 1):
-        running = step(running)
-    sent_branch, sent_input = [x[0] for x, _ in running]
-    sent_branch = sent_branch[:, :channels].astype(F32)
-    sent_input = sent_input[:, :channels].astype(F32)
-    all_rows = jnp.arange(row_count, dtype=jnp.int32)[None]
-    home_block = exchange(place_rows(mlp_landing.reshape(-1, 1), all_rows, block_share), "seq")
-    input_share, sent_branch, sent_input, home_block, sent_gate, sent_up, sent_down = tie(
-        input_share, sent_branch, sent_input, home_block, sent_gate, sent_up, sent_down
-    )
+
+    far_rec = swap(outer(hidden_far, rec_low), 0)
 
     sums = jnp.sum(sums.reshape(CONV + 2, 8, width), axis=1)[:, :channels]
     sums = jnp.concatenate(
@@ -1131,20 +1196,33 @@
         [sums.reshape(sum_rows, block_width), gains.reshape(gain_rows, block_width)], axis=0
     )
     extra = jnp.pad(extra, ((0, block_width - sum_rows - gain_rows), (0, 0)))
-    small = jnp.concatenate(
-        [
-            diagonal_blocks(grad_gates[:, :width], heads, block_width),
-            diagonal_blocks(grad_gates[:, width:], heads, block_width),
-            extra[None],
-        ],
-        axis=0,
-    )
+    small = gate_gradients(conv_low, pre_low, extra, heads)
+    small, hidden_near = tie(small, hidden_near)
     small = lax.psum(small, "seq")
-    input_share, small, sent_out = tie(input_share, small, sent_out)
-    sent_out = sent_out[:channels].astype(F32)
     sums = small[2 * heads, :sum_rows].reshape(CONV + 2, channels)
     gains = small[2 * heads, sum_rows : sum_rows + gain_rows].reshape(-1)
     gains = gains[: 2 * slab_width].reshape(2, slab_width)
+
+    out = add_all(out, out_received)
+    grad_rec = with_partner(hidden_near, far_rec, rec_low)
+    block_share, grad_rec = tie(block_share, grad_rec)
+    sent_rec = finish(two_ways(grad_rec))
+    sent_out = finish(out)
+    sent_branch = sent_rec[:, :channels].astype(F32)
+    sent_input = sent_rec[:, width : width + channels].astype(F32)
+    all_rows = jnp.arange(row_count, dtype=jnp.int32)[None]
+    home_block = exchange(place_rows(mlp_landing.reshape(-1, 1), all_rows, block_share), "seq")
+    sent_pair = finish(add_all(pair, pair_received))
+    sent_down = finish(add_all(down, down_received)).astype(F32).T
+    unit = mlp_tile(hidden_units)
+    sent_pair = sent_pair.reshape(part_width, hidden_units // unit, 2, unit)
+    sent_gate = sent_pair[:, :, 0].reshape(part_width, hidden_units).astype(F32)
+    sent_up = sent_pair[:, :, 1].reshape(part_width, hidden_units).astype(F32)
+    input_share, home_block, sent_gate, sent_up, sent_down = tie(
+        input_share, home_block, sent_gate, sent_up, sent_down
+    )
+    sent_out = scatter_sum(sent_out, "mp", 1)
+    sent_out = sent_out[:, :channels].astype(F32).T
 
     home_input = exchange(place_rows(landing.reshape(-1, 1), all_rows, input_share), "seq")
     block_out = restore_rows(dest_row, dest_col, home_block)

time: 784 us -> 700 us (0.89)
  waiting for transfers between devices: 223 us -> 167 us
  blocking collectives: 46.3 us -> 22.4 us
  starting transfers between devices: 70.4 us -> 62.3 us
    ppermute x13 -> x3, waiting for transfers between devices: 77.4 us -> 23.3 us  [shards(): lax.ppermute(sent_cot[q], 'seq', [(i, i ^ 2 * q) for i in range(shard_cou...]
    ppermute x17 -> x22, waiting for transfers between devices: 41.4 us -> 67.2 us  [swap(): lax.ppermute(x, 'seq', [(i, i ^ 1 << bit) for i in range(shard_count)])]
    all_to_all x1 -> x0, blocking collectives: 24.1 us -> none  [exchange(): return lax.all_to_all(x, axis, split_axis=0, concat_axis=0, tiled=True)]
    ppermute x13 -> x3, starting transfers between devices: 21.6 us -> 3.47 us  [shards(): lax.ppermute(sent_cot[q], 'seq', [(i, i ^ 2 * q) for i in range(shard_cou...]
    pallas_call x7 -> x9, Pallas kernels: 115 us -> 131 us  [the longest x2 66 us: mlp_chunk(): call(body, (steps,), [whole((rows, model)), rows_of, pl.BlockSpec((sub, m...]
    all_gather x2 -> x1, waiting for transfers between devices: 13.8 us -> 0.03 us  [shards(): normed = lax.all_gather(normeds[c], 'mp', axis=0, tiled=True)]
    pallas_call x2 -> x1, Pallas kernels: 17.9 us -> 8.94 us  [send_order(): call(body, (rows // tile,), [whole((1, rows)), whole((rows, 1)), whole((r...]
    another operation x5 -> x0, local copies, waits for them, and re-layouts: 8.39 us -> none  [shards(): jnp.stack(mixed_near).reshape(row_count, width)]
  transfers between devices with their start and end apart: 48 -> 43, of which waited for: 19 -> 16; matrix products, arithmetic and copies ran while one was open for 21% -> 23% of each run, Pallas kernels for 29% -> 33%
where the time goes in v2:
time: 700 us; the launch traced here: 689 us
  Pallas kernels  247 us (35%)
  waiting for transfers between devices  167 us (24%)
  local copies, waits for them, and re-layouts  74.5 us (11%)
  starting transfers between devices  62.3 us (9%)
  matrix products  58.8 us (8%)
  other arithmetic  39.8 us (6%)
  blocking collectives  22.4 us (3%)
  between operations  16.8 us (2%)
    all_to_all x8, waiting for transfers between devices, exchange(): return lax.all_to_all(x, axis, split_axis=0, concat_axis=0, tiled=True)  71.1 us
    ppermute x22, waiting for transfers between devices, swap(): lax.ppermute(x, 'seq', [(i, i ^ 1 << bit) for i in range(shard_count)])  67.2 us
    pallas_call x2, Pallas kernels, mlp_chunk(): call(body, (steps,), [whole((rows, model)), rows_of, pl.BlockSpec((sub, m...  66 us
    dot_general x8, matrix products, mm(): return lax.dot_general(left, right, dims, preferred_element_type=F32)  58.8 us
    all_to_all x8, starting transfers between devices, exchange(): return lax.all_to_all(x, axis, split_axis=0, concat_axis=0, tiled=True)  35.5 us
    unnamed x131, local copies, waits for them, and re-layouts  25.5 us
    ppermute x3, waiting for transfers between devices, shards(): lax.ppermute(sent_cot[q], 'seq', [(i, i ^ 2 * q) for i in range(shard_cou...  23.3 us
    pallas_call x1, Pallas kernels, recurrent_backward(): call(body, (tiles_n,), [whole(pieces.shape), tiles, tiles, tiles, tiles,...  20.2 us
  transfers between devices with their start and end apart: 43, of which 16 were waited for; matrix products, arithmetic and copies ran while one was open for 23% of the time, Pallas kernels for 33%

profile of v2, /device:TPU:0, one launch (start us, length us, event | category | flops | bytes accessed | tf_op | source)
XLA Modules:
  0.0 688.6 jit_solution(17545476211183578688)
XLA Ops:
  16.1 8.9 %shard_map.298 = bf16[1024,2048]{1,0:T(8,128)(2,1)} custom-call(s32[1]{0:T(128)} %constant.187.clone.1.turn_ref, s32[1,1024]{1,0:T(1,128)} %bitcast.190, s32[1024,1]{1,0:T(8,128)} %copy.179.col_ref, bf16[1024,2048]{1,0:T(8,128)(2,1)} %val_ref.1), custom_call_target="tpu_custom_call" | custom-call | flops 4294967296 | bytes 8388608 | tf_op jit(solution)/shard_map/pallas_call | solution.py:103
  25.0 5.2 all-to-all-start
  30.2 11.5 %shard_map.299 = (bf16[128,2048]{1,0:T(8,128)(2,1)}, bf16[128,2048]{1,0:T(8,128)(2,1)}, bf16[128,2048]{1,0:T(8,128)(2,1)}, bf16[128,2048]{1,0:T(8,128)(2,1)}, bf...) custom-call(s32[1]{0:T(128)} %bitcast.16.turn_ref, ...), custom_call_target="tpu_custom_call" | custom-call | flops 4294967296 | bytes 8388608 | tf_op jit(solution)/shard_map/pallas_call | solution.py:138
  41.7 3.1 pad_maximum_fusion
  53.7 25.7 %all-to-all-done = bf16[8,128,2048]{2,1,0:T(8,128)(2,1)} async-done(((bf16[8,128,2048]{2,1,0:T(8,128)(2,1)}), bf16[8,128,2048]{2,1,0:T(8,128)(2,1)}, u32[]{:S(2)}, u32[]{:S(2)}) %all-to-all-start) | async-done | bytes 4194336 | tf_op jit(solution)/shard_map/all_to_all | solution.py:973
  79.4 18.3 %shard_map.300 = (bf16[1024,2048]{1,0:T(8,128)(2,1)}, bf16[1024,1024]{1,0:T(8,128)(2,1)}, bf16[1024,1024]{1,0:T(8,128)(2,1)}, f32[1024,768]{1,0:T(8,128)}, f32[1024,768]{1,0:T(8,128)}) custom-call(s32[3]{0:T(128)} %pad_add_fusion.my_ref.place_ref, s32[1,1024]{1,0:T(1,128)} %bitcast.187, bf16[1024,2048]{1,0:T(8,128)(2,1)} %bitcast.15.arr_ref, ...), custom_call_target="tpu_custom_call" | custom-call | flops 10737418240 | bytes 25165824 | tf_op jit(solution)/shard_map/pallas_call | solution.py:267
  103.0 13.3 %shard_map.301 = (bf16[1024,768]{1,0:T(8,128)(2,1)}, f32[1024,1536]{1,0:T(8,128)}, f32[1024,768]{1,0:T(8,128)}, f32[1024,768]{1,0:T(8,128)}, f32[1024,768]{1,0:T(8,128)}, /*index=5*/f32[8,768]{1,0:T(8,128)}) custom-call(f32[1024,768]{1,0:T(8,128)} %get-tuple-element.170.in_ref.in_before_ref, f32[8,768]{1,0:T(8,128)} %copy-done.45, ...), custom_call_target="tpu_custom_call" | custom-call | flops 2573205504 | bytes 23592960 | tf_op jit(solution)/shard_map/pallas_call | solution.py:367
  116.3 11.5 %all-gather = f32[64,768]{1,0:T(8,128)} all-gather(f32[8,768]{1,0:T(8,128)} %get-tuple-element.172.tail_ref), channel_id=2, replica_groups=mesh['seq'=8,'mp'=4] {'seq'}, dimensions={0}, use_global_device_ids=true | all-gather | bytes 221184 | tf_op jit(solution)/shard_map/all_gather | solution.py:1069
  127.9 9.4 %shard_map.302 = (f32[1024,768]{1,0:T(8,128)}, f32[8,768]{1,0:T(8,128)}, bf16[4,128,768]{2,1,0:T(8,128)(2,1)}, bf16[4,128,768]{2,1,0:T(8,128)(2,1)}) custom-call(s32[3]{0:T(128)} %pad_add_fusion.my_ref.place_ref, f32[8,8,768]{2,1,0:T(8,128)} %bitcast.181, f32[1024,768]{1,0:T(8,128)} %get-tuple-element.178.local_ref, ...), custom_call_target="tpu_custom_call" | custom-call | flops 47185920 | bytes 14155776 | tf_op jit(solution)/shard_map/pallas_call | solution.py:428
  137.8 5.6 all-to-all-start.2
  145.4 23.1 %collective-permute-done.3.refs_1_ = bf16[256,2048]{1,0:T(8,128)(2,1)S(1)} collective-permute-done((bf16[256,2048]{1,0:T(8,128)(2,1)}, bf16[256,2048]{1,0:T(8,128)(2,1)S(1)}, u32[]{:S(2)}, u32[]{:S(2)}) %collective-permute-start.3) | collective-permute-done | bytes 1048608 | tf_op jit(solution)/shard_map/ppermute | solution.py:1072
  170.6 8.8 %shard_map.303 = (f32[256,2048]{1,0:T(8,128)}, bf16[256,3072]{1,0:T(8,128)(2,1)}, bf16[128,2048]{1,0:T(8,128)(2,1)}) custom-call(s32[3]{0:T(128)} %pad_add_fusion.my_ref.place_ref, bf16[4,128,768]{2,1,0:T(8,128)(2,1)} %copy-done.22, bf16[4,688,1024]{2,1,0:T(8,128)(2,1)} %bitcast.148, bf16[4,688,1024]{2,1,0:T(8,128)(2,1)} %collective-permute-done.2.far_ref, ...), custom_call_target="tpu_custom_call" | custom-call | flops 1610612736 | bytes 14680064 | tf_op jit(solution)/shard_map/pallas_call | solution.py:474
  179.4 4.8 all-to-all-start.1
  185.7 36.2 %all-to-all-done.1.mixed_ref = bf16[4,128,768]{2,1,0:T(8,128)(2,1)S(1)} async-done(((bf16[4,128,768]{2,1,0:T(8,128)(2,1)}), bf16[4,128,768]{2,1,0:T(8,128)(2,1)S(1)}, u32[]{:S(2)}, u32[]{:S(2)}) %all-to-all-start.1) | async-done | bytes 786464 | tf_op jit(solution)/shard_map/all_to_all | solution.py:973
  222.7 8.8 %shard_map.304 = (f32[256,2048]{1,0:T(8,128)}, bf16[256,3072]{1,0:T(8,128)(2,1)}, bf16[128,2048]{1,0:T(8,128)(2,1)}) custom-call(s32[3]{0:T(128)} %pad_add_fusion.my_ref.place_ref, bf16[4,128,768]{2,1,0:T(8,128)(2,1)} %copy-done.28, bf16[4,688,1024]{2,1,0:T(8,128)(2,1)} %bitcast.149, ...), custom_call_target="tpu_custom_call", output_to_operand_aliasing={{0}: (6, {}), {1}: (7, {})} | custom-call | flops 1610612736 | bytes 14680064 | tf_op jit(solution)/shard_map/pallas_call | solution.py:474
  231.5 2.6 broadcast_in_dim.42
  234.2 4.4 all-to-all-start.3
  239.3 10.4 %shard_map.305 = (bf16[1024,2048]{1,0:T(8,128)(2,1)}, bf16[1024,1024]{1,0:T(8,128)(2,1)}, bf16[1024,1024]{1,0:T(8,128)(2,1)}) custom-call(s32[3]{0:T(128)} %pad_add_fusion.my_ref.place_ref, s32[1024,1]{1,0:T(8,128)} %constant.205.clone.place_ref, s32[1,1024]{1,0:T(1,128)} %bitcast.197, bf16[256,2048]{1,0:T(8,128)(2,1)} %pad_maximum_fusion.2.refs_0_, ...), custom_call_target="tpu_custom_call" | custom-call | flops 4294967296 | bytes 12582912 | tf_op jit(solution)/shard_map/pallas_call | solution.py:203
  249.7 33.2 %shard_map.306 = (bf16[1024,1536]{1,0:T(8,128)(2,1)}, bf16[1024,3072]{1,0:T(8,128)(2,1)}, bf16[1024,1024]{1,0:T(8,128)(2,1)}, bf16[1024,1024]{1,0:T(8,128)(2,1)}...) custom-call(s32[3]{0:T(128)} %pad_add_fusion.my_ref.place_ref, ...), custom_call_target="tpu_custom_call" | custom-call | flops 19327352832 | bytes 29360128 | tf_op jit(solution)/shard_map/pallas_call | solution.py:553
  284.8 32.8 %shard_map.307 = (bf16[1024,1536]{1,0:T(8,128)(2,1)}, bf16[1024,3072]{1,0:T(8,128)(2,1)}, bf16[1024,1024]{1,0:T(8,128)(2,1)}, bf16[1024,1024]{1,0:T(8,128)(2,1)}...) custom-call(s32[3]{0:T(128)} %pad_add_fusion.my_ref.place_ref, ...), custom_call_target="tpu_custom_call", output_to_operand_aliasing={{0}: (7, {}), {1}: (8, {}), {2}: (9, {}), {3}: (10, {}), {4... | custom-call | flops 19327352832 | bytes 29360128 | tf_op jit(solution)/shard_map/pallas_call | solution.py:553
  317.6 7.8 %convolution_convert_fusion.3 = bf16[1024,1536]{1,0:T(8,128)(2,1)} fusion(bf16[1024,1024]{1,0:T(8,128)(2,1)} %get-tuple-element.215, bf16[1024,1536]{1,0:T(8,128)(2,1)} %get-tuple-element.221), kind=kOutput, calls=%fused_computation.11 | convolution fusion | flops 3222798336 | bytes 8388608 | tf_op jit(solution)/shard_map/dot_general | solution.py:30
  325.4 8.7 %convolution_convert_fusion.1 = bf16[1024,3072]{1,0:T(8,128)(2,1)} fusion(bf16[1024,1024]{1,0:T(8,128)(2,1)S(1)} %copy-done.59, bf16[1024,3072]{1,0:T(8,128)(2,1)S(1)} %copy-done.56), kind=kOutput, calls=%fused_computation.5 | convolution fusion | flops 6445596672 | bytes 14680064 | tf_op jit(solution)/shard_map/dot_general | solution.py:30
  334.2 10.3 %shard_map.308 = (bf16[256,1024]{1,0:T(8,128)(2,1)}, bf16[256,1024]{1,0:T(8,128)(2,1)}, f32[256,2048]{1,0:T(8,128)}, bf16[4,256,768]{2,1,0:T(8,128)(2,1)}, f32[1,2048]{1,0:T(1,128)}) custom-call(s32[3]{0:T(128)} %pad_add_fusion.my_ref.place_ref, bf16[128,2048]{1,0:T(8,128)(2,1)} %reduce-scatter.8.cloned.1.call-done.g_ref, ...), custom_call_target="tpu_custom_call" | custom-call | flops 1610612736 | bytes 16252928 | tf_op jit(solution)/shard_map/pallas_call | solution.py:621
  345.0 10.8 %add_convert_fusion.1 = bf16[1024,3072]{1,0:T(8,128)(2,1)S(1)} fusion(bf16[1024,3072]{1,0:T(8,128)(2,1)} %collective-permute-done.6, bf16[1024,1024]{1,0:T(8,128)(2,1)S(1)} %copy-done.57, bf16[1024,3072]{1,0:T(8,128)(2,1)} %get-tuple-element.219), kind=kOutput, calls=%fused_computation.1 | convolution fusion | flops 6451888128 | bytes 20971520 | tf_op jit(solution)/shard_map/dot_general | solution.py:30
  355.8 2.3 fusion.45
  359.5 2.6 copy.169
  363.2 2.7 dynamic-slice_bitcast_fusion.2
  366.0 5.9 add_convert_fusion.3
  373.8 4.3 reduce-scatter.6.cloned.1.call-done.g_ref
  379.6 9.7 %shard_map.309 = (bf16[256,1024]{1,0:T(8,128)(2,1)}, bf16[256,1024]{1,0:T(8,128)(2,1)}, f32[256,2048]{1,0:T(8,128)}, bf16[4,256,768]{2,1,0:T(8,128)(2,1)}, f32[1,2048]{1,0:T(1,128)}) custom-call(s32[3]{0:T(128)} %pad_add_fusion.my_ref.place_ref, ...), custom_call_target="tpu_custom_call", output_to_operand_aliasing={{0}: (7, {}), {1}: (8, {}), {2}: (9, {}), {3}: (10, {})} | custom-call | flops 1610612736 | bytes 16252928 | tf_op jit(solution)/shard_map/pallas_call | solution.py:621
  389.4 3.7 all-to-all-start.4
  393.4 6.1 convolution_convert_fusion
  399.4 3.0 collective-permute-done.8
  409.2 14.6 %collective-permute-done.11 = bf16[1,256,1536]{1,2,0:T(8,128)(2,1)S(1)} collective-permute-done((bf16[1,256,1536]{1,2,0:T(8,128)(2,1)S(1)}, bf16[1,256,1536]{1,2,0:T(8,128)(2,1)S(1)}, u32[]{:S(2)}, u32[]{:S(2)}) %collective-permute-start.11) | collective-permute-done | bytes 786464 | tf_op jit(solution)/shard_map/ppermute | solution.py:976
  423.9 2.3 collective-permute-done.10
  426.2 3.7 all-to-all-done.4
  431.0 8.9 %shard_map.310 = (f32[1024,768]{1,0:T(8,128)}, f32[1024,768]{1,0:T(8,128)}, f32[8,768]{1,0:T(8,128)}) custom-call(bf16[1024,768]{1,0:T(8,128)(2,1)} %bitcast.153, f32[1024,768]{1,0:T(8,128)} %get-tuple-element.180.branch_ref, f32[1024,768]{1,0:T(8,128)} %get-tuple-element.237.keep_ref, f32[8,768]{1,0:T(8,128)} %get-tuple-element.172.tail_ref), custom_call_target="tpu_custom_call" | custom-call | flops 78643200 | bytes 14155776 | tf_op jit(solution)/shard_map/pallas_call | solution.py:692
  440.0 10.9 %all-gather.2 = f32[64,768]{1,0:T(8,128)} all-gather(f32[8,768]{1,0:T(8,128)} %get-tuple-element.238), channel_id=4, replica_groups=mesh['seq'=8,'mp'=4] {'seq'}, dimensions={0}, use_global_device_ids=true | all-gather | bytes 221184 | tf_op jit(solution)/shard_map/all_gather | solution.py:1162
  450.9 2.1 dynamic-slice_bitcast_fusion.5
  455.9 20.2 %shard_map.311 = (bf16[1024,1536]{1,0:T(8,128)(2,1)}, bf16[1024,768]{1,0:T(8,128)(2,1)}, bf16[1024,1536]{1,0:T(8,128)(2,1)}, f32[48,768]{1,0:T(8,128)}, f32[8,768]{1,0:T(8,128)}, /*index=5*/f32[8,768]{1,0:T(8,128)}) custom-call(s32[3]{0:T(128)} %pad_add_fusion.my_ref.place_ref, f32[8,8,768]{2,1,0:T(8,128)} %bitcast.179, ...), custom_call_target="tpu_custom_call" | custom-call | flops 2651848704 | bytes 31457280 | tf_op jit(solution)/shard_map/pallas_call | solution.py:803
  477.8 4.6 add_convert_fusion
  486.7 2.0 collective-permute-start.16
  489.6 15.8 %shard_map.312 = (bf16[1024,2048]{1,0:T(8,128)(2,1)}, bf16[1024,1536]{1,0:T(8,128)(2,1)}, f32[1,2048]{1,0:T(1,128)}) custom-call(s32[3]{0:T(128)} %pad_add_fusion.my_ref.place_ref, bf16[1024,1536]{1,0:T(8,128)(2,1)} %get-tuple-element.248.bl_ref, bf16[1024,768]{1,0:T(8,128)(2,1)} %get-tuple-element.249.il_ref, ...), custom_call_target="tpu_custom_call", output_to_operand_aliasing={{1}: (1, {})} | custom-call | flops 6505365504 | bytes 19398656 | tf_op jit(solution)/shard_map/pallas_call | solution.py:884
  506.6 3.3 all-to-all-start.5
  510.0 5.4 all-to-all-done.5
  516.3 7.8 %collective-permute-done.16 = bf16[2,256,1536]{2,1,0:T(8,128)(2,1)} collective-permute-done((bf16[2,256,1536]{2,1,0:T(8,128)(2,1)}, bf16[2,256,1536]{2,1,0:T(8,128)(2,1)}, u32[]{:S(2)}, u32[]{:S(2)}) %collective-permute-start.16) | collective-permute-done | bytes 1572896 | tf_op jit(solution)/shard_map/ppermute | solution.py:976
  524.8 6.9 %shard_map.313 = f32[9,171,171]{2,1,0:T(8,128)} custom-call(bf16[1024,768]{1,0:T(8,128)(2,1)} %get-tuple-element.247.conv_ref, bf16[1024,1536]{1,0:T(8,128)(2,1)} %get-tuple-element.272.pre_ref, f32[171,171]{1,0:T(8,128)} %select_maximum_fusion.extra_ref), custom_call_target="tpu_custom_call" | custom-call | flops 2415919104 | bytes 4718592 | tf_op jit(solution)/shard_map/pallas_call | solution.py:912
  534.6 7.8 %convolution_convert_fusion.2 = bf16[1024,1536]{1,0:T(8,128)(2,1)} fusion(bf16[1024,1024]{1,0:T(8,128)(2,1)} %get-tuple-element.280, bf16[1024,1536]{1,0:T(8,128)(2,1)} %get-tuple-element.279), kind=kOutput, calls=%fused_computation.10 | convolution fusion | flops 3222798336 | bytes 8388608 | tf_op jit(solution)/shard_map/dot_general | solution.py:30
  559.8 18.7 %collective-permute-done.19 = bf16[1,256,768]{2,1,0:T(8,128)(2,1)S(1)} collective-permute-done((bf16[1,256,768]{2,1,0:T(8,128)(2,1)S(1)}, bf16[1,256,768]{2,1,0:T(8,128)(2,1)S(1)}, u32[]{:S(2)}, u32[]{:S(2)}) %collective-permute-start.19) | collective-permute-done | bytes 393248 | tf_op jit(solution)/shard_map/ppermute | solution.py:976
  578.6 2.6 collective-permute-done.20
  587.7 7.1 %add_convert_fusion.2 = bf16[1024,1536]{1,0:T(8,128)(2,1)S(1)} fusion(bf16[1024,1536]{1,0:T(8,128)(2,1)} %collective-permute-done.18, bf16[1024,1024]{1,0:T(8,128)(2,1)} %get-tuple-element.278, bf16[1024,1536]{1,0:T(8,128)(2,1)} %get-tuple-element.279), kind=kOutput, calls=%fused_computation.2 | convolution fusion | flops 3225944064 | bytes 11534336 | tf_op jit(solution)/shard_map/dot_general | solution.py:30
  597.9 2.4 fusion.50
  600.3 2.6 constant_dynamic-slice_fusion.4
  602.8 2.3 copy.183
  607.2 2.4 copy.185
  616.8 4.6 shard_map.314
  621.4 4.2 all-to-all-start.6
  632.7 15.8 %collective-permute-done.22 = bf16[1,256,768]{2,1,0:T(8,128)(2,1)S(1)} collective-permute-done((bf16[1,256,768]{2,1,0:T(8,128)(2,1)S(1)}, bf16[1,256,768]{2,1,0:T(8,128)(2,1)S(1)}, u32[]{:S(2)}, u32[]{:S(2)}) %collective-permute-start.22) | collective-permute-done | bytes 393248 | tf_op jit(solution)/shard_map/ppermute | solution.py:976
  649.2 4.6 shard_map.316
  653.8 4.3 all-to-all-start.7
  662.4 3.0 copy.188
  667.1 3.0 copy.190
  670.1 5.5 shard_map.315
  675.6 5.4 shard_map.317
  (300 shorter events, 111.4 us)
Async XLA Ops:
  8.0 38.3 %sort.10.cloned.1.call-start = ((), (), s32[]{:S(2)}) async-start(), calls=%async_computation.21 | async-start | bytes 98336 | tf_op jit(solution)/shard_map/jit(sort)/sort | solution.py:1016
  9.6 127.7 %all-gather.8.cloned.1.call-start = ((), (), s32[]{:S(2)}) async-start(), calls=%async_computation.20 | async-start | bytes 7045120 | tf_op jit(solution)/shard_map/all_gather | solution.py:1057
  25.0 54.4 %all-to-all-start = ((bf16[8,128,2048]{2,1,0:T(8,128)(2,1)}), bf16[8,128,2048]{2,1,0:T(8,128)(2,1)}, u32[]{:S(2)}, u32[]{:S(2)}) async-start(bf16[8,128,2048]{2,1,0:T(8,128)(2,1)} %bitcast.170), calls=%async_computation | async-start | bytes 8388608 | tf_op jit(solution)/shard_map/all_to_all | solution.py:973
  44.8 4.5 collective-permute-start
  79.4 21.2 %copy-start.47 = (f32[684]{0:T(1024)S(1)}, f32[684]{0:T(1024)}, u32[]{:S(2)}) copy-start(f32[684]{0:T(1024)} %param.30) | copy-start | bytes 8212
  79.4 21.2 %copy-start.48 = (f32[4,684]{1,0:T(4,128)S(1)}, f32[4,684]{1,0:T(4,128)}, u32[]{:S(2)}) copy-start(f32[4,684]{1,0:T(4,128)} %param.26) | copy-start | bytes 32836
  79.4 22.4 %copy-start.51 = (f32[684]{0:T(1024)S(1)}, f32[684]{0:T(1024)}, u32[]{:S(2)}) copy-start(f32[684]{0:T(1024)} %param.27) | copy-start | bytes 8212
  98.5 3.9 collective-permute-start.1
  137.3 32.3 %collective-permute-start.2 = (bf16[4,688,1024]{2,1,0:T(8,128)(2,1)}, bf16[4,688,1024]{2,1,0:T(8,128)(2,1)}, u32[]{:S(2)}, u32[]{:S(2)}) collective-permute-start(bf16[4,688,1024]{2,1,0:T(8,128)(2,1)} %bitcast.147), channel_id=1, source_target_pairs={{0,4},{4,0},{8,12},{12,8},{16,20},{20,16},{24,28},{28,24},{1,5},{5... | collective-permute-start | bytes 16908296 | tf_op jit(solution)/shard_map/ppermute | solution.py:976
  137.8 31.9 %all-to-all-start.2 = ((bf16[4,128,768]{2,1,0:T(8,128)(2,1)}), bf16[4,128,768]{2,1,0:T(8,128)(2,1)S(1)}, u32[]{:S(2)}, u32[]{:S(2)}) async-start(bf16[4,128,768]{2,1,0:T(8,128)(2,1)} %get-tuple-element.185), calls=%async_computation.2 | async-start | bytes 1572864 | tf_op jit(solution)/shard_map/all_to_all | solution.py:973
  143.4 106.4 %all-gather.6.cloned.1.call-start = ((), (), s32[]{:S(2)}) async-start(), calls=%async_computation.13 | async-start | bytes 2621440 | tf_op jit(solution)/shard_map/all_gather | solution.py:1098
  143.4 25.2 %collective-permute-start.3 = (bf16[256,2048]{1,0:T(8,128)(2,1)}, bf16[256,2048]{1,0:T(8,128)(2,1)S(1)}, u32[]{:S(2)}, u32[]{:S(2)}) collective-permute-start(bf16[256,2048]{1,0:T(8,128)(2,1)} %pad_maximum_fusion.3), channel_id=1, source_target_pairs={{0,8},{4,12},{8,0},{12,4},{16,24},{20,28},{24,16},{28,20},{1,9},{5... | collective-permute-start | bytes 3145736 | tf_op jit(solution)/shard_map/ppermute | solution.py:1072
  144.7 25.0 %collective-permute-start.4 = (bf16[256,2048]{1,0:T(8,128)(2,1)}, bf16[256,2048]{1,0:T(8,128)(2,1)}, u32[]{:S(2)}, u32[]{:S(2)}) collective-permute-start(bf16[256,2048]{1,0:T(8,128)(2,1)} %pad_maximum_fusion.4), channel_id=1, source_target_pairs={{0,16},{4,20},{8,24},{12,28},{16,0},{20,4},{24,8},{28,12},{1,17},{... | collective-permute-start | bytes 3145736 | tf_op jit(solution)/shard_map/ppermute | solution.py:1072
  179.4 42.5 %all-to-all-start.1 = ((bf16[4,128,768]{2,1,0:T(8,128)(2,1)}), bf16[4,128,768]{2,1,0:T(8,128)(2,1)S(1)}, u32[]{:S(2)}, u32[]{:S(2)}) async-start(bf16[4,128,768]{2,1,0:T(8,128)(2,1)} %get-tuple-element.181), calls=%async_computation.1 | async-start | bytes 1572864 | tf_op jit(solution)/shard_map/all_to_all | solution.py:973
  184.2 47.3 %collective-permute-start.5 = (bf16[256,2048]{1,0:T(8,128)(2,1)S(1)}, bf16[256,2048]{1,0:T(8,128)(2,1)}, u32[]{:S(2)}, u32[]{:S(2)}) collective-permute-start(bf16[256,2048]{1,0:T(8,128)(2,1)S(1)} %pad_maximum_fusion.5), channel_id=1, source_target_pairs={{0,24},{4,28},{8,16},{12,20},{16,8},{20,12},{24,0},{28,4},{1,25},{... | collective-permute-start | bytes 3145736 | tf_op jit(solution)/shard_map/ppermute | solution.py:1072
  234.2 49.2 %all-to-all-start.3 = ((bf16[4,128,2048]{2,1,0:T(8,128)(2,1)}), bf16[4,128,2048]{2,1,0:T(8,128)(2,1)S(1)}, u32[]{:S(2)}, u32[]{:S(2)}) async-start(bf16[4,128,2048]{2,1,0:T(8,128)(2,1)} %broadcast_in_dim.42), calls=%async_computation.3 | async-start | bytes 4194304 | tf_op jit(solution)/shard_map/all_to_all | solution.py:973
  238.6 95.6 %reduce-scatter.8.cloned.1.call-start = ((), (), s32[]{:S(2)}) async-start(), calls=%async_computation.15 | async-start | bytes 2621440 | tf_op jit(solution)/shard_map/reduce_scatter | solution.py:970
  283.0 95.1 %reduce-scatter.6.cloned.1.call-start = ((), (), s32[]{:S(2)}) async-start(), calls=%async_computation.14 | async-start | bytes 2621440 | tf_op jit(solution)/shard_map/reduce_scatter | solution.py:970
  317.6 7.8 %copy-start.56 = (bf16[1024,3072]{1,0:T(8,128)(2,1)S(1)}, bf16[1024,3072]{1,0:T(8,128)(2,1)}, u32[]{:S(2)}) copy-start(bf16[1024,3072]{1,0:T(8,128)(2,1)} %get-tuple-element.219) | copy-start | bytes 18874372
  317.6 7.8 %copy-start.59 = (bf16[1024,1024]{1,0:T(8,128)(2,1)S(1)}, bf16[1024,1024]{1,0:T(8,128)(2,1)}, u32[]{:S(2)}) copy-start(bf16[1024,1024]{1,0:T(8,128)(2,1)} %get-tuple-element.213) | copy-start | bytes 6291460
  334.2 10.8 %collective-permute-start.6 = (bf16[1024,3072]{1,0:T(8,128)(2,1)}, bf16[1024,3072]{1,0:T(8,128)(2,1)}, u32[]{:S(2)}, u32[]{:S(2)}) collective-permute-start(bf16[1024,3072]{1,0:T(8,128)(2,1)} %convolution_convert_fusion.1), channel_id=1, source_target_pairs={{0,4},{4,0},{8,12},{12,8},{16,20},{20,16},{24,28},{28,24},{1,5},{5... | collective-permute-start | bytes 18874376 | tf_op jit(solution)/shard_map/ppermute | solution.py:976
  334.2 10.8 %copy-start.57 = (bf16[1024,1024]{1,0:T(8,128)(2,1)S(1)}, bf16[1024,1024]{1,0:T(8,128)(2,1)}, u32[]{:S(2)}) copy-start(bf16[1024,1024]{1,0:T(8,128)(2,1)} %get-tuple-element.211) | copy-start | bytes 6291460
  344.5 21.5 %collective-permute-start.7 = (bf16[1024,1536]{1,0:T(8,128)(2,1)}, bf16[1024,1536]{1,0:T(8,128)(2,1)}, u32[]{:S(2)}, u32[]{:S(2)}) collective-permute-start(bf16[1024,1536]{1,0:T(8,128)(2,1)} %convolution_convert_fusion.3), channel_id=1, source_target_pairs={{0,4},{4,0},{8,12},{12,8},{16,20},{20,16},{24,28},{28,24},{1,5},{5... | collective-permute-start | bytes 9437192 | tf_op jit(solution)/shard_map/ppermute | solution.py:976
  362.1 37.4 %collective-permute-start.9 = (bf16[2,256,1536]{1,2,0:T(8,128)(2,1)}, bf16[2,256,1536]{1,2,0:T(8,128)(2,1)}, u32[]{:S(2)}, u32[]{:S(2)}) collective-permute-start(bf16[2,256,1536]{1,2,0:T(8,128)(2,1)} %bitcast.176), channel_id=1, source_target_pairs={{0,16},{4,20},{8,24},{12,28},{16,0},{20,4},{24,8},{28,12},{1,17},{... | collective-permute-start | bytes 4718600 | tf_op jit(solution)/shard_map/ppermute | solution.py:976
  365.9 36.5 %collective-permute-start.8 = (bf16[2,256,1536]{2,1,0:T(8,128)(2,1)}, bf16[2,256,1536]{2,1,0:T(8,128)(2,1)}, u32[]{:S(2)}, u32[]{:S(2)}) collective-permute-start(bf16[2,256,1536]{2,1,0:T(8,128)(2,1)} %dynamic-slice_bitcast_fusion.2), channel_id=1, source_target_pairs={{0,8},{4,12},{8,0},{12,4},{16,24},{20,28},{24,16},{28,20},{1,9},{5... | collective-permute-start | bytes 4718600 | tf_op jit(solution)/shard_map/ppermute | solution.py:976
  389.4 40.5 %all-to-all-start.4 = ((bf16[4,256,768]{2,1,0:T(8,128)(2,1)}), bf16[4,256,768]{2,1,0:T(8,128)(2,1)S(1)}, u32[]{:S(2)}, u32[]{:S(2)}) async-start(bf16[4,256,768]{2,1,0:T(8,128)(2,1)} %get-tuple-element.228), calls=%async_computation.6 | async-start | bytes 3145728 | tf_op jit(solution)/shard_map/all_to_all | solution.py:973
  393.1 131.7 %reduce-scatter.10.cloned.1.call-start = ((), (), s32[]{:S(2)}) async-start(), calls=%async_computation.16 | async-start | bytes 5242880 | tf_op jit(solution)/shard_map/reduce_scatter | solution.py:970
  393.3 9.1 %copy-start.20 = (bf16[1,2,256,1536]{2,3,1,0:T(8,128)(2,1)S(1)}, bf16[1,2,256,1536]{2,3,1,0:T(8,128)(2,1)}, u32[]{:S(2)}) copy-start(bf16[1,2,256,1536]{2,3,1,0:T(8,128)(2,1)} %copy.199) | copy-start | bytes 4718596
  399.4 6.3 copy-start.8
  405.4 18.5 %collective-permute-start.11 = (bf16[1,256,1536]{1,2,0:T(8,128)(2,1)S(1)}, bf16[1,256,1536]{1,2,0:T(8,128)(2,1)S(1)}, u32[]{:S(2)}, u32[]{:S(2)}) collective-permute-start(bf16[1,256,1536]{1,2,0:T(8,128)(2,1)S(1)} %constant_dynamic-slice_fusion.8), channel_id=1, source_target_pairs={{0,8},{4,12},{8,0},{12,4},{16,24},{20,28},{24,16},{28,20},{1,9},{5... | collective-permute-start | bytes 2359304 | tf_op jit(solution)/shard_map/ppermute | solution.py:976
  407.5 16.4 %copy-start.9 = (bf16[2,256,1536]{2,1,0:T(8,128)(2,1)}, bf16[2,256,1536]{2,1,0:T(8,128)(2,1)S(1)}, u32[]{:S(2)}) copy-start(bf16[2,256,1536]{2,1,0:T(8,128)(2,1)S(1)} %fusion.5) | copy-start | bytes 4718596
  407.6 18.6 %collective-permute-start.10 = (bf16[1,256,1536]{2,1,0:T(8,128)(2,1)S(1)}, bf16[1,256,1536]{2,1,0:T(8,128)(2,1)}, u32[]{:S(2)}, u32[]{:S(2)}) collective-permute-start(bf16[1,256,1536]{2,1,0:T(8,128)(2,1)S(1)} %constant_dynamic-slice_fusion.10), channel_id=1, source_target_pairs={{0,16},{4,20},{8,24},{12,28},{16,0},{20,4},{24,8},{28,12},{1,17},{... | collective-permute-start | bytes 2359304 | tf_op jit(solution)/shard_map/ppermute | solution.py:976
  429.9 46.2 %collective-permute-start.12 = (bf16[1024,3072]{1,0:T(8,128)(2,1)}, bf16[1024,3072]{1,0:T(8,128)(2,1)}, u32[]{:S(2)}, u32[]{:S(2)}) collective-permute-start(bf16[1024,3072]{1,0:T(8,128)(2,1)} %convolution_convert_fusion), channel_id=1, source_target_pairs={{0,4},{4,0},{8,12},{12,8},{16,20},{20,16},{24,28},{28,24},{1,5},{5... | collective-permute-start | bytes 18874376 | tf_op jit(solution)/shard_map/ppermute | solution.py:976
  440.0 13.6 %copy-start.15 = (bf16[4,256,768]{2,1,0:T(8,128)(2,1)S(1)}, bf16[4,256,768]{2,1,0:T(8,128)(2,1)}, u32[]{:S(2)}) copy-start(bf16[4,256,768]{2,1,0:T(8,128)(2,1)} %get-tuple-element.288) | copy-start | bytes 4718596
  452.9 23.1 %collective-permute-start.13 = (bf16[2,256,768]{2,1,0:T(8,128)(2,1)}, bf16[2,256,768]{2,1,0:T(8,128)(2,1)}, u32[]{:S(2)}, u32[]{:S(2)}) collective-permute-start(bf16[2,256,768]{2,1,0:T(8,128)(2,1)} %dynamic-slice_bitcast_fusion.5), channel_id=1, source_target_pairs={{0,8},{4,12},{8,0},{12,4},{16,24},{20,28},{24,16},{28,20},{1,9},{5... | collective-permute-start | bytes 2359304 | tf_op jit(solution)/shard_map/ppermute | solution.py:976
  454.6 21.5 %collective-permute-start.14 = (bf16[2,256,768]{2,1,0:T(8,128)(2,1)}, bf16[2,256,768]{2,1,0:T(8,128)(2,1)S(1)}, u32[]{:S(2)}, u32[]{:S(2)}) collective-permute-start(bf16[2,256,768]{2,1,0:T(8,128)(2,1)} %dynamic-slice_bitcast_fusion.4), channel_id=1, source_target_pairs={{0,16},{4,20},{8,24},{12,28},{16,0},{20,4},{24,8},{28,12},{1,17},{... | collective-permute-start | bytes 2359304 | tf_op jit(solution)/shard_map/ppermute | solution.py:976
  455.9 21.9 %copy-start.3 = (bf16[256,3072]{1,0:T(8,128)(2,1)S(1)}, bf16[256,3072]{1,0:T(8,128)(2,1)}, u32[]{:S(2)}) copy-start(bf16[256,3072]{1,0:T(8,128)(2,1)} %get-tuple-element.230) | copy-start | bytes 4718596
  455.9 21.9 %copy-start.21 = (bf16[256,1024]{1,0:T(8,128)(2,1)S(1)}, bf16[256,1024]{1,0:T(8,128)(2,1)}, u32[]{:S(2)}) copy-start(bf16[256,1024]{1,0:T(8,128)(2,1)} %get-tuple-element.257) | copy-start | bytes 1572868
  476.1 6.4 copy-start.37
  476.1 10.6 %collective-permute-start.15 = (f32[8,768]{1,0:T(8,128)}, f32[8,768]{1,0:T(8,128)S(1)}, u32[]{:S(2)}, u32[]{:S(2)}) collective-permute-start(f32[8,768]{1,0:T(8,128)} %get-tuple-element.256), channel_id=1, source_target_pairs={{4,0},{8,4},{12,8},{16,12},{20,16},{24,20},{28,24},{5,1},{9,5},{13... | collective-permute-start | bytes 73736 | tf_op jit(solution)/shard_map/ppermute | solution.py:1170
  486.7 37.4 %collective-permute-start.16 = (bf16[2,256,1536]{2,1,0:T(8,128)(2,1)}, bf16[2,256,1536]{2,1,0:T(8,128)(2,1)}, u32[]{:S(2)}, u32[]{:S(2)}) collective-permute-start(bf16[2,256,1536]{2,1,0:T(8,128)(2,1)} %dynamic-slice_bitcast_fusion.1), channel_id=1, source_target_pairs={{0,8},{4,12},{8,0},{12,4},{16,24},{20,28},{24,16},{28,20},{1,9},{5... | collective-permute-start | bytes 4718600 | tf_op jit(solution)/shard_map/ppermute | solution.py:976
  488.7 36.0 %collective-permute-start.17 = (bf16[2,256,1536]{2,1,0:T(8,128)(2,1)}, bf16[2,256,1536]{2,1,0:T(8,128)(2,1)S(1)}, u32[]{:S(2)}, u32[]{:S(2)}) collective-permute-start(bf16[2,256,1536]{2,1,0:T(8,128)(2,1)} %dynamic-slice_bitcast_fusion), channel_id=1, source_target_pairs={{0,16},{4,20},{8,24},{12,28},{16,0},{20,4},{24,8},{28,12},{1,17},{... | collective-permute-start | bytes 4718600 | tf_op jit(solution)/shard_map/ppermute | solution.py:976
  506.6 8.8 %all-to-all-start.5 = ((f32[4,2,512]{2,1,0:T(2,128)}), f32[4,2,512]{2,1,0:T(2,128)S(1)}, u32[]{:S(2)}, u32[]{:S(2)}) async-start(f32[4,2,512]{2,1,0:T(2,128)} %bitcast.48), calls=%async_computation.9 | async-start | bytes 32768 | tf_op jit(solution)/shard_map/all_to_all | solution.py:973
  509.9 88.0 %all-reduce.18.cloned.1.call-start = ((), (), s32[]{:S(2)}) async-start(), calls=%async_computation.18 | async-start | bytes 3244032 | tf_op jit(solution)/shard_map/psum | solution.py:1201
  524.8 6.9 %copy-start.32 = (bf16[2,256,1536]{2,1,0:T(8,128)(2,1)}, bf16[2,256,1536]{2,1,0:T(8,128)(2,1)S(1)}, u32[]{:S(2)}) copy-start(bf16[2,256,1536]{2,1,0:T(8,128)(2,1)S(1)} %collective-permute-done.17) | copy-start | bytes 4718596
  531.7 116.9 %reduce-scatter.12.cloned.1.call-start = ((), (), s32[]{:S(2)}) async-start(), calls=%async_computation.17 | async-start | bytes 5242880 | tf_op jit(solution)/shard_map/reduce_scatter | solution.py:970
  532.4 127.8 %reduce-scatter.14.cloned.1.call-start = ((), (), s32[]{:S(2)}) async-start(), calls=%async_computation.19 | async-start | bytes 1966080 | tf_op jit(solution)/shard_map/reduce_scatter | solution.py:970
  532.9 9.6 %copy-start.31 = (s32[1024,1]{1,0:T(8,128)}, s32[1024,1]{1,0:T(8,128)S(1)}, u32[]{:S(2)}) copy-start(s32[1024,1]{1,0:T(8,128)S(1)} %copy.173.place_ref) | copy-start | bytes 12292
  534.6 7.9 %copy-start.7 = (bf16[4,256,1536]{2,1,0:T(8,128)(2,1)S(1)}, bf16[4,256,1536]{2,1,0:T(8,128)(2,1)}, u32[]{:S(2)}) copy-start(bf16[4,256,1536]{2,1,0:T(8,128)(2,1)} %copy-done.6) | copy-start | bytes 9437188
  542.5 45.3 %collective-permute-start.18 = (bf16[1024,1536]{1,0:T(8,128)(2,1)}, bf16[1024,1536]{1,0:T(8,128)(2,1)}, u32[]{:S(2)}, u32[]{:S(2)}) collective-permute-start(bf16[1024,1536]{1,0:T(8,128)(2,1)} %convolution_convert_fusion.2), channel_id=1, source_target_pairs={{0,4},{4,0},{8,12},{12,8},{16,20},{20,16},{24,28},{28,24},{1,5},{5... | collective-permute-start | bytes 9437192 | tf_op jit(solution)/shard_map/ppermute | solution.py:976
  545.5 38.1 %collective-permute-start.25 = (bf16[1,256,1536]{2,1,0:T(8,128)(2,1)}, bf16[1,256,1536]{2,1,0:T(8,128)(2,1)}, u32[]{:S(2)}, u32[]{:S(2)}) collective-permute-start(bf16[1,256,1536]{2,1,0:T(8,128)(2,1)} %constant_dynamic-slice_fusion.1), channel_id=1, source_target_pairs={{0,16},{4,20},{8,24},{12,28},{16,0},{20,4},{24,8},{28,12},{1,17},{... | collective-permute-start | bytes 2359304 | tf_op jit(solution)/shard_map/ppermute | solution.py:976
  548.4 36.6 %collective-permute-start.26 = (bf16[1,256,1536]{2,1,0:T(8,128)(2,1)}, bf16[1,256,1536]{2,1,0:T(8,128)(2,1)}, u32[]{:S(2)}, u32[]{:S(2)}) collective-permute-start(bf16[1,256,1536]{2,1,0:T(8,128)(2,1)} %constant_dynamic-slice_fusion), channel_id=1, source_target_pairs={{0,8},{4,12},{8,0},{12,4},{16,24},{20,28},{24,16},{28,20},{1,9},{5... | collective-permute-start | bytes 2359304 | tf_op jit(solution)/shard_map/ppermute | solution.py:976
  550.6 27.9 %collective-permute-start.19 = (bf16[1,256,768]{2,1,0:T(8,128)(2,1)S(1)}, bf16[1,256,768]{2,1,0:T(8,128)(2,1)S(1)}, u32[]{:S(2)}, u32[]{:S(2)}) collective-permute-start(bf16[1,256,768]{2,1,0:T(8,128)(2,1)S(1)} %constant_dynamic-slice_fusion.7), channel_id=1, source_target_pairs={{0,16},{4,20},{8,24},{12,28},{16,0},{20,4},{24,8},{28,12},{1,17},{... | collective-permute-start | bytes 1179656 | tf_op jit(solution)/shard_map/ppermute | solution.py:976
  553.0 28.2 %collective-permute-start.20 = (bf16[1,256,768]{2,1,0:T(8,128)(2,1)}, bf16[1,256,768]{2,1,0:T(8,128)(2,1)}, u32[]{:S(2)}, u32[]{:S(2)}) collective-permute-start(bf16[1,256,768]{2,1,0:T(8,128)(2,1)} %constant_dynamic-slice_fusion.6), channel_id=1, source_target_pairs={{0,8},{4,12},{8,0},{12,4},{16,24},{20,28},{24,16},{28,20},{1,9},{5... | collective-permute-start | bytes 1179656 | tf_op jit(solution)/shard_map/ppermute | solution.py:976
  557.1 21.4 %copy-start.24 = (bf16[2,256,768]{2,1,0:T(8,128)(2,1)S(1)}, bf16[2,256,768]{2,1,0:T(8,128)(2,1)}, u32[]{:S(2)}) copy-start(bf16[2,256,768]{2,1,0:T(8,128)(2,1)} %copy-done.23) | copy-start | bytes 2359300
  558.5 22.8 %copy-start.26 = (bf16[2,256,768]{2,1,0:T(8,128)(2,1)S(1)}, bf16[2,256,768]{2,1,0:T(8,128)(2,1)}, u32[]{:S(2)}) copy-start(bf16[2,256,768]{2,1,0:T(8,128)(2,1)} %copy-done.25) | copy-start | bytes 2359300
  559.8 23.9 %copy-start.12 = (bf16[2,256,1536]{2,1,0:T(8,128)(2,1)S(1)}, bf16[2,256,1536]{2,1,0:T(8,128)(2,1)}, u32[]{:S(2)}) copy-start(bf16[2,256,1536]{2,1,0:T(8,128)(2,1)} %copy-done.11) | copy-start | bytes 4718596
  597.1 28.6 %collective-permute-start.21 = (bf16[2,256,768]{2,1,0:T(8,128)(2,1)}, bf16[2,256,768]{2,1,0:T(8,128)(2,1)}, u32[]{:S(2)}, u32[]{:S(2)}) collective-permute-start(bf16[2,256,768]{2,1,0:T(8,128)(2,1)} %dynamic-slice_bitcast_fusion.3), channel_id=1, source_target_pairs={{0,8},{4,12},{8,0},{12,4},{16,24},{20,28},{24,16},{28,20},{1,9},{5... | collective-permute-start | bytes 2359304 | tf_op jit(solution)/shard_map/ppermute | solution.py:976
  605.1 24.0 %collective-permute-start.23 = (bf16[2,256,768]{1,2,0:T(8,128)(2,1)}, bf16[2,256,768]{1,2,0:T(8,128)(2,1)}, u32[]{:S(2)}, u32[]{:S(2)}) collective-permute-start(bf16[2,256,768]{1,2,0:T(8,128)(2,1)} %bitcast.180), channel_id=1, source_target_pairs={{0,16},{4,20},{8,24},{12,28},{16,0},{20,4},{24,8},{28,12},{1,17},{... | collective-permute-start | bytes 2359304 | tf_op jit(solution)/shard_map/ppermute | solution.py:976
  621.4 27.1 %all-to-all-start.6 = ((bf16[8,128,512]{2,1,0:T(8,128)(2,1)}), bf16[8,128,512]{2,1,0:T(8,128)(2,1)}, u32[]{:S(2)}, u32[]{:S(2)}) async-start(bf16[8,128,512]{2,1,0:T(8,128)(2,1)} %bitcast.177), calls=%async_computation.10 | async-start | bytes 2097152 | tf_op jit(solution)/shard_map/all_to_all | solution.py:973
  627.1 21.3 %collective-permute-start.22 = (bf16[1,256,768]{2,1,0:T(8,128)(2,1)S(1)}, bf16[1,256,768]{2,1,0:T(8,128)(2,1)S(1)}, u32[]{:S(2)}, u32[]{:S(2)}) collective-permute-start(bf16[1,256,768]{2,1,0:T(8,128)(2,1)S(1)} %constant_dynamic-slice_fusion.5), channel_id=1, source_target_pairs={{0,16},{4,20},{8,24},{12,28},{16,0},{20,4},{24,8},{28,12},{1,17},{... | collective-permute-start | bytes 1179656 | tf_op jit(solution)/shard_map/ppermute | solution.py:976
  631.2 28.0 %collective-permute-start.24 = (bf16[1,256,768]{1,2,0:T(8,128)(2,1)}, bf16[1,256,768]{1,2,0:T(8,128)(2,1)S(1)}, u32[]{:S(2)}, u32[]{:S(2)}) collective-permute-start(bf16[1,256,768]{1,2,0:T(8,128)(2,1)} %constant_dynamic-slice_fusion.2), channel_id=1, source_target_pairs={{0,8},{4,12},{8,0},{12,4},{16,24},{20,28},{24,16},{28,20},{1,9},{5... | collective-permute-start | bytes 1179656 | tf_op jit(solution)/shard_map/ppermute | solution.py:976
  653.8 21.7 %all-to-all-start.7 = ((bf16[8,128,512]{2,1,0:T(8,128)(2,1)}), bf16[8,128,512]{2,1,0:T(8,128)(2,1)}, u32[]{:S(2)}, u32[]{:S(2)}) async-start(bf16[8,128,512]{2,1,0:T(8,128)(2,1)} %bitcast.178), calls=%async_computation.11 | async-start | bytes 2097152 | tf_op jit(solution)/shard_map/all_to_all | solution.py:973
  670.1 10.8 %copy-start.1 = (bf16[684,2048]{1,0:T(8,128)(2,1)S(1)}, bf16[684,2048]{1,0:T(8,128)(2,1)}, u32[]{:S(2)}) copy-start(bf16[684,2048]{1,0:T(8,128)(2,1)} %param.31) | copy-start | bytes 8404996
  (40 other events, 113.8 us)
Sparse Core Ops, SparseCore 0:
  11.3 3.4 sort.12.cloned.1.call-done
  531.8 61.9 all-reduce.17
  (1 shorter events, 0.0 us)
Sparse Core Ops, SparseCore 1:
  12.2 107.1 all-gather.7
  179.4 64.3 all-gather.5
  283.1 43.6 reduce-scatter.7
  334.3 43.7 reduce-scatter.5
  430.0 75.9 reduce-scatter.9
  534.9 74.6 reduce-scatter.11
  612.3 35.7 reduce-scatter.13

commit v3 on v2

--- a/solution.py
+++ b/solution.py
@@ -1175,12 +1175,17 @@
     input_part, rec_low, norm_gain_part = input_backward(
         place, rec_low, inputs_part, end, returned, w_branch, w_input, stream, gain, resid_grad
     )
-    input_part, block_share, pre_low, pair, down, pair_received, down_received, *out_received = tie(
-        input_part, block_share, pre_low, pair, down, pair_received, down_received, *out_received
+    input_part, block_share, pre_low, pair, down, pair_received, down_received = tie(
+        input_part, block_share, pre_low, pair, down, pair_received, down_received
     )
     input_share = scatter_sum(input_part, "mp", 1)
 
-    far_rec = swap(outer(hidden_far, rec_low), 0)
+    far_rec = outer(hidden_far, rec_low)
+    far_rec, pre_low, *out_received = tie(far_rec, pre_low, *out_received)
+    far_rec = swap(far_rec, 0)
+    all_rows = jnp.arange(row_count, dtype=jnp.int32)[None]
+    home_block = exchange(place_rows(mlp_landing.reshape(-1, 1), all_rows, block_share), "seq")
+    home_block, pre_low = tie(home_block, pre_low)
 
     sums = jnp.sum(sums.reshape(CONV + 2, 8, width), axis=1)[:, :channels]
     sums = jnp.concatenate(
@@ -1205,13 +1210,9 @@
 
     out = add_all(out, out_received)
     grad_rec = with_partner(hidden_near, far_rec, rec_low)
-    block_share, grad_rec = tie(block_share, grad_rec)
-    sent_rec = finish(two_ways(grad_rec))
+    rec = two_ways(grad_rec)
+    rec_received = send_all(rec)
     sent_out = finish(out)
-    sent_branch = sent_rec[:, :channels].astype(F32)
-    sent_input = sent_rec[:, width : width + channels].astype(F32)
-    all_rows = jnp.arange(row_count, dtype=jnp.int32)[None]
-    home_block = exchange(place_rows(mlp_landing.reshape(-1, 1), all_rows, block_share), "seq")
     sent_pair = finish(add_all(pair, pair_received))
     sent_down = finish(add_all(down, down_received)).astype(F32).T
     unit = mlp_tile(hidden_units)
@@ -1221,10 +1222,15 @@
     input_share, home_block, sent_gate, sent_up, sent_down = tie(
         input_share, home_block, sent_gate, sent_up, sent_down
     )
+    input_share, sent_out = tie(input_share, sent_out)
     sent_out = scatter_sum(sent_out, "mp", 1)
     sent_out = sent_out[:, :channels].astype(F32).T
 
     home_input = exchange(place_rows(landing.reshape(-1, 1), all_rows, input_share), "seq")
+    home_input, *rec_received = tie(home_input, *rec_received)
+    sent_rec = finish(add_all(rec, rec_received))
+    sent_branch = sent_rec[:, :channels].astype(F32)
+    sent_input = sent_rec[:, width : width + channels].astype(F32)
     block_out = restore_rows(dest_row, dest_col, home_block)
     input_grad = restore_rows(dest_row, dest_col, home_input)
     return (

time: 700 us -> 719 us (1.027)
  waiting for transfers between devices: 167 us -> 182 us
    psum x1, waiting for transfers between devices: 0.01 us -> 38.9 us  [shards(): small = lax.psum(small, 'seq')]
    ppermute x22, waiting for transfers between devices: 67.2 us -> 50.1 us  [swap(): lax.ppermute(x, 'seq', [(i, i ^ 1 << bit) for i in range(shard_count)])]
  transfers between devices with their start and end apart: 43 -> 43, of which waited for: 16 -> 17; matrix products, arithmetic and copies ran while one was open for 23% -> 23% of each run, Pallas kernels for 33% -> 34%
where the time goes in v3:
time: 719 us; the launch traced here: 708 us
  Pallas kernels  247 us (34%)
  waiting for transfers between devices  182 us (25%)
  local copies, waits for them, and re-layouts  73.1 us (10%)
  starting transfers between devices  62.6 us (9%)
  matrix products  59.7 us (8%)
  other arithmetic  43.8 us (6%)
  blocking collectives  22.4 us (3%)
  between operations  17 us (2%)
    pallas_call x2, Pallas kernels, mlp_chunk(): call(body, (steps,), [whole((rows, model)), rows_of, pl.BlockSpec((sub, m...  65.9 us
    all_to_all x8, waiting for transfers between devices, exchange(): return lax.all_to_all(x, axis, split_axis=0, concat_axis=0, tiled=True)  65.5 us
    dot_general x8, matrix products, mm(): return lax.dot_general(left, right, dims, preferred_element_type=F32)  59.7 us
    ppermute x22, waiting for transfers between devices, swap(): lax.ppermute(x, 'seq', [(i, i ^ 1 << bit) for i in range(shard_count)])  50.1 us
    psum x1, waiting for transfers between devices, shards(): small = lax.psum(small, 'seq')  38.9 us
    all_to_all x8, starting transfers between devices, exchange(): return lax.all_to_all(x, axis, split_axis=0, concat_axis=0, tiled=True)  35.8 us
    unnamed x131, local copies, waits for them, and re-layouts  25.7 us
    ppermute x3, waiting for transfers between devices, shards(): lax.ppermute(sent_cot[q], 'seq', [(i, i ^ 2 * q) for i in range(shard_cou...  23.3 us
  transfers between devices with their start and end apart: 43, of which 17 were waited for; matrix products, arithmetic and copies ran while one was open for 23% of the time, Pallas kernels for 34%

profile of v3, /device:TPU:0, one launch (start us, length us, event | category | flops | bytes accessed | tf_op | source)
XLA Modules:
  0.0 707.7 jit_solution(3623017986011089667)
XLA Ops:
  16.1 8.9 %shard_map.298 = bf16[1024,2048]{1,0:T(8,128)(2,1)} custom-call(s32[1]{0:T(128)} %constant.187.clone.1.turn_ref, s32[1,1024]{1,0:T(1,128)} %bitcast.190, s32[1024,1]{1,0:T(8,128)} %copy.178.col_ref, bf16[1024,2048]{1,0:T(8,128)(2,1)} %val_ref.1), custom_call_target="tpu_custom_call" | custom-call | flops 4294967296 | bytes 8388608 | tf_op jit(solution)/shard_map/pallas_call | solution.py:103
  25.0 5.2 all-to-all-start
  30.2 11.5 %shard_map.299 = (bf16[128,2048]{1,0:T(8,128)(2,1)}, bf16[128,2048]{1,0:T(8,128)(2,1)}, bf16[128,2048]{1,0:T(8,128)(2,1)}, bf16[128,2048]{1,0:T(8,128)(2,1)}, bf...) custom-call(s32[1]{0:T(128)} %bitcast.16.turn_ref, ...), custom_call_target="tpu_custom_call" | custom-call | flops 4294967296 | bytes 8388608 | tf_op jit(solution)/shard_map/pallas_call | solution.py:138
  41.7 3.1 pad_maximum_fusion
  53.7 25.7 %all-to-all-done = bf16[8,128,2048]{2,1,0:T(8,128)(2,1)} async-done(((bf16[8,128,2048]{2,1,0:T(8,128)(2,1)}), bf16[8,128,2048]{2,1,0:T(8,128)(2,1)}, u32[]{:S(2)}, u32[]{:S(2)}) %all-to-all-start) | async-done | bytes 4194336 | tf_op jit(solution)/shard_map/all_to_all | solution.py:973
  79.4 18.3 %shard_map.300 = (bf16[1024,2048]{1,0:T(8,128)(2,1)}, bf16[1024,1024]{1,0:T(8,128)(2,1)}, bf16[1024,1024]{1,0:T(8,128)(2,1)}, f32[1024,768]{1,0:T(8,128)}, f32[1024,768]{1,0:T(8,128)}) custom-call(s32[3]{0:T(128)} %pad_add_fusion.my_ref.place_ref, s32[1,1024]{1,0:T(1,128)} %bitcast.187, bf16[1024,2048]{1,0:T(8,128)(2,1)} %bitcast.15.arr_ref, ...), custom_call_target="tpu_custom_call" | custom-call | flops 10737418240 | bytes 25165824 | tf_op jit(solution)/shard_map/pallas_call | solution.py:267
  103.0 13.3 %shard_map.301 = (bf16[1024,768]{1,0:T(8,128)(2,1)}, f32[1024,1536]{1,0:T(8,128)}, f32[1024,768]{1,0:T(8,128)}, f32[1024,768]{1,0:T(8,128)}, f32[1024,768]{1,0:T(8,128)}, /*index=5*/f32[8,768]{1,0:T(8,128)}) custom-call(f32[1024,768]{1,0:T(8,128)} %get-tuple-element.177.in_ref.in_before_ref, f32[8,768]{1,0:T(8,128)} %copy-done.43, ...), custom_call_target="tpu_custom_call" | custom-call | flops 2573205504 | bytes 23592960 | tf_op jit(solution)/shard_map/pallas_call | solution.py:367
  116.3 11.5 %all-gather = f32[64,768]{1,0:T(8,128)} all-gather(f32[8,768]{1,0:T(8,128)} %get-tuple-element.179.tail_ref), channel_id=2, replica_groups=mesh['seq'=8,'mp'=4] {'seq'}, dimensions={0}, use_global_device_ids=true | all-gather | bytes 221184 | tf_op jit(solution)/shard_map/all_gather | solution.py:1069
  127.8 9.4 %shard_map.302 = (f32[1024,768]{1,0:T(8,128)}, f32[8,768]{1,0:T(8,128)}, bf16[4,128,768]{2,1,0:T(8,128)(2,1)}, bf16[4,128,768]{2,1,0:T(8,128)(2,1)}) custom-call(s32[3]{0:T(128)} %pad_add_fusion.my_ref.place_ref, f32[8,8,768]{2,1,0:T(8,128)} %bitcast.181, f32[1024,768]{1,0:T(8,128)} %get-tuple-element.185.local_ref, ...), custom_call_target="tpu_custom_call" | custom-call | flops 47185920 | bytes 14155776 | tf_op jit(solution)/shard_map/pallas_call | solution.py:428
  137.6 5.6 all-to-all-start.2
  145.3 23.1 %collective-permute-done.3.refs_1_ = bf16[256,2048]{1,0:T(8,128)(2,1)S(1)} collective-permute-done((bf16[256,2048]{1,0:T(8,128)(2,1)}, bf16[256,2048]{1,0:T(8,128)(2,1)S(1)}, u32[]{:S(2)}, u32[]{:S(2)}) %collective-permute-start.3) | collective-permute-done | bytes 1048608 | tf_op jit(solution)/shard_map/ppermute | solution.py:1072
  170.4 8.8 %shard_map.303 = (f32[256,2048]{1,0:T(8,128)}, bf16[256,3072]{1,0:T(8,128)(2,1)}, bf16[128,2048]{1,0:T(8,128)(2,1)}) custom-call(s32[3]{0:T(128)} %pad_add_fusion.my_ref.place_ref, bf16[4,128,768]{2,1,0:T(8,128)(2,1)} %copy-done.23, bf16[4,688,1024]{2,1,0:T(8,128)(2,1)} %bitcast.148, bf16[4,688,1024]{2,1,0:T(8,128)(2,1)} %collective-permute-done.2.far_ref, ...), custom_call_target="tpu_custom_call" | custom-call | flops 1610612736 | bytes 14680064 | tf_op jit(solution)/shard_map/pallas_call | solution.py:474
  179.2 4.9 all-to-all-start.1
  185.5 36.1 %all-to-all-done.1.mixed_ref = bf16[4,128,768]{2,1,0:T(8,128)(2,1)S(1)} async-done(((bf16[4,128,768]{2,1,0:T(8,128)(2,1)}), bf16[4,128,768]{2,1,0:T(8,128)(2,1)S(1)}, u32[]{:S(2)}, u32[]{:S(2)}) %all-to-all-start.1) | async-done | bytes 786464 | tf_op jit(solution)/shard_map/all_to_all | solution.py:973
  222.6 8.8 %shard_map.304 = (f32[256,2048]{1,0:T(8,128)}, bf16[256,3072]{1,0:T(8,128)(2,1)}, bf16[128,2048]{1,0:T(8,128)(2,1)}) custom-call(s32[3]{0:T(128)} %pad_add_fusion.my_ref.place_ref, bf16[4,128,768]{2,1,0:T(8,128)(2,1)} %copy-done.29, bf16[4,688,1024]{2,1,0:T(8,128)(2,1)} %bitcast.149, ...), custom_call_target="tpu_custom_call", output_to_operand_aliasing={{0}: (6, {}), {1}: (7, {})} | custom-call | flops 1610612736 | bytes 14680064 | tf_op jit(solution)/shard_map/pallas_call | solution.py:474
  231.4 2.6 broadcast_in_dim.42
  234.0 4.5 all-to-all-start.3
  239.1 10.4 %shard_map.305 = (bf16[1024,2048]{1,0:T(8,128)(2,1)}, bf16[1024,1024]{1,0:T(8,128)(2,1)}, bf16[1024,1024]{1,0:T(8,128)(2,1)}) custom-call(s32[3]{0:T(128)} %pad_add_fusion.my_ref.place_ref, s32[1024,1]{1,0:T(8,128)} %constant.205.clone.place_ref, s32[1,1024]{1,0:T(1,128)} %bitcast.197, bf16[256,2048]{1,0:T(8,128)(2,1)} %pad_maximum_fusion.2.refs_0_, ...), custom_call_target="tpu_custom_call" | custom-call | flops 4294967296 | bytes 12582912 | tf_op jit(solution)/shard_map/pallas_call | solution.py:203
  249.6 33.2 %shard_map.306 = (bf16[1024,1536]{1,0:T(8,128)(2,1)}, bf16[1024,3072]{1,0:T(8,128)(2,1)}, bf16[1024,1024]{1,0:T(8,128)(2,1)}, bf16[1024,1024]{1,0:T(8,128)(2,1)}...) custom-call(s32[3]{0:T(128)} %pad_add_fusion.my_ref.place_ref, ...), custom_call_target="tpu_custom_call" | custom-call | flops 19327352832 | bytes 29360128 | tf_op jit(solution)/shard_map/pallas_call | solution.py:553
  284.5 32.7 %shard_map.307 = (bf16[1024,1536]{1,0:T(8,128)(2,1)}, bf16[1024,3072]{1,0:T(8,128)(2,1)}, bf16[1024,1024]{1,0:T(8,128)(2,1)}, bf16[1024,1024]{1,0:T(8,128)(2,1)}...) custom-call(s32[3]{0:T(128)} %pad_add_fusion.my_ref.place_ref, ...), custom_call_target="tpu_custom_call", output_to_operand_aliasing={{0}: (7, {}), {1}: (8, {}), {2}: (9, {}), {3}: (10, {}), {4... | custom-call | flops 19327352832 | bytes 29360128 | tf_op jit(solution)/shard_map/pallas_call | solution.py:553
  317.2 7.8 %convolution_convert_fusion.3 = bf16[1024,1536]{1,0:T(8,128)(2,1)} fusion(bf16[1024,1024]{1,0:T(8,128)(2,1)} %get-tuple-element.222, bf16[1024,1536]{1,0:T(8,128)(2,1)} %get-tuple-element.228), kind=kOutput, calls=%fused_computation.11 | convolution fusion | flops 3222798336 | bytes 8388608 | tf_op jit(solution)/shard_map/dot_general | solution.py:30
  325.1 8.7 %convolution_convert_fusion.1 = bf16[1024,3072]{1,0:T(8,128)(2,1)} fusion(bf16[1024,1024]{1,0:T(8,128)(2,1)S(1)} %copy-done.59, bf16[1024,3072]{1,0:T(8,128)(2,1)S(1)} %copy-done.55), kind=kOutput, calls=%fused_computation.5 | convolution fusion | flops 6445596672 | bytes 14680064 | tf_op jit(solution)/shard_map/dot_general | solution.py:30
  333.9 10.5 %shard_map.308 = (bf16[256,1024]{1,0:T(8,128)(2,1)}, bf16[256,1024]{1,0:T(8,128)(2,1)}, f32[256,2048]{1,0:T(8,128)}, bf16[4,256,768]{2,1,0:T(8,128)(2,1)}, f32[1,2048]{1,0:T(1,128)}) custom-call(s32[3]{0:T(128)} %pad_add_fusion.my_ref.place_ref, bf16[128,2048]{1,0:T(8,128)(2,1)} %reduce-scatter.8.cloned.1.call-done.g_ref, ...), custom_call_target="tpu_custom_call" | custom-call | flops 1610612736 | bytes 16252928 | tf_op jit(solution)/shard_map/pallas_call | solution.py:621
  344.8 10.8 %add_convert_fusion.1 = bf16[1024,3072]{1,0:T(8,128)(2,1)S(1)} fusion(bf16[1024,3072]{1,0:T(8,128)(2,1)} %collective-permute-done.6, bf16[1024,1024]{1,0:T(8,128)(2,1)S(1)} %copy-done.56, bf16[1024,3072]{1,0:T(8,128)(2,1)} %get-tuple-element.226), kind=kOutput, calls=%fused_computation.1 | convolution fusion | flops 6451888128 | bytes 20971520 | tf_op jit(solution)/shard_map/dot_general | solution.py:30
  355.6 2.3 fusion.45
  359.3 2.6 copy.169
  363.1 2.7 dynamic-slice_bitcast_fusion.2
  365.9 5.9 add_convert_fusion.3
  373.7 4.0 reduce-scatter.6.cloned.1.call-done.g_ref
  379.3 9.7 %shard_map.309 = (bf16[256,1024]{1,0:T(8,128)(2,1)}, bf16[256,1024]{1,0:T(8,128)(2,1)}, f32[256,2048]{1,0:T(8,128)}, bf16[4,256,768]{2,1,0:T(8,128)(2,1)}, f32[1,2048]{1,0:T(1,128)}) custom-call(s32[3]{0:T(128)} %pad_add_fusion.my_ref.place_ref, ...), custom_call_target="tpu_custom_call", output_to_operand_aliasing={{0}: (7, {}), {1}: (8, {}), {2}: (9, {}), {3}: (10, {})} | custom-call | flops 1610612736 | bytes 16252928 | tf_op jit(solution)/shard_map/pallas_call | solution.py:621
  389.0 3.7 all-to-all-start.4
  393.0 6.1 convolution_convert_fusion
  399.1 3.2 collective-permute-done.8
  409.1 14.5 %collective-permute-done.11 = bf16[1,256,1536]{1,2,0:T(8,128)(2,1)S(1)} collective-permute-done((bf16[1,256,1536]{1,2,0:T(8,128)(2,1)S(1)}, bf16[1,256,1536]{1,2,0:T(8,128)(2,1)S(1)}, u32[]{:S(2)}, u32[]{:S(2)}) %collective-permute-start.11) | collective-permute-done | bytes 786464 | tf_op jit(solution)/shard_map/ppermute | solution.py:976
  423.6 2.4 collective-permute-done.10
  426.0 3.6 all-to-all-done.4
  430.7 8.9 %shard_map.310 = (f32[1024,768]{1,0:T(8,128)}, f32[1024,768]{1,0:T(8,128)}, f32[8,768]{1,0:T(8,128)}) custom-call(bf16[1024,768]{1,0:T(8,128)(2,1)} %bitcast.153, f32[1024,768]{1,0:T(8,128)} %get-tuple-element.187.branch_ref, f32[1024,768]{1,0:T(8,128)} %get-tuple-element.244.keep_ref, f32[8,768]{1,0:T(8,128)} %get-tuple-element.179.tail_ref), custom_call_target="tpu_custom_call" | custom-call | flops 78643200 | bytes 14155776 | tf_op jit(solution)/shard_map/pallas_call | solution.py:692
  439.7 10.9 %all-gather.2 = f32[64,768]{1,0:T(8,128)} all-gather(f32[8,768]{1,0:T(8,128)} %get-tuple-element.245), channel_id=4, replica_groups=mesh['seq'=8,'mp'=4] {'seq'}, dimensions={0}, use_global_device_ids=true | all-gather | bytes 221184 | tf_op jit(solution)/shard_map/all_gather | solution.py:1162
  450.6 2.1 dynamic-slice_bitcast_fusion.5
  457.7 20.2 %shard_map.311 = (bf16[1024,1536]{1,0:T(8,128)(2,1)}, bf16[1024,768]{1,0:T(8,128)(2,1)}, bf16[1024,1536]{1,0:T(8,128)(2,1)}, f32[48,768]{1,0:T(8,128)}, f32[8,768]{1,0:T(8,128)}, /*index=5*/f32[8,768]{1,0:T(8,128)}) custom-call(s32[3]{0:T(128)} %pad_add_fusion.my_ref.place_ref, f32[8,8,768]{2,1,0:T(8,128)} %bitcast.179, ...), custom_call_target="tpu_custom_call" | custom-call | flops 2651848704 | bytes 31457280 | tf_op jit(solution)/shard_map/pallas_call | solution.py:803
  480.5 4.7 add_convert_fusion
  489.4 2.0 collective-permute-start.16
  492.2 15.8 %shard_map.312 = (bf16[1024,2048]{1,0:T(8,128)(2,1)}, bf16[1024,1536]{1,0:T(8,128)(2,1)}, f32[1,2048]{1,0:T(1,128)}) custom-call(s32[3]{0:T(128)} %pad_add_fusion.my_ref.place_ref, bf16[1024,1536]{1,0:T(8,128)(2,1)} %get-tuple-element.255.bl_ref, bf16[1024,768]{1,0:T(8,128)(2,1)} %get-tuple-element.256.il_ref, ...), custom_call_target="tpu_custom_call", output_to_operand_aliasing={{1}: (1, {})} | custom-call | flops 6505365504 | bytes 19398656 | tf_op jit(solution)/shard_map/pallas_call | solution.py:884
  509.4 3.3 all-to-all-start.7
  512.6 8.4 %convolution_convert_fusion.2 = bf16[1024,1536]{1,0:T(8,128)(2,1)} fusion(bf16[1024,1024]{1,0:T(8,128)(2,1)} %get-tuple-element.277, bf16[1024,1536]{1,0:T(8,128)(2,1)} %get-tuple-element.278), kind=kOutput, calls=%fused_computation.10 | convolution fusion | flops 3222798336 | bytes 8388608 | tf_op jit(solution)/shard_map/dot_general | solution.py:30
  521.8 5.1 collective-permute-done.16
  528.1 4.6 shard_map.313
  532.7 4.2 all-to-all-start.5
  537.6 2.4 fusion.3
  556.5 20.0 %collective-permute-done.18 = bf16[1,256,768]{2,1,0:T(8,128)(2,1)S(1)} collective-permute-done((bf16[1,256,768]{2,1,0:T(8,128)(2,1)S(1)}, bf16[1,256,768]{2,1,0:T(8,128)(2,1)S(1)}, u32[]{:S(2)}, u32[]{:S(2)}) %collective-permute-start.18) | collective-permute-done | bytes 393248 | tf_op jit(solution)/shard_map/ppermute | solution.py:976
  583.3 6.4 shard_map.316
  589.8 7.3 %add_convert_fusion.2 = bf16[1024,1536]{1,0:T(8,128)(2,1)} fusion(bf16[1024,1536]{1,0:T(8,128)(2,1)} %collective-permute-done.22, bf16[1024,1024]{1,0:T(8,128)(2,1)S(1)} %copy-done.58, bf16[1024,1536]{1,0:T(8,128)(2,1)} %get-tuple-element.278), kind=kOutput, calls=%fused_computation.2 | convolution fusion | flops 3225944064 | bytes 11534336 | tf_op jit(solution)/shard_map/dot_general | solution.py:30
  597.1 2.1 fusion.46
  600.4 2.5 copy.181
  605.0 4.6 shard_map.315
  609.6 4.5 all-to-all-start.6
  615.1 2.0 collective-permute-start.23
  617.0 38.9 %all-reduce.18.cloned.1.call-done = f32[9,171,171]{2,1,0:T(8,128)} async-done(((f32[9,171,171]{2,1,0:T(8,128)}), f32[9,171,171]{2,1,0:T(8,128)}) %all-reduce.18.cloned.1.call-update) | async-done | bytes 1052692 | tf_op jit(solution)/shard_map/psum | solution.py:1206
  666.1 3.0 copy.188
  670.8 3.0 copy.190
  673.8 5.4 shard_map.314
  684.1 5.3 shard_map.317
  689.5 2.0 collective-permute-done.25
  697.5 2.2 copy.187
  (300 shorter events, 112.2 us)
Async XLA Ops:
  8.0 38.3 %sort.10.cloned.1.call-start = ((), (), s32[]{:S(2)}) async-start(), calls=%async_computation.21 | async-start | bytes 98336 | tf_op jit(solution)/shard_map/jit(sort)/sort | solution.py:1016
  9.6 127.6 %all-gather.8.cloned.1.call-start = ((), (), s32[]{:S(2)}) async-start(), calls=%async_computation.20 | async-start | bytes 7045120 | tf_op jit(solution)/shard_map/all_gather | solution.py:1057
  25.0 54.4 %all-to-all-start = ((bf16[8,128,2048]{2,1,0:T(8,128)(2,1)}), bf16[8,128,2048]{2,1,0:T(8,128)(2,1)}, u32[]{:S(2)}, u32[]{:S(2)}) async-start(bf16[8,128,2048]{2,1,0:T(8,128)(2,1)} %bitcast.170), calls=%async_computation | async-start | bytes 8388608 | tf_op jit(solution)/shard_map/all_to_all | solution.py:973
  44.8 4.5 collective-permute-start
  79.4 21.2 %copy-start.45 = (f32[684]{0:T(1024)S(1)}, f32[684]{0:T(1024)}, u32[]{:S(2)}) copy-start(f32[684]{0:T(1024)} %param.30) | copy-start | bytes 8212
  79.4 21.2 %copy-start.46 = (f32[4,684]{1,0:T(4,128)S(1)}, f32[4,684]{1,0:T(4,128)}, u32[]{:S(2)}) copy-start(f32[4,684]{1,0:T(4,128)} %param.26) | copy-start | bytes 32836
  79.4 22.4 %copy-start.50 = (f32[684]{0:T(1024)S(1)}, f32[684]{0:T(1024)}, u32[]{:S(2)}) copy-start(f32[684]{0:T(1024)} %param.27) | copy-start | bytes 8212
  98.5 3.9 collective-permute-start.1
  137.2 32.3 %collective-permute-start.2 = (bf16[4,688,1024]{2,1,0:T(8,128)(2,1)}, bf16[4,688,1024]{2,1,0:T(8,128)(2,1)}, u32[]{:S(2)}, u32[]{:S(2)}) collective-permute-start(bf16[4,688,1024]{2,1,0:T(8,128)(2,1)} %bitcast.147), channel_id=1, source_target_pairs={{0,4},{4,0},{8,12},{12,8},{16,20},{20,16},{24,28},{28,24},{1,5},{5... | collective-permute-start | bytes 16908296 | tf_op jit(solution)/shard_map/ppermute | solution.py:976
  137.6 31.9 %all-to-all-start.2 = ((bf16[4,128,768]{2,1,0:T(8,128)(2,1)}), bf16[4,128,768]{2,1,0:T(8,128)(2,1)S(1)}, u32[]{:S(2)}, u32[]{:S(2)}) async-start(bf16[4,128,768]{2,1,0:T(8,128)(2,1)} %get-tuple-element.192), calls=%async_computation.2 | async-start | bytes 1572864 | tf_op jit(solution)/shard_map/all_to_all | solution.py:973
  143.2 106.4 %all-gather.6.cloned.1.call-start = ((), (), s32[]{:S(2)}) async-start(), calls=%async_computation.13 | async-start | bytes 2621440 | tf_op jit(solution)/shard_map/all_gather | solution.py:1098
  143.2 25.2 %collective-permute-start.3 = (bf16[256,2048]{1,0:T(8,128)(2,1)}, bf16[256,2048]{1,0:T(8,128)(2,1)S(1)}, u32[]{:S(2)}, u32[]{:S(2)}) collective-permute-start(bf16[256,2048]{1,0:T(8,128)(2,1)} %pad_maximum_fusion.3), channel_id=1, source_target_pairs={{0,8},{4,12},{8,0},{12,4},{16,24},{20,28},{24,16},{28,20},{1,9},{5... | collective-permute-start | bytes 3145736 | tf_op jit(solution)/shard_map/ppermute | solution.py:1072
  144.6 25.0 %collective-permute-start.4 = (bf16[256,2048]{1,0:T(8,128)(2,1)}, bf16[256,2048]{1,0:T(8,128)(2,1)}, u32[]{:S(2)}, u32[]{:S(2)}) collective-permute-start(bf16[256,2048]{1,0:T(8,128)(2,1)} %pad_maximum_fusion.4), channel_id=1, source_target_pairs={{0,16},{4,20},{8,24},{12,28},{16,0},{20,4},{24,8},{28,12},{1,17},{... | collective-permute-start | bytes 3145736 | tf_op jit(solution)/shard_map/ppermute | solution.py:1072
  179.2 42.4 %all-to-all-start.1 = ((bf16[4,128,768]{2,1,0:T(8,128)(2,1)}), bf16[4,128,768]{2,1,0:T(8,128)(2,1)S(1)}, u32[]{:S(2)}, u32[]{:S(2)}) async-start(bf16[4,128,768]{2,1,0:T(8,128)(2,1)} %get-tuple-element.188), calls=%async_computation.1 | async-start | bytes 1572864 | tf_op jit(solution)/shard_map/all_to_all | solution.py:973
  184.1 47.3 %collective-permute-start.5 = (bf16[256,2048]{1,0:T(8,128)(2,1)S(1)}, bf16[256,2048]{1,0:T(8,128)(2,1)}, u32[]{:S(2)}, u32[]{:S(2)}) collective-permute-start(bf16[256,2048]{1,0:T(8,128)(2,1)S(1)} %pad_maximum_fusion.5), channel_id=1, source_target_pairs={{0,24},{4,28},{8,16},{12,20},{16,8},{20,12},{24,0},{28,4},{1,25},{... | collective-permute-start | bytes 3145736 | tf_op jit(solution)/shard_map/ppermute | solution.py:1072
  234.0 49.1 %all-to-all-start.3 = ((bf16[4,128,2048]{2,1,0:T(8,128)(2,1)}), bf16[4,128,2048]{2,1,0:T(8,128)(2,1)S(1)}, u32[]{:S(2)}, u32[]{:S(2)}) async-start(bf16[4,128,2048]{2,1,0:T(8,128)(2,1)} %broadcast_in_dim.42), calls=%async_computation.3 | async-start | bytes 4194304 | tf_op jit(solution)/shard_map/all_to_all | solution.py:973
  238.5 95.3 %reduce-scatter.8.cloned.1.call-start = ((), (), s32[]{:S(2)}) async-start(), calls=%async_computation.15 | async-start | bytes 2621440 | tf_op jit(solution)/shard_map/reduce_scatter | solution.py:970
  282.8 94.9 %reduce-scatter.6.cloned.1.call-start = ((), (), s32[]{:S(2)}) async-start(), calls=%async_computation.14 | async-start | bytes 2621440 | tf_op jit(solution)/shard_map/reduce_scatter | solution.py:970
  317.2 7.9 %copy-start.55 = (bf16[1024,3072]{1,0:T(8,128)(2,1)S(1)}, bf16[1024,3072]{1,0:T(8,128)(2,1)}, u32[]{:S(2)}) copy-start(bf16[1024,3072]{1,0:T(8,128)(2,1)} %get-tuple-element.226) | copy-start | bytes 18874372
  317.2 7.9 %copy-start.59 = (bf16[1024,1024]{1,0:T(8,128)(2,1)S(1)}, bf16[1024,1024]{1,0:T(8,128)(2,1)}, u32[]{:S(2)}) copy-start(bf16[1024,1024]{1,0:T(8,128)(2,1)} %get-tuple-element.220) | copy-start | bytes 6291460
  333.8 11.0 %collective-permute-start.6 = (bf16[1024,3072]{1,0:T(8,128)(2,1)}, bf16[1024,3072]{1,0:T(8,128)(2,1)}, u32[]{:S(2)}, u32[]{:S(2)}) collective-permute-start(bf16[1024,3072]{1,0:T(8,128)(2,1)} %convolution_convert_fusion.1), channel_id=1, source_target_pairs={{0,4},{4,0},{8,12},{12,8},{16,20},{20,16},{24,28},{28,24},{1,5},{5... | collective-permute-start | bytes 18874376 | tf_op jit(solution)/shard_map/ppermute | solution.py:976
  333.9 10.9 %copy-start.56 = (bf16[1024,1024]{1,0:T(8,128)(2,1)S(1)}, bf16[1024,1024]{1,0:T(8,128)(2,1)}, u32[]{:S(2)}) copy-start(bf16[1024,1024]{1,0:T(8,128)(2,1)} %get-tuple-element.218) | copy-start | bytes 6291460
  344.4 21.6 %collective-permute-start.7 = (bf16[1024,1536]{1,0:T(8,128)(2,1)}, bf16[1024,1536]{1,0:T(8,128)(2,1)}, u32[]{:S(2)}, u32[]{:S(2)}) collective-permute-start(bf16[1024,1536]{1,0:T(8,128)(2,1)} %convolution_convert_fusion.3), channel_id=1, source_target_pairs={{0,4},{4,0},{8,12},{12,8},{16,20},{20,16},{24,28},{28,24},{1,5},{5... | collective-permute-start | bytes 9437192 | tf_op jit(solution)/shard_map/ppermute | solution.py:976
  361.9 37.2 %collective-permute-start.9 = (bf16[2,256,1536]{1,2,0:T(8,128)(2,1)}, bf16[2,256,1536]{1,2,0:T(8,128)(2,1)}, u32[]{:S(2)}, u32[]{:S(2)}) collective-permute-start(bf16[2,256,1536]{1,2,0:T(8,128)(2,1)} %bitcast.176), channel_id=1, source_target_pairs={{0,16},{4,20},{8,24},{12,28},{16,0},{20,4},{24,8},{28,12},{1,17},{... | collective-permute-start | bytes 4718600 | tf_op jit(solution)/shard_map/ppermute | solution.py:976
  365.8 36.4 %collective-permute-start.8 = (bf16[2,256,1536]{2,1,0:T(8,128)(2,1)}, bf16[2,256,1536]{2,1,0:T(8,128)(2,1)}, u32[]{:S(2)}, u32[]{:S(2)}) collective-permute-start(bf16[2,256,1536]{2,1,0:T(8,128)(2,1)} %dynamic-slice_bitcast_fusion.2), channel_id=1, source_target_pairs={{0,8},{4,12},{8,0},{12,4},{16,24},{20,28},{24,16},{28,20},{1,9},{5... | collective-permute-start | bytes 4718600 | tf_op jit(solution)/shard_map/ppermute | solution.py:976
  389.0 40.5 %all-to-all-start.4 = ((bf16[4,256,768]{2,1,0:T(8,128)(2,1)}), bf16[4,256,768]{2,1,0:T(8,128)(2,1)S(1)}, u32[]{:S(2)}, u32[]{:S(2)}) async-start(bf16[4,256,768]{2,1,0:T(8,128)(2,1)} %get-tuple-element.235), calls=%async_computation.6 | async-start | bytes 3145728 | tf_op jit(solution)/shard_map/all_to_all | solution.py:973
  392.7 115.3 %reduce-scatter.10.cloned.1.call-start = ((), (), s32[]{:S(2)}) async-start(), calls=%async_computation.16 | async-start | bytes 5242880 | tf_op jit(solution)/shard_map/reduce_scatter | solution.py:970
  393.0 9.3 %copy-start.21 = (bf16[1,2,256,1536]{2,3,1,0:T(8,128)(2,1)S(1)}, bf16[1,2,256,1536]{2,3,1,0:T(8,128)(2,1)}, u32[]{:S(2)}) copy-start(bf16[1,2,256,1536]{2,3,1,0:T(8,128)(2,1)} %copy.199) | copy-start | bytes 4718596
  405.2 18.4 %collective-permute-start.11 = (bf16[1,256,1536]{1,2,0:T(8,128)(2,1)S(1)}, bf16[1,256,1536]{1,2,0:T(8,128)(2,1)S(1)}, u32[]{:S(2)}, u32[]{:S(2)}) collective-permute-start(bf16[1,256,1536]{1,2,0:T(8,128)(2,1)S(1)} %constant_dynamic-slice_fusion.8), channel_id=1, source_target_pairs={{0,8},{4,12},{8,0},{12,4},{16,24},{20,28},{24,16},{28,20},{1,9},{5... | collective-permute-start | bytes 2359304 | tf_op jit(solution)/shard_map/ppermute | solution.py:976
  407.4 16.2 %copy-start.8 = (bf16[2,256,1536]{2,1,0:T(8,128)(2,1)}, bf16[2,256,1536]{2,1,0:T(8,128)(2,1)S(1)}, u32[]{:S(2)}) copy-start(bf16[2,256,1536]{2,1,0:T(8,128)(2,1)S(1)} %fusion.5) | copy-start | bytes 4718596
  407.4 18.5 %collective-permute-start.10 = (bf16[1,256,1536]{2,1,0:T(8,128)(2,1)S(1)}, bf16[1,256,1536]{2,1,0:T(8,128)(2,1)}, u32[]{:S(2)}, u32[]{:S(2)}) collective-permute-start(bf16[1,256,1536]{2,1,0:T(8,128)(2,1)S(1)} %constant_dynamic-slice_fusion.10), channel_id=1, source_target_pairs={{0,16},{4,20},{8,24},{12,28},{16,0},{20,4},{24,8},{28,12},{1,17},{... | collective-permute-start | bytes 2359304 | tf_op jit(solution)/shard_map/ppermute | solution.py:976
  429.6 49.4 %collective-permute-start.12 = (bf16[1024,3072]{1,0:T(8,128)(2,1)}, bf16[1024,3072]{1,0:T(8,128)(2,1)}, u32[]{:S(2)}, u32[]{:S(2)}) collective-permute-start(bf16[1024,3072]{1,0:T(8,128)(2,1)} %convolution_convert_fusion), channel_id=1, source_target_pairs={{0,4},{4,0},{8,12},{12,8},{16,20},{20,16},{24,28},{28,24},{1,5},{5... | collective-permute-start | bytes 18874376 | tf_op jit(solution)/shard_map/ppermute | solution.py:976
  430.7 166.4 %reduce-scatter.12.cloned.1.call-start = ((), (), s32[]{:S(2)}) async-start(), calls=%async_computation.17 | async-start | bytes 5242880 | tf_op jit(solution)/shard_map/reduce_scatter | solution.py:970
  439.7 13.7 %copy-start.14 = (bf16[4,256,768]{2,1,0:T(8,128)(2,1)S(1)}, bf16[4,256,768]{2,1,0:T(8,128)(2,1)}, u32[]{:S(2)}) copy-start(bf16[4,256,768]{2,1,0:T(8,128)(2,1)} %get-tuple-element.290) | copy-start | bytes 4718596
  450.6 7.1 %copy-start.47 = (f32[1,2048]{1,0:T(1,128)S(1)}, f32[1,2048]{1,0:T(1,128)}, u32[]{:S(2)}) copy-start(f32[1,2048]{1,0:T(1,128)} %get-tuple-element.302) | copy-start | bytes 24580
  450.6 7.1 %copy-start.48 = (f32[1,2048]{1,0:T(1,128)S(1)}, f32[1,2048]{1,0:T(1,128)}, u32[]{:S(2)}) copy-start(f32[1,2048]{1,0:T(1,128)} %get-tuple-element.303) | copy-start | bytes 24580
  452.7 26.2 %collective-permute-start.13 = (bf16[2,256,768]{2,1,0:T(8,128)(2,1)}, bf16[2,256,768]{2,1,0:T(8,128)(2,1)}, u32[]{:S(2)}, u32[]{:S(2)}) collective-permute-start(bf16[2,256,768]{2,1,0:T(8,128)(2,1)} %dynamic-slice_bitcast_fusion.5), channel_id=1, source_target_pairs={{0,8},{4,12},{8,0},{12,4},{16,24},{20,28},{24,16},{28,20},{1,9},{5... | collective-permute-start | bytes 2359304 | tf_op jit(solution)/shard_map/ppermute | solution.py:976
  454.4 24.6 %collective-permute-start.14 = (bf16[2,256,768]{2,1,0:T(8,128)(2,1)}, bf16[2,256,768]{2,1,0:T(8,128)(2,1)}, u32[]{:S(2)}, u32[]{:S(2)}) collective-permute-start(bf16[2,256,768]{2,1,0:T(8,128)(2,1)} %dynamic-slice_bitcast_fusion.4), channel_id=1, source_target_pairs={{0,16},{4,20},{8,24},{12,28},{16,0},{20,4},{24,8},{28,12},{1,17},{... | collective-permute-start | bytes 2359304 | tf_op jit(solution)/shard_map/ppermute | solution.py:976
  455.9 22.0 %copy-start.32 = (s32[1024,1]{1,0:T(8,128)}, s32[1024,1]{1,0:T(8,128)S(1)}, u32[]{:S(2)}) copy-start(s32[1024,1]{1,0:T(8,128)S(1)} %copy.173.place_ref) | copy-start | bytes 12292
  457.7 22.8 %copy-start.3 = (bf16[256,3072]{1,0:T(8,128)(2,1)S(1)}, bf16[256,3072]{1,0:T(8,128)(2,1)}, u32[]{:S(2)}) copy-start(bf16[256,3072]{1,0:T(8,128)(2,1)} %get-tuple-element.237) | copy-start | bytes 4718596
  457.7 22.8 %copy-start.22 = (bf16[256,1024]{1,0:T(8,128)(2,1)S(1)}, bf16[256,1024]{1,0:T(8,128)(2,1)}, u32[]{:S(2)}) copy-start(bf16[256,1024]{1,0:T(8,128)(2,1)} %get-tuple-element.264) | copy-start | bytes 1572868
  478.9 10.5 %collective-permute-start.15 = (f32[8,768]{1,0:T(8,128)}, f32[8,768]{1,0:T(8,128)S(1)}, u32[]{:S(2)}, u32[]{:S(2)}) collective-permute-start(f32[8,768]{1,0:T(8,128)} %get-tuple-element.263), channel_id=1, source_target_pairs={{4,0},{8,4},{12,8},{16,12},{20,16},{24,20},{28,24},{5,1},{9,5},{13... | collective-permute-start | bytes 73736 | tf_op jit(solution)/shard_map/ppermute | solution.py:1170
  489.4 37.5 %collective-permute-start.16 = (bf16[2,256,1536]{2,1,0:T(8,128)(2,1)}, bf16[2,256,1536]{2,1,0:T(8,128)(2,1)}, u32[]{:S(2)}, u32[]{:S(2)}) collective-permute-start(bf16[2,256,1536]{2,1,0:T(8,128)(2,1)} %dynamic-slice_bitcast_fusion.1), channel_id=1, source_target_pairs={{0,8},{4,12},{8,0},{12,4},{16,24},{20,28},{24,16},{28,20},{1,9},{5... | collective-permute-start | bytes 4718600 | tf_op jit(solution)/shard_map/ppermute | solution.py:976
  491.4 36.0 %collective-permute-start.17 = (bf16[2,256,1536]{2,1,0:T(8,128)(2,1)}, bf16[2,256,1536]{2,1,0:T(8,128)(2,1)S(1)}, u32[]{:S(2)}, u32[]{:S(2)}) collective-permute-start(bf16[2,256,1536]{2,1,0:T(8,128)(2,1)} %dynamic-slice_bitcast_fusion), channel_id=1, source_target_pairs={{0,16},{4,20},{8,24},{12,28},{16,0},{20,4},{24,8},{28,12},{1,17},{... | collective-permute-start | bytes 4718600 | tf_op jit(solution)/shard_map/ppermute | solution.py:976
  509.4 11.6 %all-to-all-start.7 = ((f32[4,2,512]{2,1,0:T(2,128)}), f32[4,2,512]{2,1,0:T(2,128)S(1)}, u32[]{:S(2)}, u32[]{:S(2)}) async-start(f32[4,2,512]{2,1,0:T(2,128)} %bitcast.69), calls=%async_computation.11 | async-start | bytes 32768 | tf_op jit(solution)/shard_map/all_to_all | solution.py:973
  532.7 50.6 %all-to-all-start.5 = ((bf16[8,128,512]{2,1,0:T(8,128)(2,1)}), bf16[8,128,512]{2,1,0:T(8,128)(2,1)}, u32[]{:S(2)}, u32[]{:S(2)}) async-start(bf16[8,128,512]{2,1,0:T(8,128)(2,1)} %bitcast.177), calls=%async_computation.9 | async-start | bytes 2097152 | tf_op jit(solution)/shard_map/all_to_all | solution.py:973
  536.9 119.0 %all-reduce.18.cloned.1.call-start = ((), (), s32[]{:S(2)}) async-start(), calls=%async_computation.18 | async-start | bytes 3244032 | tf_op jit(solution)/shard_map/psum | solution.py:1206
  537.2 52.6 %collective-permute-start.22 = (bf16[1024,1536]{1,0:T(8,128)(2,1)}, bf16[1024,1536]{1,0:T(8,128)(2,1)}, u32[]{:S(2)}, u32[]{:S(2)}) collective-permute-start(bf16[1024,1536]{1,0:T(8,128)(2,1)} %convolution_convert_fusion.2), channel_id=1, source_target_pairs={{0,4},{4,0},{8,12},{12,8},{16,20},{20,16},{24,28},{28,24},{1,5},{5... | collective-permute-start | bytes 9437192 | tf_op jit(solution)/shard_map/ppermute | solution.py:976
  541.1 38.1 %collective-permute-start.20 = (bf16[1,256,1536]{2,1,0:T(8,128)(2,1)}, bf16[1,256,1536]{2,1,0:T(8,128)(2,1)}, u32[]{:S(2)}, u32[]{:S(2)}) collective-permute-start(bf16[1,256,1536]{2,1,0:T(8,128)(2,1)} %constant_dynamic-slice_fusion.5), channel_id=1, source_target_pairs={{0,16},{4,20},{8,24},{12,28},{16,0},{20,4},{24,8},{28,12},{1,17},{... | collective-permute-start | bytes 2359304 | tf_op jit(solution)/shard_map/ppermute | solution.py:976
  544.2 36.4 %collective-permute-start.21 = (bf16[1,256,1536]{2,1,0:T(8,128)(2,1)}, bf16[1,256,1536]{2,1,0:T(8,128)(2,1)}, u32[]{:S(2)}, u32[]{:S(2)}) collective-permute-start(bf16[1,256,1536]{2,1,0:T(8,128)(2,1)} %constant_dynamic-slice_fusion.4), channel_id=1, source_target_pairs={{0,8},{4,12},{8,0},{12,4},{16,24},{20,28},{24,16},{28,20},{1,9},{5... | collective-permute-start | bytes 2359304 | tf_op jit(solution)/shard_map/ppermute | solution.py:976
  547.1 29.5 %collective-permute-start.18 = (bf16[1,256,768]{2,1,0:T(8,128)(2,1)S(1)}, bf16[1,256,768]{2,1,0:T(8,128)(2,1)S(1)}, u32[]{:S(2)}, u32[]{:S(2)}) collective-permute-start(bf16[1,256,768]{2,1,0:T(8,128)(2,1)S(1)} %constant_dynamic-slice_fusion.7), channel_id=1, source_target_pairs={{0,16},{4,20},{8,24},{12,28},{16,0},{20,4},{24,8},{28,12},{1,17},{... | collective-permute-start | bytes 1179656 | tf_op jit(solution)/shard_map/ppermute | solution.py:976
  550.0 26.8 %collective-permute-start.19 = (bf16[1,256,768]{2,1,0:T(8,128)(2,1)}, bf16[1,256,768]{2,1,0:T(8,128)(2,1)}, u32[]{:S(2)}, u32[]{:S(2)}) collective-permute-start(bf16[1,256,768]{2,1,0:T(8,128)(2,1)} %constant_dynamic-slice_fusion.6), channel_id=1, source_target_pairs={{0,8},{4,12},{8,0},{12,4},{16,24},{20,28},{24,16},{28,20},{1,9},{5... | collective-permute-start | bytes 1179656 | tf_op jit(solution)/shard_map/ppermute | solution.py:976
  553.9 22.7 %copy-start.25 = (bf16[2,256,768]{2,1,0:T(8,128)(2,1)S(1)}, bf16[2,256,768]{2,1,0:T(8,128)(2,1)}, u32[]{:S(2)}) copy-start(bf16[2,256,768]{2,1,0:T(8,128)(2,1)} %copy-done.24) | copy-start | bytes 2359300
  555.2 21.6 %copy-start.27 = (bf16[2,256,768]{2,1,0:T(8,128)(2,1)S(1)}, bf16[2,256,768]{2,1,0:T(8,128)(2,1)}, u32[]{:S(2)}) copy-start(bf16[2,256,768]{2,1,0:T(8,128)(2,1)} %copy-done.26) | copy-start | bytes 2359300
  556.5 22.7 %copy-start.11 = (bf16[2,256,1536]{2,1,0:T(8,128)(2,1)S(1)}, bf16[2,256,1536]{2,1,0:T(8,128)(2,1)}, u32[]{:S(2)}) copy-start(bf16[2,256,1536]{2,1,0:T(8,128)(2,1)} %copy-done.10) | copy-start | bytes 4718596
  583.3 6.5 copy-start.58
  589.7 105.8 %reduce-scatter.14.cloned.1.call-start = ((), (), s32[]{:S(2)}) async-start(), calls=%async_computation.19 | async-start | bytes 1966080 | tf_op jit(solution)/shard_map/reduce_scatter | solution.py:970
  599.3 14.8 %copy-start.19 = (bf16[4,256,768]{2,1,0:T(8,128)(2,1)}, bf16[4,256,768]{2,1,0:T(8,128)(2,1)S(1)}, u32[]{:S(2)}) copy-start(bf16[4,256,768]{2,1,0:T(8,128)(2,1)S(1)} %get-tuple-element.395) | copy-start | bytes 4718596
  602.9 76.4 %collective-permute-start.24 = (bf16[2,256,768]{1,2,0:T(8,128)(2,1)}, bf16[2,256,768]{1,2,0:T(8,128)(2,1)}, u32[]{:S(2)}, u32[]{:S(2)}) collective-permute-start(bf16[2,256,768]{1,2,0:T(8,128)(2,1)} %bitcast.180), channel_id=1, source_target_pairs={{0,16},{4,20},{8,24},{12,28},{16,0},{20,4},{24,8},{28,12},{1,17},{... | collective-permute-start | bytes 2359304 | tf_op jit(solution)/shard_map/ppermute | solution.py:976
  609.6 69.7 %all-to-all-start.6 = ((bf16[8,128,512]{2,1,0:T(8,128)(2,1)}), bf16[8,128,512]{2,1,0:T(8,128)(2,1)}, u32[]{:S(2)}, u32[]{:S(2)}) async-start(bf16[8,128,512]{2,1,0:T(8,128)(2,1)} %bitcast.178), calls=%async_computation.10 | async-start | bytes 2097152 | tf_op jit(solution)/shard_map/all_to_all | solution.py:973
  615.1 64.2 %collective-permute-start.23 = (bf16[2,256,768]{2,1,0:T(8,128)(2,1)}, bf16[2,256,768]{2,1,0:T(8,128)(2,1)}, u32[]{:S(2)}, u32[]{:S(2)}) collective-permute-start(bf16[2,256,768]{2,1,0:T(8,128)(2,1)} %dynamic-slice_bitcast_fusion.3), channel_id=1, source_target_pairs={{0,8},{4,12},{8,0},{12,4},{16,24},{20,28},{24,16},{28,20},{1,9},{5... | collective-permute-start | bytes 2359304 | tf_op jit(solution)/shard_map/ppermute | solution.py:976
  680.6 10.8 %collective-permute-start.25 = (bf16[1,256,768]{2,1,0:T(8,128)(2,1)S(1)}, bf16[1,256,768]{2,1,0:T(8,128)(2,1)S(1)}, u32[]{:S(2)}, u32[]{:S(2)}) collective-permute-start(bf16[1,256,768]{2,1,0:T(8,128)(2,1)S(1)} %constant_dynamic-slice_fusion.2), channel_id=1, source_target_pairs={{0,16},{4,20},{8,24},{12,28},{16,0},{20,4},{24,8},{28,12},{1,17},{... | collective-permute-start | bytes 1179656 | tf_op jit(solution)/shard_map/ppermute | solution.py:976
  682.9 6.5 copy-start.28
  683.0 10.4 %collective-permute-start.26 = (bf16[1,256,768]{1,2,0:T(8,128)(2,1)S(1)}, bf16[1,256,768]{1,2,0:T(8,128)(2,1)S(1)}, u32[]{:S(2)}, u32[]{:S(2)}) collective-permute-start(bf16[1,256,768]{1,2,0:T(8,128)(2,1)S(1)} %constant_dynamic-slice_fusion), channel_id=1, source_target_pairs={{0,8},{4,12},{8,0},{12,4},{16,24},{20,28},{24,16},{28,20},{1,9},{5... | collective-permute-start | bytes 1179656 | tf_op jit(solution)/shard_map/ppermute | solution.py:976
  (40 other events, 120.7 us)
Sparse Core Ops, SparseCore 0:
  11.3 3.4 sort.12.cloned.1.call-done
  589.9 66.0 all-reduce.17
  (1 shorter events, 0.0 us)
Sparse Core Ops, SparseCore 1:
  12.2 107.1 all-gather.7
  179.3 64.2 all-gather.5
  282.9 43.6 reduce-scatter.7
  333.9 43.7 reduce-scatter.5
  429.7 75.9 reduce-scatter.9
  508.2 77.1 reduce-scatter.11
  597.2 33.0 reduce-scatter.13
